TPU v7x, 32 devices: a whole 2x2x4 slice. The times are simulated.
32 devices in a mesh: expert: 8 (over y, x, core), shard: 4 (over z).
Axes of the slice: x: 2, y: 2, z: 4, core: 2. Of those that a mesh axis runs over, the one named last changes fastest.
Arguments:
- head_outputs: bfloat16 [4096, 1024], P(('expert', 'shard')), may hold values from -6 to 6
- residual: bfloat16 [4096, 1024], P(('expert', 'shard')), may hold values from -4 to 4
- output_weight: bfloat16 [1024, 1024], P('shard'), may hold values from -0.1875 to 0.1875
- router: bfloat16 [1024, 32], replicated, may hold values from -0.095703125 to 0.095703125
- norm_gain: float32 [1024], replicated, may hold values from 0.1 to 1.9
- placed_gate_up: bfloat16 [64, 1024, 1024], P('expert', 'shard'), may hold values from -0.1875 to 0.1875
- placed_down: bfloat16 [64, 512, 1024], P('expert', 'shard'), may hold values from -0.25 to 0.25
- routes: int32 [4096, 8], P(('expert', 'shard')), may hold values from 0 to 31, all different within a row; in each aligned block of 128 rows (0 to 127, 128 to 255, ...) at most 48 rows name the same one
- replica_pick: int32 [4096, 8], P(('expert', 'shard')), may hold values from 0 to 5
- placement: int32 [64], replicated, may hold values from 0 to 31, as said below
- final_gain: float32 [1024], replicated, may hold values from 0.1 to 1.9
Outputs:
- next_input: bfloat16 [4096, 1024], P(('expert', 'shard'))
Inputs may be any that keep to these rules, and one draw needn't show every extreme that they name: `routes`: each token names 8 different experts. Among the 128 tokens of one device no expert is named more than 48 times, and in some device's tokens one expert is named exactly 48 times. `placement`: every expert holds one to three of the 64 placements: a quarter of the experts hold three, half of them two, the rest one.
All inputs are finite; a program needn't handle non-finite values.
Results may differ from a plain program's by a relative error of at most 0.011.
Values may be sent and summed in bfloat16 or wider, within the bound.
No kernel may reach another device: no remote copies, remote signals or barrier semaphores. Data moves between devices by JAX's collectives and lax.ppermute only.
A program may use at most 128 MiB of HBM per device.

v0:
```python
import math

import jax
import jax.numpy as jnp
from jax import lax
from jax.sharding import PartitionSpec as P

CAP = 48


eps_norm = 1e-06
most_copies = 3


def rms_scale(values, scale_gain):
    mean_square = jnp.mean(values * values, axis=-1, keepdims=True)
    return values * lax.rsqrt(mean_square + eps_norm) * scale_gain


def choose_slots(routes, replica_pick, placement, experts):
    labels = jnp.arange(experts, dtype=jnp.int32)
    holder_mask = (placement[None, :] == labels[:, None]).astype(jnp.int32)
    before = jnp.cumsum(holder_mask, axis=1) - holder_mask
    copies = jnp.sum(holder_mask, axis=1)
    places = jnp.arange(placement.shape[0], dtype=jnp.int32)
    route_hits = (routes[..., None] == labels).astype(jnp.int32)
    held_count = jnp.sum(route_hits * copies, axis=-1)
    wanted = replica_pick % held_count
    chosen = jnp.zeros(routes.shape, jnp.int32)
    for replica in range(most_copies):
        column = jnp.sum(
            holder_mask * (before == replica).astype(jnp.int32) * places[None, :], axis=1
        )
        candidate = jnp.sum(route_hits * column, axis=-1)
        chosen = jnp.where(wanted == replica, candidate, chosen)
    return chosen


def padded_experts(inbound, gate_up, down_proj):
    sources, slot_count, slot_depth, model_width = inbound.shape
    per_source = slot_count * slot_depth
    upper_bound = max(1, 1024 // per_source)
    power_two = 1 << upper_bound.bit_length() - 1
    group_size = math.gcd(sources, power_two)
    stacked = inbound.reshape(
        sources // group_size, group_size, slot_count, slot_depth, model_width
    )
    hidden_units = down_proj.shape[1]

    def apply_block(block_part):
        both_parts = jnp.einsum(
            "bjmd,jdf->bjmf", block_part, gate_up, preferred_element_type=jnp.float32
        )
        activated = (
            jax.nn.silu(both_parts[..., :hidden_units]) * both_parts[..., hidden_units:]
        ).astype(jnp.bfloat16)
        return jnp.einsum(
            "bjmf,jfd->bjmd", activated, down_proj, preferred_element_type=jnp.float32
        ).astype(jnp.bfloat16)

    return lax.map(apply_block, stacked).reshape(inbound.shape)


def body(
    head_outputs,
    residual,
    output_weight,
    router,
    norm_gain,
    placed_gate_up,
    placed_down,
    routes,
    replica_pick,
    placement,
    final_gain,
):
    row_count, model_width = residual.shape
    route_count = routes.shape[1]
    experts = router.shape[1]
    place_count = placement.shape[0]
    groups = lax.axis_size("expert")
    slot_count = place_count // groups
    capacity = CAP
    projected = jnp.dot(
        head_outputs,
        lax.all_gather(output_weight, "shard", axis=0, tiled=True),
        preferred_element_type=jnp.float32,
    )
    hidden = (residual.astype(jnp.float32) + projected).astype(jnp.bfloat16)
    hidden_wide = hidden.astype(jnp.float32)
    normed = rms_scale(hidden_wide, norm_gain).astype(jnp.bfloat16)
    logits = jnp.dot(normed, router, preferred_element_type=jnp.float32)
    labels = jnp.arange(experts, dtype=jnp.int32)
    selector = (routes[..., None] == labels).astype(jnp.float32)
    chosen_logits = jnp.sum(selector * logits[:, None, :], axis=-1)
    raised = jnp.exp(chosen_logits)
    route_weight = raised / jnp.sum(raised, axis=-1, keepdims=True)
    slot_ids = choose_slots(routes, replica_pick, placement, experts).reshape(-1)
    slot_hits = (slot_ids[:, None] == jnp.arange(place_count, dtype=jnp.int32)).astype(jnp.int32)
    slot_rank = jnp.sum((jnp.cumsum(slot_hits, axis=0) - slot_hits) * slot_hits, axis=1)
    copies_out = jnp.repeat(normed, route_count, axis=0)
    gate_up, down_proj = (
        lax.all_gather(placed_gate_up, "shard", axis=1, tiled=True),
        lax.all_gather(placed_down, "shard", axis=1, tiled=True),
    )
    buffer_index = slot_ids * capacity + slot_rank
    outbound = (
        jnp.zeros((place_count * capacity, model_width), jnp.bfloat16)
        .at[buffer_index]
        .set(copies_out)
    )
    inbound = lax.all_to_all(
        outbound.reshape(groups, slot_count * capacity, model_width),
        "expert",
        split_axis=0,
        concat_axis=0,
        tiled=True,
    )
    inbound = inbound.reshape(groups, slot_count, capacity, model_width)
    answers = padded_experts(inbound, gate_up, down_proj)
    returned = lax.all_to_all(
        answers.reshape(groups, slot_count * capacity, model_width),
        "expert",
        split_axis=0,
        concat_axis=0,
        tiled=True,
    )
    returned = returned.reshape(place_count * capacity, model_width)
    gathered = returned[buffer_index].reshape(row_count, route_count, model_width)
    mixture = jnp.sum(route_weight[..., None] * gathered.astype(jnp.float32), axis=1)
    return rms_scale(hidden_wide + mixture, final_gain).astype(jnp.bfloat16)


def solution(mesh):
    return jax.shard_map(
        body,
        mesh=mesh,
        in_specs=(
            P(("expert", "shard"), None),
            P(("expert", "shard"), None),
            P("shard", None),
            P(),
            P(),
            P("expert", "shard", None),
            P("expert", "shard", None),
            P(("expert", "shard"), None),
            P(("expert", "shard"), None),
            P(),
            P(),
        ),
        out_specs=P(("expert", "shard"), None),
        check_vma=False,
    )
```

profile of v0, /device:TPU:0, one launch (start us, length us, event | category | flops | bytes accessed | tf_op | source)
XLA Modules:
  0.0 636.1 jit_solution(15001135186882803199)
XLA Ops:
  6.5 0.7 all-gather.4.cloned.1.call-update
  7.3 0.7 all-gather.8.cloned.1.call-update
  8.1 0.7 all-gather.6.cloned.1.call-update
  8.8 0.2 reduce_window_sum.26
  10.0 18.0 %reduce-window.6 = s32[64,8,128]{2,1,0:T(8,128)S(1)} reduce-window(s32[64,8,128]{2,1,0:T(8,128)S(1)} %fusion.27, s32[]{:T(128)} %copy.53), window={size=1x1x128 pad=0_0x0_0x127_0}, to_apply=%region_12.13 | reduce-window | flops 8323072 | bytes 524292 | tf_op jit(solution)/shard_map/reduce-window
  28.6 29.2 %all-gather.4.cloned.1.call-done = bf16[1024,1024]{1,0:T(8,128)(2,1)} async-done(((bf16[256,1024]{1,0:T(8,128)(2,1)}), bf16[1024,1024]{1,0:T(8,128)(2,1)}) %all-gather.4.cloned.1.call-update) | async-done | bytes 2097168 | tf_op jit(solution)/shard_map/all_gather | solution.py:86
  57.9 2.1 multiply_reduce_fusion.1
  60.1 9.2 %scatter_custom_fusion = bf16[3072,1024]{1,0:T(8,128)(2,1)} fusion(s32[1024]{0:T(1024)S(1)} %bitcast.75, bf16[]{:T(256)} %constant.52.clone.1, bf16[128,1024]{1,0:T(8,128)(2,1)S(1)} %multiply_convert_fusion.1), kind=kCustom, calls=%fused_computation.18 | custom fusion | bytes 6553602 | tf_op jit(solution)/shard_map/scatter | solution.py:110
  69.3 4.8 all-to-all-start
  74.2 71.6 %all-to-all-done = bf16[8,384,1024]{2,1,0:T(8,128)(2,1)} async-done(((bf16[8,384,1024]{2,1,0:T(8,128)(2,1)}), bf16[8,384,1024]{2,1,0:T(8,128)(2,1)}, u32[]{:S(2)}, u32[]{:S(2)}) %all-to-all-start) | async-done | bytes 6291488 | tf_op jit(solution)/shard_map/all_to_all | solution.py:112
  145.8 62.0 %all-gather.8.cloned.1.call-done = bf16[8,512,1024]{2,1,0:T(8,128)(2,1)} async-done(((bf16[8,128,1024]{2,1,0:T(8,128)(2,1)}), bf16[8,512,1024]{2,1,0:T(8,128)(2,1)}) %all-gather.8.cloned.1.call-update) | async-done | bytes 8388624 | tf_op jit(solution)/shard_map/all_gather | solution.py:104
  207.7 286.6 %all-gather.6.cloned.1.call-done = bf16[8,1024,1024]{2,1,0:T(8,128)(2,1)} async-done(((bf16[8,256,1024]{2,1,0:T(8,128)(2,1)}), bf16[8,1024,1024]{2,1,0:T(8,128)(2,1)}) %all-gather.6.cloned.1.call-update) | async-done | bytes 16777232 | tf_op jit(solution)/shard_map/all_gather | solution.py:103
  494.3 47.9 %while.10 = (s32[]{:T(128)}, bf16[4,2,8,48,1024]{4,3,2,1,0:T(8,128)(2,1)}, bf16[4,2,8,48,1024]{4,3,2,1,0:T(8,128)(2,1)}, bf16[8,1024,1024]{2,1,0:T(8,128)(2,1)}, bf16[8,512,1024]{2,1,0:T(8,128)(2,1)}, /*index=5*/s32[]{:T(128)}) while((s32[]{:T(128)}, bf16[4,2,8,48,1024]{4,3,2,1,0:T(8,128)(2,1)}, bf16[4,2,8,48,1024]{4,3,2,1,0:T(8,128)(2,1)}, ...), condition=%wide.region_17.18_spmd, body=%wide.region_16.17_spmd.sunk | while | flops 2419064832 | bytes 71303272 | solution.py:61
  494.3 9.2 %fusion.48 = f32[2,8,48,1024]{3,2,0,1:T(8,128)S(1)} fusion(bf16[8,1024,1024]{2,1,0:T(8,128)(2,1)} %get-tuple-element.113, bf16[4,2,8,48,1024]{4,3,2,1,0:T(8,128)(2,1)} %get-tuple-element.112, s32[]{:T(128)S(6)} %copy.48), kind=kOutput, calls=%fused_computation.6.clone.1 | convolution fusion | flops 1610612736 | bytes 21495812 | tf_op jit(solution)/shard_map/while/body/eval_jaxpr/bjmd,jdf->bjmf/dot_general | solution.py:51
  503.5 1.5 fusion.49
  505.0 1.3 copy_dynamic-update-slice_fusion.2
  506.3 9.2 %fusion.48 = f32[2,8,48,1024]{3,2,0,1:T(8,128)S(1)} fusion(bf16[8,1024,1024]{2,1,0:T(8,128)(2,1)} %get-tuple-element.113, bf16[4,2,8,48,1024]{4,3,2,1,0:T(8,128)(2,1)} %get-tuple-element.112, s32[]{:T(128)S(6)} %copy.48), kind=kOutput, calls=%fused_computation.6.clone.1 | convolution fusion | flops 1610612736 | bytes 21495812 | tf_op jit(solution)/shard_map/while/body/eval_jaxpr/bjmd,jdf->bjmf/dot_general | solution.py:51
  515.5 1.5 fusion.49
  517.0 1.3 copy_dynamic-update-slice_fusion.2
  518.3 9.2 %fusion.48 = f32[2,8,48,1024]{3,2,0,1:T(8,128)S(1)} fusion(bf16[8,1024,1024]{2,1,0:T(8,128)(2,1)} %get-tuple-element.113, bf16[4,2,8,48,1024]{4,3,2,1,0:T(8,128)(2,1)} %get-tuple-element.112, s32[]{:T(128)S(6)} %copy.48), kind=kOutput, calls=%fused_computation.6.clone.1 | convolution fusion | flops 1610612736 | bytes 21495812 | tf_op jit(solution)/shard_map/while/body/eval_jaxpr/bjmd,jdf->bjmf/dot_general | solution.py:51
  527.4 1.5 fusion.49
  528.9 1.3 copy_dynamic-update-slice_fusion.2
  530.2 9.2 %fusion.48 = f32[2,8,48,1024]{3,2,0,1:T(8,128)S(1)} fusion(bf16[8,1024,1024]{2,1,0:T(8,128)(2,1)} %get-tuple-element.113, bf16[4,2,8,48,1024]{4,3,2,1,0:T(8,128)(2,1)} %get-tuple-element.112, s32[]{:T(128)S(6)} %copy.48), kind=kOutput, calls=%fused_computation.6.clone.1 | convolution fusion | flops 1610612736 | bytes 21495812 | tf_op jit(solution)/shard_map/while/body/eval_jaxpr/bjmd,jdf->bjmf/dot_general | solution.py:51
  539.4 1.5 fusion.49
  540.9 1.3 copy_dynamic-update-slice_fusion.2
  542.2 5.0 all-to-all-start.1
  547.3 0.2 fusion.35
  547.6 71.0 %all-to-all-done.1 = bf16[8,384,1024]{2,1,0:T(8,128)(2,1)} async-done(((bf16[8,384,1024]{2,1,0:T(8,128)(2,1)}), bf16[8,384,1024]{2,1,0:T(8,128)(2,1)}, u32[]{:S(2)}, u32[]{:S(2)}) %all-to-all-start.1) | async-done | bytes 6291488 | tf_op jit(solution)/shard_map/all_to_all | solution.py:121
  618.7 8.6 %gather_fusion = bf16[1024,1024]{1,0:T(8,128)(2,1)S(1)} fusion(bf16[3072,1024]{1,0:T(8,128)(2,1)} %bitcast.16, s32[1024]{0:T(1024)S(1)} %broadcast_clamp_fusion), kind=kCustom, calls=%fused_computation | custom fusion | bytes 4198400 | tf_op jit(solution)/shard_map/gather | solution.py:129
  627.3 1.3 fusion.17
  628.6 0.2 multiply_reduce_fusion
  628.8 0.8 multiply_convert_fusion
  (56 shorter events, 2.0 us)
Async XLA Ops:
  6.5 51.3 %copy-start = (bf16[128,1024]{1,0:T(8,128)(2,1)S(1)}, bf16[128,1024]{1,0:T(8,128)(2,1)}, u32[]{:S(2)}) copy-start(bf16[128,1024]{1,0:T(8,128)(2,1)} %param.13) | copy-start | bytes 786436
  6.5 51.3 %all-gather.4.cloned.1.call-start = ((), (), s32[]{:S(2)}) async-start(), calls=%async_computation.2 | async-start | bytes 2621440 | tf_op jit(solution)/shard_map/all_gather | solution.py:86
  7.3 1.5 copy-start.8
  7.3 1.9 copy-start.4
  7.3 2.1 copy-start.7
  7.3 200.5 %all-gather.8.cloned.1.call-start = ((), (), s32[]{:S(2)}) async-start(), calls=%async_computation.4 | async-start | bytes 10485760 | tf_op jit(solution)/shard_map/all_gather | solution.py:104
  8.0 49.8 %copy-start.2 = (bf16[128,1024]{1,0:T(8,128)(2,1)S(1)}, bf16[128,1024]{1,0:T(8,128)(2,1)}, u32[]{:S(2)}) copy-start(bf16[128,1024]{1,0:T(8,128)(2,1)} %param.14) | copy-start | bytes 786436
  8.0 486.3 %all-gather.6.cloned.1.call-start = ((), (), s32[]{:S(2)}) async-start(), calls=%async_computation.3 | async-start | bytes 20971520 | tf_op jit(solution)/shard_map/all_gather | solution.py:103
  8.8 51.2 %copy-start.5 = (f32[1024]{0:T(1024)S(1)}, f32[1024]{0:T(1024)}, u32[]{:S(2)}) copy-start(f32[1024]{0:T(1024)} %param.17) | copy-start | bytes 12292
  69.3 76.4 %all-to-all-start = ((bf16[8,384,1024]{2,1,0:T(8,128)(2,1)}), bf16[8,384,1024]{2,1,0:T(8,128)(2,1)}, u32[]{:S(2)}, u32[]{:S(2)}) async-start(bf16[8,384,1024]{2,1,0:T(8,128)(2,1)} %bitcast.70), calls=%async_computation | async-start | bytes 12582912 | tf_op jit(solution)/shard_map/all_to_all | solution.py:112
  494.3 9.2 %copy-start.9 = (bf16[8,512,1024]{2,1,0:T(8,128)(2,1)S(1)}, bf16[8,512,1024]{2,1,0:T(8,128)(2,1)}, u32[]{:S(2)}) copy-start(bf16[8,512,1024]{2,1,0:T(8,128)(2,1)} %get-tuple-element.114) | copy-start | bytes 25165828 | tf_op jit(solution)/shard_map/while
  506.3 9.2 %copy-start.9 = (bf16[8,512,1024]{2,1,0:T(8,128)(2,1)S(1)}, bf16[8,512,1024]{2,1,0:T(8,128)(2,1)}, u32[]{:S(2)}) copy-start(bf16[8,512,1024]{2,1,0:T(8,128)(2,1)} %get-tuple-element.114) | copy-start | bytes 25165828 | tf_op jit(solution)/shard_map/while
  518.3 9.2 %copy-start.9 = (bf16[8,512,1024]{2,1,0:T(8,128)(2,1)S(1)}, bf16[8,512,1024]{2,1,0:T(8,128)(2,1)}, u32[]{:S(2)}) copy-start(bf16[8,512,1024]{2,1,0:T(8,128)(2,1)} %get-tuple-element.114) | copy-start | bytes 25165828 | tf_op jit(solution)/shard_map/while
  530.2 9.2 %copy-start.9 = (bf16[8,512,1024]{2,1,0:T(8,128)(2,1)S(1)}, bf16[8,512,1024]{2,1,0:T(8,128)(2,1)}, u32[]{:S(2)}) copy-start(bf16[8,512,1024]{2,1,0:T(8,128)(2,1)} %get-tuple-element.114) | copy-start | bytes 25165828 | tf_op jit(solution)/shard_map/while
  542.2 5.1 copy-start.3
  542.2 76.5 %all-to-all-start.1 = ((bf16[8,384,1024]{2,1,0:T(8,128)(2,1)}), bf16[8,384,1024]{2,1,0:T(8,128)(2,1)}, u32[]{:S(2)}, u32[]{:S(2)}) async-start(bf16[8,384,1024]{2,1,0:T(8,128)(2,1)} %bitcast.71), calls=%async_computation.1 | async-start | bytes 12582912 | tf_op jit(solution)/shard_map/all_to_all | solution.py:121
  618.7 10.9 %copy-start.1 = (bf16[128,1024]{1,0:T(8,128)(2,1)S(1)}, bf16[128,1024]{1,0:T(8,128)(2,1)}, u32[]{:S(2)}) copy-start(bf16[128,1024]{1,0:T(8,128)(2,1)} %param.13) | copy-start | bytes 786436
  627.3 1.5 copy-start.6
Sparse Core Ops, SparseCore 0:
  8.9 48.8 all-gather.3
  59.4 148.2 all-gather.7
  209.3 284.9 all-gather.5
where the time goes:
time: 636 us
  waiting for transfers between devices  522 us (82%)
  matrix products  45 us (7%)
  local copies, waits for them, and re-layouts  24 us (4%)
  other arithmetic  21.4 us (3%)
  between operations  13.3 us (2%)
  starting transfers between devices  9.97 us (2%)
    all_gather x1, waiting for transfers between devices, body(): lax.all_gather(placed_gate_up, 'shard', axis=1, tiled=True)  287 us
    all_to_all x1, waiting for transfers between devices, body(): lax.all_to_all(outbound.reshape(groups, slot_count * capacity, model_widt...  71.6 us
    all_to_all x1, waiting for transfers between devices, body(): lax.all_to_all(answers.reshape(groups, slot_count * capacity, model_width...  71 us
    all_gather x1, waiting for transfers between devices, body(): lax.all_gather(placed_down, 'shard', axis=1, tiled=True)  62 us
    dot_general x4, matrix products, apply_block(): jnp.einsum('bjmd,jdf->bjmf', block_part, gate_up, preferred_element_type=...  36.6 us
    all_gather x1, waiting for transfers between devices, body(): lax.all_gather(output_weight, 'shard', axis=0, tiled=True)  29.2 us
    another operation x3, other arithmetic  18.2 us
  transfers between devices with their start and end apart: 5, of which 5 were waited for; matrix products, arithmetic and copies ran while one was open for 5% of the time, Pallas kernels for 0%

commit v1 on v0

--- a/solution.py
+++ b/solution.py
@@ -1,8 +1,11 @@
+import functools
 import math
 
 import jax
 import jax.numpy as jnp
 from jax import lax
+from jax.experimental import pallas as pl
+from jax.experimental.pallas import tpu as pltpu
 from jax.sharding import PartitionSpec as P
 
 CAP = 48
@@ -15,6 +18,319 @@
 def rms_scale(values, scale_gain):
     mean_square = jnp.mean(values * values, axis=-1, keepdims=True)
     return values * lax.rsqrt(mean_square + eps_norm) * scale_gain
+
+
+bf16 = jnp.bfloat16
+f32 = jnp.float32
+vmem_limit = 48 * 1024 * 1024
+row_tile = 256
+chunk_slots = 2
+
+
+def swap(value, axis, bits):
+    size = lax.axis_size(axis)
+    return lax.ppermute(value, axis, [(i, i ^ bits) for i in range(size)])
+
+
+def hit_table(routes, replica_pick, placement):
+    same = placement[:, None] == placement[None, :]
+    place = jnp.arange(placement.shape[0], dtype=jnp.int32)
+    copies = jnp.sum(same.astype(jnp.int32), axis=1)
+    rank = jnp.sum((same & (place[None, :] < place[:, None])).astype(jnp.int32), axis=1)
+    named = routes[:, :, None] == placement
+    picked = lax.rem(replica_pick[:, :, None], jnp.broadcast_to(copies, named.shape)) == rank
+    return jnp.any(named & picked, axis=1).astype(f32)
+
+
+def project_kernel(where_ref, heads_ref, residual_ref, gain_ref, router_ref, hits_ref, mine_ref, other_ref, rows_ref, hidden_ref, weight, sems):
+    e = where_ref[0]
+    s = where_ref[1]
+    piece = mine_ref.shape[2]
+    chips, shards = mine_ref.shape[0], mine_ref.shape[1]
+    depth = weight.shape[0] // shards
+    copies = []
+    for core, source in enumerate((mine_ref, other_ref)):
+        for chip in range(chips):
+            for k in range(shards):
+                start = pl.multiple_of((s ^ k) * depth + (e ^ (2 * chip + core)) * piece, piece)
+                copies.append(
+                    pltpu.make_async_copy(
+                        source.at[chip, k],
+                        weight.at[pl.ds(start, piece), :],
+                        sems.at[(core * chips + chip) * shards + k],
+                    )
+                )
+    for copy in copies:
+        copy.start()
+    for copy in copies:
+        copy.wait()
+    projected = jnp.dot(heads_ref[...], weight[...], preferred_element_type=f32)
+    hidden = (residual_ref[...].astype(f32) + projected).astype(bf16)
+    hidden_ref[...] = hidden
+    normed = rms_scale(hidden.astype(f32), gain_ref[...]).astype(bf16)
+    width = normed.shape[1]
+    rows_ref[:, :width] = normed
+    logits = jnp.dot(normed, router_ref[...], preferred_element_type=f32)
+    places = logits.shape[1] // 2
+    raised = jnp.where(hits_ref[...] > 0, jnp.exp(logits), 0.0)
+    total = jnp.sum(raised, axis=-1, keepdims=True) * 0.5
+    share = raised / total
+    high = share.astype(bf16)
+    low = (share - high.astype(f32)).astype(bf16)
+    lane = lax.broadcasted_iota(jnp.int32, share.shape, 1)
+    rows_ref[:, width:] = jnp.where(lane < places, high.astype(f32), low.astype(f32)).astype(bf16)
+
+
+def project(where, heads, residual, gain, router_pairs, hits, mine, other):
+    rows, width = residual.shape
+    pieces = 2 * mine.shape[0] * mine.shape[1]
+    vm = pl.BlockSpec(memory_space=pltpu.VMEM)
+    hbm = pl.BlockSpec(memory_space=pl.ANY)
+    return pl.pallas_call(
+        project_kernel,
+        out_shape=(
+            jax.ShapeDtypeStruct((rows, width + router_pairs.shape[1]), bf16),
+            jax.ShapeDtypeStruct((rows, width), bf16),
+        ),
+        in_specs=[pl.BlockSpec(memory_space=pltpu.SMEM), vm, vm, vm, vm, vm, hbm, hbm],
+        out_specs=(vm, vm),
+        scratch_shapes=[
+            pltpu.VMEM((width, width), bf16),
+            pltpu.SemaphoreType.DMA((pieces,)),
+        ],
+        compiler_params=pltpu.CompilerParams(vmem_limit_bytes=vmem_limit),
+        cost_estimate=pl.CostEstimate(flops=2 * rows * width * width, bytes_accessed=3 * width * width, transcendentals=rows * 128),
+        name="project",
+    )(where, heads, residual, gain, router_pairs, hits, mine, other)
+
+
+def load_weights(where_ref, sources, weight, sems):
+    s = where_ref[1]
+    depth = sources[0].shape[1]
+    copies = []
+    for k, source in enumerate(sources):
+        start = pl.multiple_of((s ^ k) * depth, depth)
+        copies.append(pltpu.make_async_copy(source, weight.at[:, pl.ds(start, depth), :], sems.at[k]))
+    return copies
+
+
+def activate(where_ref, x_ref, weight, first_slot, group_slots):
+    slots, width, columns = weight.shape
+    units = columns // 2
+    x = x_ref[:, :width]
+    shares = x_ref[:, width:]
+    first = where_ref[0] * group_slots + first_slot
+    pairs = shares.shape[1]
+    place = lax.broadcasted_iota(jnp.int32, (pairs, slots * units), 0) % (pairs // 2)
+    lane = lax.broadcasted_iota(jnp.int32, (pairs, slots * units), 1) // units
+    spread = jnp.where(place == lane + first, 1.0, 0.0).astype(bf16)
+    factor = jnp.dot(shares, spread, preferred_element_type=f32)
+    parts = []
+    for slot in range(slots):
+        both = jnp.dot(x, weight[slot], preferred_element_type=f32)
+        gate, up = both[:, :units], both[:, units:]
+        act = gate / (1.0 + jnp.exp(-gate)) * up
+        parts.append((act * factor[:, slot * units:(slot + 1) * units]).astype(bf16))
+    return parts
+
+
+def act_kernel(first_slot, group_slots, shards, where_ref, x_ref, *refs):
+    sources, (act_ref, weight, sems) = refs[:shards], refs[shards:]
+
+    @pl.when(pl.program_id(0) == 0)
+    def _():
+        copies = load_weights(where_ref, sources, weight, sems)
+        for copy in copies:
+            copy.start()
+        for copy in copies:
+            copy.wait()
+
+    parts = activate(where_ref, x_ref, weight, first_slot, group_slots)
+    units = parts[0].shape[1]
+    for slot, part in enumerate(parts):
+        act_ref[:, slot * units:(slot + 1) * units] = part
+
+
+def act_block(where, x, sources, first_slot, group_slots):
+    rows, wide = x.shape
+    slots, depth, columns = sources[0].shape
+    units = columns // 2
+    shards = len(sources)
+    hbm = pl.BlockSpec(memory_space=pl.ANY)
+    return pl.pallas_call(
+        functools.partial(act_kernel, first_slot, group_slots, shards),
+        out_shape=jax.ShapeDtypeStruct((rows, slots * units), bf16),
+        grid=(rows // row_tile,),
+        in_specs=[pl.BlockSpec(memory_space=pltpu.SMEM), pl.BlockSpec((row_tile, wide), lambda i: (i, 0))] + [hbm] * shards,
+        out_specs=pl.BlockSpec((row_tile, slots * units), lambda i: (i, 0)),
+        scratch_shapes=[
+            pltpu.VMEM((slots, depth * shards, columns), bf16),
+            pltpu.SemaphoreType.DMA((shards,)),
+        ],
+        compiler_params=pltpu.CompilerParams(vmem_limit_bytes=vmem_limit),
+        cost_estimate=pl.CostEstimate(
+            flops=2 * rows * depth * shards * columns * slots,
+            bytes_accessed=2 * (rows * wide + rows * slots * units + slots * depth * shards * columns),
+            transcendentals=rows * slots * units,
+        ),
+        name="act_block",
+    )(where, x, *sources)
+
+
+def down_kernel(first_slot, group_slots, shards, earlier, where_ref, x_ref, *refs):
+    acts = refs[:earlier]
+    sources = refs[earlier:earlier + shards]
+    down_hbm, out_ref, weight, down, act, sems = refs[earlier + shards:]
+
+    @pl.when(pl.program_id(0) == 0)
+    def _():
+        copies = load_weights(where_ref, sources, weight, sems)
+        copies.append(pltpu.make_async_copy(down_hbm, down, sems.at[shards]))
+        for copy in copies:
+            copy.start()
+        for copy in copies:
+            copy.wait()
+
+    parts = activate(where_ref, x_ref, weight, first_slot, group_slots)
+    units = parts[0].shape[1]
+    at = 0
+    for ref in acts:
+        act[:, at:at + ref.shape[1]] = ref[...]
+        at += ref.shape[1]
+    for part in parts:
+        act[:, at:at + units] = part
+        at += units
+    out_ref[...] = jnp.dot(act[...], down[...], preferred_element_type=f32).astype(bf16)
+
+
+def down_block(where, x, acts, sources, down, first_slot, group_slots):
+    rows, wide = x.shape
+    slots, depth, columns = sources[0].shape
+    units = columns // 2
+    shards = len(sources)
+    total, width = down.shape
+    hbm = pl.BlockSpec(memory_space=pl.ANY)
+    return pl.pallas_call(
+        functools.partial(down_kernel, first_slot, group_slots, shards, len(acts)),
+        out_shape=jax.ShapeDtypeStruct((rows, width), bf16),
+        grid=(rows // row_tile,),
+        in_specs=[pl.BlockSpec(memory_space=pltpu.SMEM), pl.BlockSpec((row_tile, wide), lambda i: (i, 0))]
+        + [pl.BlockSpec((row_tile, a.shape[1]), lambda i: (i, 0)) for a in acts]
+        + [hbm] * (shards + 1),
+        out_specs=pl.BlockSpec((row_tile, width), lambda i: (i, 0)),
+        scratch_shapes=[
+            pltpu.VMEM((slots, depth * shards, columns), bf16),
+            pltpu.VMEM((total, width), bf16),
+            pltpu.VMEM((row_tile, total), bf16),
+            pltpu.SemaphoreType.DMA((shards + 1,)),
+        ],
+        compiler_params=pltpu.CompilerParams(vmem_limit_bytes=vmem_limit),
+        cost_estimate=pl.CostEstimate(
+            flops=2 * rows * (depth * shards * columns * slots + total * width),
+            bytes_accessed=2 * (rows * (wide + total + width) + slots * depth * shards * columns + total * width),
+            transcendentals=rows * slots * units,
+        ),
+        name="down_block",
+    )(where, x, *acts, *sources, down)
+
+
+def plane_gather(block):
+    half = block.shape[0] // 2
+    a, b = block[:half], block[half:]
+    a_x = swap(a, "expert", 2)
+    b_y = swap(b, "expert", 4)
+    a_y = swap(jnp.concatenate([a, a_x]), "expert", 4)
+    b_x = swap(jnp.concatenate([b, b_y]), "expert", 2)
+    mine = jnp.concatenate([a, b, a_x, b_x[:half], a_y[:half], b_y, a_y[half:], b_x[half:]])
+    other = swap(mine, "expert", 1)
+    return jnp.concatenate([mine, other])
+
+
+def add(left, right):
+    return (left.astype(f32) + right.astype(f32)).astype(bf16)
+
+
+def plane_scatter(partial):
+    rows, width = partial.shape
+    half = width // 2
+    other = swap(partial[rows // 2:], "expert", 1)
+    chips = add(partial[:rows // 2], other).reshape(4, rows // 8, width)
+    a, b = chips[..., :half], chips[..., half:]
+    a_x = swap(jnp.stack([a[1], a[3]]), "expert", 2)
+    b_y = swap(b[2:], "expert", 4)
+    a_y = swap(add(a[2], a_x[1]), "expert", 4)
+    b_x = swap(add(b[1], b_y[1]), "expert", 2)
+    left = a[0].astype(f32) + a_x[0].astype(f32) + a_y.astype(f32)
+    right = b[0].astype(f32) + b_y[0].astype(f32) + b_x.astype(f32)
+    return jnp.concatenate([left, right], axis=1)
+
+
+def quarter_body(
+    head_outputs,
+    residual,
+    output_weight,
+    router,
+    norm_gain,
+    placed_gate_up,
+    placed_down,
+    routes,
+    replica_pick,
+    placement,
+    final_gain,
+):
+    rows, width = residual.shape
+    slots, depth, columns = placed_gate_up.shape
+    groups, shards = lax.axis_size("expert"), lax.axis_size("shard")
+    e, s = lax.axis_index("expert"), lax.axis_index("shard")
+    where = jnp.stack([e, s]).astype(jnp.int32)
+    hidden_units = columns // 2
+    units = hidden_units // shards
+
+    piece = output_weight.shape[0] // groups
+    own = lax.dynamic_slice_in_dim(output_weight, e * piece, piece, 0)
+    pieces = jnp.stack([own] + [swap(own, "shard", k) for k in range(1, shards)])
+    mine = jnp.stack([pieces] + [swap(pieces, "expert", 2 * chip) for chip in range(1, groups // 2)])
+    other = swap(mine, "expert", 1)
+
+    def quarter(k, first):
+        at = (s ^ k) * units
+        part = placed_gate_up[first:first + chunk_slots]
+        return jnp.concatenate(
+            [
+                lax.dynamic_slice_in_dim(part, at, units, 2),
+                lax.dynamic_slice_in_dim(part, hidden_units + at, units, 2),
+            ],
+            axis=2,
+        )
+
+    weights = []
+    for first in range(0, slots, chunk_slots):
+        weights.append([quarter(0, first)] + [swap(quarter(k, first), "shard", k) for k in range(1, shards)])
+
+    hits = hit_table(routes, replica_pick, placement)
+    spread = jnp.take(router, placement, axis=1)
+    block, hidden = project(
+        where, head_outputs, residual, norm_gain.reshape(1, -1),
+        jnp.concatenate([spread, spread], axis=1), jnp.concatenate([hits, hits], axis=1), mine, other,
+    )
+
+    xs = [plane_gather(block if k == 0 else swap(block, "shard", k)) for k in range(shards)]
+
+    down = placed_down.reshape(slots * units, width)
+    last = len(weights) - 1
+    total = hidden.astype(f32)
+    acts = [[] for _ in xs]
+    for chunk in range(last):
+        for k in range(shards):
+            acts[k].append(act_block(where, xs[k], weights[chunk], chunk * chunk_slots, slots))
+    sums = []
+    for k in list(range(1, shards)) + [0]:
+        partial = down_block(where, xs[k], acts[k], weights[last], down, last * chunk_slots, slots)
+        mine_sum = plane_scatter(partial)
+        sums.append(swap(mine_sum.astype(bf16), "shard", k).astype(f32) if k else mine_sum)
+    for part in sums:
+        total = total + part
+    return rms_scale(total, final_gain).astype(bf16)
 
 
 def choose_slots(routes, replica_pick, placement, experts):
@@ -132,8 +448,9 @@
 
 
 def solution(mesh):
+    by_quarters = mesh.shape["expert"] == 8 and mesh.shape["shard"] == 4
     return jax.shard_map(
-        body,
+        quarter_body if by_quarters else body,
         mesh=mesh,
         in_specs=(
             P(("expert", "shard"), None),

time: 636 us -> 375 us (0.59)
  waiting for transfers between devices: 522 us -> 154 us
  starting transfers between devices: 9.97 us -> 96.5 us
  Pallas kernels: 0 us -> 66.2 us
  matrix products: 45 us -> 0 us
  between operations: 13.3 us -> 1.18 us
  local copies, waits for them, and re-layouts: 24 us -> 34.1 us
    all_gather x3 -> x0, waiting for transfers between devices: 378 us -> none  [the longest x1 287 us: body(): lax.all_gather(placed_gate_up, 'shard', axis=1, tiled=True)]
    ppermute x0 -> x65, waiting for transfers between devices: none -> 154 us  [swap(): return lax.ppermute(value, axis, [(i, i ^ bits) for i in range(size)])]
    all_to_all x2 -> x0, waiting for transfers between devices: 143 us -> none  [the longest x1 71.6 us: body(): lax.all_to_all(outbound.reshape(groups, slot_count * capacity, model_widt...]
    ppermute x0 -> x65, starting transfers between devices: none -> 96.5 us  [swap(): return lax.ppermute(value, axis, [(i, i ^ bits) for i in range(size)])]
    pallas_call x0 -> x17, Pallas kernels: none -> 66.2 us  [the longest x12 32.7 us: act_block(): pl.pallas_call(functools.partial(act_kernel, first_slot, group_slots, sha...]
    dot_general x10 -> x0, matrix products: 45 us -> none  [the longest x4 36.6 us: apply_block(): jnp.einsum('bjmd,jdf->bjmf', block_part, gate_up, preferred_element_type=...]
    another operation x4 -> x10, other arithmetic: 18.4 us -> 1.58 us  [the longest x2 1.08 us: quarter_body(): jnp.stack([pieces] + [swap(pieces, 'expert', 2 * chip) for chip in range(...]
    unnamed x18 -> x114, local copies, waits for them, and re-layouts: 0.04 us -> 14.1 us
  transfers between devices with their start and end apart: 5 -> 65, of which waited for: 5 -> 32; matrix products, arithmetic and copies ran while one was open for 5% -> 14% of each run, Pallas kernels for 0% -> 18%
where the time goes in v1:
time: 375 us; the launch traced here: 373 us
  waiting for transfers between devices  154 us (41%)
  starting transfers between devices  96.5 us (26%)
  Pallas kernels  66.2 us (18%)
  local copies, waits for them, and re-layouts  34.1 us (9%)
  other arithmetic  20.9 us (6%)
    ppermute x65, waiting for transfers between devices, swap(): return lax.ppermute(value, axis, [(i, i ^ bits) for i in range(size)])  154 us
    ppermute x65, starting transfers between devices, swap(): return lax.ppermute(value, axis, [(i, i ^ bits) for i in range(size)])  96.5 us
    pallas_call x12, Pallas kernels, act_block(): pl.pallas_call(functools.partial(act_kernel, first_slot, group_slots, sha...  32.7 us
    pallas_call x4, Pallas kernels, down_block(): pl.pallas_call(functools.partial(down_kernel, first_slot, group_slots, sh...  28.9 us
    unnamed x114, local copies, waits for them, and re-layouts  14.1 us
    concatenate x16, other arithmetic, quarter(): jnp.concatenate([lax.dynamic_slice_in_dim(part, at, units, 2), lax.dynami...  9.21 us
  transfers between devices with their start and end apart: 65, of which 32 were waited for; matrix products, arithmetic and copies ran while one was open for 14% of the time, Pallas kernels for 18%

profile of v1, /device:TPU:0, one launch (start us, length us, event | category | flops | bytes accessed | tf_op | source)
XLA Modules:
  0.0 372.7 jit_solution(4856217903569814059)
XLA Ops:
  7.3 4.1 %fusion.18 = (bf16[2,256,1024]{2,1,0:T(8,128)(2,1)S(1)}, bf16[2,256,1024]{2,1,0:T(8,128)(2,1)S(1)}, bf16[2,256,1024]{2,1,0:T(8,128)(2,1)}, bf16[2,256,1024]{2,1,0:T(8,128)(2,1)}) fusion(bf16[8,256,1024]{2,1,0:T(8,128)(2,1)} %param.16), kind=kLoop, calls=%fused_computation.181 | loop fusion | bytes 8388608 | tf_op jit(solution)/shard_map/slice | solution.py:297
  16.3 3.5 collective-permute-start.20
  33.5 7.9 %collective-permute-done.4 = bf16[4,32,1024]{2,1,0:T(8,128)(2,1)S(1)} collective-permute-done((bf16[4,32,1024]{2,1,0:T(8,128)(2,1)S(1)}, bf16[4,32,1024]{2,1,0:T(8,128)(2,1)S(1)}, u32[]{:S(2)}, u32[]{:S(2)}) %collective-permute-start.4) | collective-permute-done | bytes 262176 | tf_op jit(solution)/shard_map/ppermute | solution.py:32
  47.4 4.7 %project.1 = (bf16[128,1152]{1,0:T(8,128)(2,1)S(1)}, bf16[128,1024]{1,0:T(8,128)(2,1)S(1)}) custom-call(s32[2]{0:T(128)S(1)} %pad_add_fusion.where_ref, bf16[128,1024]{1,0:T(8,128)(2,1)S(1)} %copy-done.2, bf16[128,1024]{1,0:T(8,128)(2,1)S(1)} %copy-done.3, f32[1,1024]{1,0:T(1,128)S(1)} %bitcast.64, bf16[1024,128]{1,0:T(8,128)(2,1)S(1)} %pad_maximum_fusion.9.router_ref, ...), custom_call_target="tpu_custom_call" | custom-call | flops 268435456 | bytes 3145728 | tf_op jit(solution)/shard_map/project/pallas_call | solution.py:89
  54.1 4.4 %collective-permute-done.56 = bf16[64,1152]{1,0:T(8,128)(2,1)S(1)} collective-permute-done((bf16[64,1152]{1,0:T(8,128)(2,1)S(1)}, bf16[64,1152]{1,0:T(8,128)(2,1)S(1)}, u32[]{:S(2)}, u32[]{:S(2)}) %collective-permute-start.56) | collective-permute-done | bytes 147488 | tf_op jit(solution)/shard_map/ppermute | solution.py:32
  60.1 3.6 collective-permute-done.55
  68.0 17.8 %collective-permute-done.31 = bf16[128,1152]{1,0:T(8,128)(2,1)S(1)} collective-permute-done((bf16[128,1152]{1,0:T(8,128)(2,1)S(1)}, bf16[128,1152]{1,0:T(8,128)(2,1)S(1)}, u32[]{:S(2)}, u32[]{:S(2)}) %collective-permute-start.31) | collective-permute-done | bytes 294944 | tf_op jit(solution)/shard_map/ppermute | solution.py:32
  94.1 3.8 %collective-permute-done.9 = bf16[64,1152]{1,0:T(8,128)(2,1)S(1)} collective-permute-done((bf16[64,1152]{1,0:T(8,128)(2,1)S(1)}, bf16[64,1152]{1,0:T(8,128)(2,1)S(1)}, u32[]{:S(2)}, u32[]{:S(2)}) %collective-permute-start.9) | collective-permute-done | bytes 147488 | tf_op jit(solution)/shard_map/ppermute | solution.py:32
  99.3 3.8 %collective-permute-done.8 = bf16[64,1152]{1,0:T(8,128)(2,1)S(1)} collective-permute-done((bf16[64,1152]{1,0:T(8,128)(2,1)S(1)}, bf16[64,1152]{1,0:T(8,128)(2,1)S(1)}, u32[]{:S(2)}, u32[]{:S(2)}) %collective-permute-start.8) | collective-permute-done | bytes 147488 | tf_op jit(solution)/shard_map/ppermute | solution.py:32
  104.6 3.6 collective-permute-done.33
  109.5 3.8 %collective-permute-done.32 = bf16[64,1152]{1,0:T(8,128)(2,1)S(1)} collective-permute-done((bf16[64,1152]{1,0:T(8,128)(2,1)S(1)}, bf16[64,1152]{1,0:T(8,128)(2,1)S(1)}, u32[]{:S(2)}, u32[]{:S(2)}) %collective-permute-start.32) | collective-permute-done | bytes 147488 | tf_op jit(solution)/shard_map/ppermute | solution.py:32
  114.9 3.6 collective-permute-done.45
  119.8 3.8 %collective-permute-done.44 = bf16[64,1152]{1,0:T(8,128)(2,1)S(1)} collective-permute-done((bf16[64,1152]{1,0:T(8,128)(2,1)S(1)}, bf16[64,1152]{1,0:T(8,128)(2,1)S(1)}, u32[]{:S(2)}, u32[]{:S(2)}) %collective-permute-start.44) | collective-permute-done | bytes 147488 | tf_op jit(solution)/shard_map/ppermute | solution.py:32
  123.6 6.2 %collective-permute-start.16 = (bf16[2,256,256]{2,1,0:T(8,128)(2,1)}, bf16[2,256,256]{2,1,0:T(8,128)(2,1)S(1)}, u32[]{:S(2)}, u32[]{:S(2)}) collective-permute-start(bf16[2,256,256]{2,1,0:T(8,128)(2,1)} %pad_maximum_fusion.16), channel_id=1, source_target_pairs={{0,1},{1,0},{2,3},{3,2},{4,5},{5,4},{6,7},{7,6},{8,9},{9,8},{10,11... | collective-permute-start | bytes 786440 | tf_op jit(solution)/shard_map/ppermute | solution.py:32
  139.3 5.9 %collective-permute-done.11 = bf16[128,1152]{1,0:T(8,128)(2,1)S(1)} collective-permute-done((bf16[128,1152]{1,0:T(8,128)(2,1)S(1)}, bf16[128,1152]{1,0:T(8,128)(2,1)S(1)}, u32[]{:S(2)}, u32[]{:S(2)}) %collective-permute-start.11) | collective-permute-done | bytes 294944 | tf_op jit(solution)/shard_map/ppermute | solution.py:32
  149.5 5.0 %collective-permute-done.34 = bf16[128,1152]{1,0:T(8,128)(2,1)S(1)} collective-permute-done((bf16[128,1152]{1,0:T(8,128)(2,1)S(1)}, bf16[128,1152]{1,0:T(8,128)(2,1)S(1)}, u32[]{:S(2)}, u32[]{:S(2)}) %collective-permute-start.34) | collective-permute-done | bytes 294944 | tf_op jit(solution)/shard_map/ppermute | solution.py:32
  156.7 7.0 %collective-permute-done.35 = bf16[128,1152]{1,0:T(8,128)(2,1)S(1)} collective-permute-done((bf16[128,1152]{1,0:T(8,128)(2,1)S(1)}, bf16[128,1152]{1,0:T(8,128)(2,1)S(1)}, u32[]{:S(2)}, u32[]{:S(2)}) %collective-permute-start.35) | collective-permute-done | bytes 294944 | tf_op jit(solution)/shard_map/ppermute | solution.py:32
  172.7 4.5 %collective-permute-done.47 = bf16[128,1152]{1,0:T(8,128)(2,1)S(1)} collective-permute-done((bf16[128,1152]{1,0:T(8,128)(2,1)S(1)}, bf16[128,1152]{1,0:T(8,128)(2,1)S(1)}, u32[]{:S(2)}, u32[]{:S(2)}) %collective-permute-start.47) | collective-permute-done | bytes 294944 | tf_op jit(solution)/shard_map/ppermute | solution.py:32
  180.7 3.6 collective-permute-start.18
  184.6 17.0 %collective-permute-done.17.refs_2_ = bf16[2,256,256]{2,1,0:T(8,128)(2,1)S(1)} collective-permute-done((bf16[2,256,256]{2,1,0:T(8,128)(2,1)}, bf16[2,256,256]{2,1,0:T(8,128)(2,1)S(1)}, u32[]{:S(2)}, u32[]{:S(2)}) %collective-permute-start.17) | collective-permute-done | bytes 262176 | tf_op jit(solution)/shard_map/ppermute | solution.py:32
  202.7 16.3 %collective-permute-start.22 = (bf16[2,256,256]{2,1,0:T(8,128)(2,1)}, bf16[2,256,256]{2,1,0:T(8,128)(2,1)S(1)}, u32[]{:S(2)}, u32[]{:S(2)}) collective-permute-start(bf16[2,256,256]{2,1,0:T(8,128)(2,1)} %pad_maximum_fusion.24), channel_id=1, source_target_pairs={{0,1},{1,0},{2,3},{3,2},{4,5},{5,4},{6,7},{7,6},{8,9},{9,8},{10,11... | collective-permute-start | bytes 786440 | tf_op jit(solution)/shard_map/ppermute | solution.py:32
  219.0 5.1 %collective-permute-done.14.refs_2_ = bf16[2,256,256]{2,1,0:T(8,128)(2,1)S(1)} collective-permute-done((bf16[2,256,256]{2,1,0:T(8,128)(2,1)S(1)}, bf16[2,256,256]{2,1,0:T(8,128)(2,1)S(1)}, u32[]{:S(2)}, u32[]{:S(2)}) %collective-permute-start.14) | collective-permute-done | bytes 262176 | tf_op jit(solution)/shard_map/ppermute | solution.py:32
  233.8 12.8 %collective-permute-done.23.refs_5_ = bf16[2,256,256]{2,1,0:T(8,128)(2,1)S(1)} collective-permute-done((bf16[2,256,256]{2,1,0:T(8,128)(2,1)}, bf16[2,256,256]{2,1,0:T(8,128)(2,1)S(1)}, u32[]{:S(2)}, u32[]{:S(2)}) %collective-permute-start.23) | collective-permute-done | bytes 262176 | tf_op jit(solution)/shard_map/ppermute | solution.py:32
  246.6 7.3 %down_block.7 = bf16[1024,1024]{1,0:T(8,128)(2,1)S(1)} custom-call(s32[2]{0:T(128)S(1)} %pad_add_fusion.where_ref, bf16[1024,1152]{1,0:T(8,128)(2,1)} %copy-done.9, bf16[1024,256]{1,0:T(8,128)(2,1)S(1)} %act_block.21.refs_0_, bf16[1024,256]{1,0:T(8,128)(2,1)S(1)} %act_block.22.refs_1_, bf16[1024,256]{1,0:T(8,128)(2,1)S(1)} %act_block.23.refs_2_, ...), custom_call_target="tpu_custom_call" | custom-call | flops 3221225472 | bytes 9699328 | tf_op jit(solution)/shard_map/down_block/pallas_call | solution.py:213
  264.6 7.2 %down_block.4 = bf16[1024,1024]{1,0:T(8,128)(2,1)S(1)} custom-call(s32[2]{0:T(128)S(1)} %pad_add_fusion.where_ref, bf16[1024,1152]{1,0:T(8,128)(2,1)} %copy-done.4, bf16[1024,256]{1,0:T(8,128)(2,1)S(1)} %act_block.12.refs_0_, bf16[1024,256]{1,0:T(8,128)(2,1)S(1)} %act_block.13.refs_1_, bf16[1024,256]{1,0:T(8,128)(2,1)S(1)} %act_block.14.refs_2_, ...), custom_call_target="tpu_custom_call" | custom-call | flops 3221225472 | bytes 9699328 | tf_op jit(solution)/shard_map/down_block/pallas_call | solution.py:213
  283.2 7.3 %down_block.5 = bf16[1024,1024]{1,0:T(8,128)(2,1)S(1)} custom-call(s32[2]{0:T(128)S(1)} %pad_add_fusion.where_ref, bf16[1024,1152]{1,0:T(8,128)(2,1)} %copy-done.8, bf16[1024,256]{1,0:T(8,128)(2,1)S(1)} %act_block.15.refs_0_, bf16[1024,256]{1,0:T(8,128)(2,1)S(1)} %act_block.16.refs_1_, bf16[1024,256]{1,0:T(8,128)(2,1)S(1)} %act_block.17.refs_2_, ...), custom_call_target="tpu_custom_call" | custom-call | flops 3221225472 | bytes 9699328 | tf_op jit(solution)/shard_map/down_block/pallas_call | solution.py:213
  306.1 7.1 %down_block.6 = bf16[1024,1024]{1,0:T(8,128)(2,1)S(1)} custom-call(s32[2]{0:T(128)S(1)} %pad_add_fusion.where_ref, bf16[1024,1152]{1,0:T(8,128)(2,1)} %copy-done.5, bf16[1024,256]{1,0:T(8,128)(2,1)S(1)} %act_block.18.refs_0_, bf16[1024,256]{1,0:T(8,128)(2,1)S(1)} %act_block.19.refs_1_, bf16[1024,256]{1,0:T(8,128)(2,1)S(1)} %act_block.20.refs_2_, ...), custom_call_target="tpu_custom_call" | custom-call | flops 3221225472 | bytes 9699328 | tf_op jit(solution)/shard_map/down_block/pallas_call | solution.py:213
  327.2 4.2 %collective-permute-done.38 = bf16[2,128,512]{2,1,0:T(8,128)(2,1)S(1)} collective-permute-done((bf16[2,128,512]{2,1,0:T(8,128)(2,1)S(1)}, bf16[2,128,512]{2,1,0:T(8,128)(2,1)S(1)}, u32[]{:S(2)}, u32[]{:S(2)}) %collective-permute-start.38) | collective-permute-done | bytes 262176 | tf_op jit(solution)/shard_map/ppermute | solution.py:32
  332.8 4.2 %collective-permute-done.50 = bf16[2,128,512]{2,1,0:T(8,128)(2,1)S(1)} collective-permute-done((bf16[2,128,512]{2,1,0:T(8,128)(2,1)S(1)}, bf16[2,128,512]{2,1,0:T(8,128)(2,1)S(1)}, u32[]{:S(2)}, u32[]{:S(2)}) %collective-permute-start.50) | collective-permute-done | bytes 262176 | tf_op jit(solution)/shard_map/ppermute | solution.py:32
  346.4 5.7 %collective-permute-start.30 = (bf16[128,1024]{1,0:T(8,128)(2,1)S(1)}, bf16[128,1024]{1,0:T(8,128)(2,1)S(1)}, u32[]{:S(2)}, u32[]{:S(2)}) collective-permute-start(bf16[128,1024]{1,0:T(8,128)(2,1)S(1)} %pad_maximum_fusion.28), channel_id=1, source_target_pairs={{0,1},{1,0},{2,3},{3,2},{4,5},{5,4},{6,7},{7,6},{8,9},{9,8},{10,11... | collective-permute-start | bytes 786440 | tf_op jit(solution)/shard_map/ppermute | solution.py:32
  356.6 3.8 %collective-permute-done.30 = bf16[128,1024]{1,0:T(8,128)(2,1)S(1)} collective-permute-done((bf16[128,1024]{1,0:T(8,128)(2,1)S(1)}, bf16[128,1024]{1,0:T(8,128)(2,1)S(1)}, u32[]{:S(2)}, u32[]{:S(2)}) %collective-permute-start.30) | collective-permute-done | bytes 262176 | tf_op jit(solution)/shard_map/ppermute | solution.py:32
  360.5 11.1 %collective-permute-done.42 = bf16[128,1024]{1,0:T(8,128)(2,1)S(1)} collective-permute-done((bf16[128,1024]{1,0:T(8,128)(2,1)S(1)}, bf16[128,1024]{1,0:T(8,128)(2,1)S(1)}, u32[]{:S(2)}, u32[]{:S(2)}) %collective-permute-start.42) | collective-permute-done | bytes 262176 | tf_op jit(solution)/shard_map/ppermute | solution.py:32
  (318 shorter events, 162.0 us)
Async XLA Ops:
  1.7 26.4 %collective-permute-start = (bf16[32,1024]{1,0:T(8,128)(2,1)}, bf16[32,1024]{1,0:T(8,128)(2,1)}, u32[]{:S(2)}, u32[]{:S(2)}) collective-permute-start(bf16[32,1024]{1,0:T(8,128)(2,1)} %constant_dynamic-slice_fusion.32), channel_id=1, source_target_pairs={{0,1},{1,0},{2,3},{3,2},{4,5},{5,4},{6,7},{7,6},{8,9},{9,8},{10,11... | collective-permute-start | bytes 196616 | tf_op jit(solution)/shard_map/ppermute | solution.py:32
  4.7 23.4 %collective-permute-start.1 = (bf16[32,1024]{1,0:T(8,128)(2,1)}, bf16[32,1024]{1,0:T(8,128)(2,1)}, u32[]{:S(2)}, u32[]{:S(2)}) collective-permute-start(bf16[32,1024]{1,0:T(8,128)(2,1)} %constant_dynamic-slice_fusion.32), channel_id=1, source_target_pairs={{0,2},{1,3},{2,0},{3,1},{4,6},{5,7},{6,4},{7,5},{8,10},{9,11},{10,... | collective-permute-start | bytes 196616 | tf_op jit(solution)/shard_map/ppermute | solution.py:32
  7.3 20.8 %collective-permute-start.2 = (bf16[32,1024]{1,0:T(8,128)(2,1)}, bf16[32,1024]{1,0:T(8,128)(2,1)}, u32[]{:S(2)}, u32[]{:S(2)}) collective-permute-start(bf16[32,1024]{1,0:T(8,128)(2,1)} %constant_dynamic-slice_fusion.32), channel_id=1, source_target_pairs={{0,3},{1,2},{2,1},{3,0},{4,7},{5,6},{6,5},{7,4},{8,11},{9,10},{10,... | collective-permute-start | bytes 196616 | tf_op jit(solution)/shard_map/ppermute | solution.py:32
  14.7 165.4 %collective-permute-start.19 = (bf16[2,256,256]{2,1,0:T(8,128)(2,1)}, bf16[2,256,256]{2,1,0:T(8,128)(2,1)S(1)}, u32[]{:S(2)}, u32[]{:S(2)}) collective-permute-start(bf16[2,256,256]{2,1,0:T(8,128)(2,1)} %pad_maximum_fusion.20), channel_id=1, source_target_pairs={{0,1},{1,0},{2,3},{3,2},{4,5},{5,4},{6,7},{7,6},{8,9},{9,8},{10,11... | collective-permute-start | bytes 786440 | tf_op jit(solution)/shard_map/ppermute | solution.py:32
  16.3 163.8 %collective-permute-start.20 = (bf16[2,256,256]{2,1,0:T(8,128)(2,1)}, bf16[2,256,256]{2,1,0:T(8,128)(2,1)S(1)}, u32[]{:S(2)}, u32[]{:S(2)}) collective-permute-start(bf16[2,256,256]{2,1,0:T(8,128)(2,1)} %pad_maximum_fusion.21), channel_id=1, source_target_pairs={{0,2},{1,3},{2,0},{3,1},{4,6},{5,7},{6,4},{7,5},{8,10},{9,11},{10,... | collective-permute-start | bytes 786440 | tf_op jit(solution)/shard_map/ppermute | solution.py:32
  29.0 12.3 %collective-permute-start.4 = (bf16[4,32,1024]{2,1,0:T(8,128)(2,1)S(1)}, bf16[4,32,1024]{2,1,0:T(8,128)(2,1)S(1)}, u32[]{:S(2)}, u32[]{:S(2)}) collective-permute-start(bf16[4,32,1024]{2,1,0:T(8,128)(2,1)S(1)} %get-tuple-element.96), channel_id=1, source_target_pairs={{0,16},{4,20},{8,24},{12,28},{16,0},{20,4},{24,8},{28,12},{1,17},{... | collective-permute-start | bytes 786440 | tf_op jit(solution)/shard_map/ppermute | solution.py:32
  41.4 139.3 %collective-permute-start.21 = (bf16[2,256,256]{2,1,0:T(8,128)(2,1)S(1)}, bf16[2,256,256]{2,1,0:T(8,128)(2,1)S(1)}, u32[]{:S(2)}, u32[]{:S(2)}) collective-permute-start(bf16[2,256,256]{2,1,0:T(8,128)(2,1)S(1)} %pad_maximum_fusion.22), channel_id=1, source_target_pairs={{0,3},{1,2},{2,1},{3,0},{4,7},{5,6},{6,5},{7,4},{8,11},{9,10},{10,... | collective-permute-start | bytes 786440 | tf_op jit(solution)/shard_map/ppermute | solution.py:32
  52.1 14.5 %collective-permute-start.7 = (bf16[128,1152]{1,0:T(8,128)(2,1)S(1)}, bf16[128,1152]{1,0:T(8,128)(2,1)S(1)}, u32[]{:S(2)}, u32[]{:S(2)}) collective-permute-start(bf16[128,1152]{1,0:T(8,128)(2,1)S(1)} %get-tuple-element.8), channel_id=1, source_target_pairs={{0,1},{1,0},{2,3},{3,2},{4,5},{5,4},{6,7},{7,6},{8,9},{9,8},{10,11... | collective-permute-start | bytes 884744 | tf_op jit(solution)/shard_map/ppermute | solution.py:32
  63.7 22.0 %collective-permute-start.31 = (bf16[128,1152]{1,0:T(8,128)(2,1)S(1)}, bf16[128,1152]{1,0:T(8,128)(2,1)S(1)}, u32[]{:S(2)}, u32[]{:S(2)}) collective-permute-start(bf16[128,1152]{1,0:T(8,128)(2,1)S(1)} %get-tuple-element.8), channel_id=1, source_target_pairs={{0,2},{1,3},{2,0},{3,1},{4,6},{5,7},{6,4},{7,5},{8,10},{9,11},{10,... | collective-permute-start | bytes 884744 | tf_op jit(solution)/shard_map/ppermute | solution.py:32
  66.7 21.4 %collective-permute-start.43 = (bf16[128,1152]{1,0:T(8,128)(2,1)S(1)}, bf16[128,1152]{1,0:T(8,128)(2,1)S(1)}, u32[]{:S(2)}, u32[]{:S(2)}) collective-permute-start(bf16[128,1152]{1,0:T(8,128)(2,1)S(1)} %get-tuple-element.8), channel_id=1, source_target_pairs={{0,3},{1,2},{2,1},{3,0},{4,7},{5,6},{6,5},{7,4},{8,11},{9,10},{10,... | collective-permute-start | bytes 884744 | tf_op jit(solution)/shard_map/ppermute | solution.py:32
  88.0 41.8 %collective-permute-start.58 = (bf16[128,1152]{1,0:T(8,128)(2,1)S(1)}, bf16[128,1152]{1,0:T(8,128)(2,1)S(1)}, u32[]{:S(2)}, u32[]{:S(2)}) collective-permute-start(bf16[128,1152]{1,0:T(8,128)(2,1)S(1)} %pad_maximum_fusion.8), channel_id=1, source_target_pairs={{0,16},{4,20},{8,24},{12,28},{16,0},{20,4},{24,8},{28,12},{1,17},{... | collective-permute-start | bytes 884744 | tf_op jit(solution)/shard_map/ppermute | solution.py:32
  123.6 60.7 %collective-permute-start.16 = (bf16[2,256,256]{2,1,0:T(8,128)(2,1)}, bf16[2,256,256]{2,1,0:T(8,128)(2,1)S(1)}, u32[]{:S(2)}, u32[]{:S(2)}) collective-permute-start(bf16[2,256,256]{2,1,0:T(8,128)(2,1)} %pad_maximum_fusion.16), channel_id=1, source_target_pairs={{0,1},{1,0},{2,3},{3,2},{4,5},{5,4},{6,7},{7,6},{8,9},{9,8},{10,11... | collective-permute-start | bytes 786440 | tf_op jit(solution)/shard_map/ppermute | solution.py:32
  177.2 24.4 %collective-permute-start.59 = (bf16[512,1152]{1,0:T(8,128)(2,1)S(1)}, bf16[512,1152]{1,0:T(8,128)(2,1)S(1)}, u32[]{:S(2)}, u32[]{:S(2)}) collective-permute-start(bf16[512,1152]{1,0:T(8,128)(2,1)S(1)} %get-tuple-element.89), channel_id=1, source_target_pairs={{0,4},{4,0},{8,12},{12,8},{16,20},{20,16},{24,28},{28,24},{1,5},{5... | collective-permute-start | bytes 3538952 | tf_op jit(solution)/shard_map/ppermute | solution.py:32
  180.0 21.6 %collective-permute-start.17 = (bf16[2,256,256]{2,1,0:T(8,128)(2,1)}, bf16[2,256,256]{2,1,0:T(8,128)(2,1)S(1)}, u32[]{:S(2)}, u32[]{:S(2)}) collective-permute-start(bf16[2,256,256]{2,1,0:T(8,128)(2,1)} %pad_maximum_fusion.17), channel_id=1, source_target_pairs={{0,2},{1,3},{2,0},{3,1},{4,6},{5,7},{6,4},{7,5},{8,10},{9,11},{10,... | collective-permute-start | bytes 786440 | tf_op jit(solution)/shard_map/ppermute | solution.py:32
  180.1 74.8 %collective-permute-start.12 = (bf16[512,1152]{1,0:T(8,128)(2,1)}, bf16[512,1152]{1,0:T(8,128)(2,1)}, u32[]{:S(2)}, u32[]{:S(2)}) collective-permute-start(bf16[512,1152]{1,0:T(8,128)(2,1)} %get-tuple-element.71), channel_id=1, source_target_pairs={{0,4},{4,0},{8,12},{12,8},{16,20},{20,16},{24,28},{28,24},{1,5},{5... | collective-permute-start | bytes 3538952 | tf_op jit(solution)/shard_map/ppermute | solution.py:32
  180.7 22.0 %collective-permute-start.18 = (bf16[2,256,256]{2,1,0:T(8,128)(2,1)S(1)}, bf16[2,256,256]{2,1,0:T(8,128)(2,1)S(1)}, u32[]{:S(2)}, u32[]{:S(2)}) collective-permute-start(bf16[2,256,256]{2,1,0:T(8,128)(2,1)S(1)} %copy-done.29), channel_id=1, source_target_pairs={{0,3},{1,2},{2,1},{3,0},{4,7},{5,6},{6,5},{7,4},{8,11},{9,10},{10,... | collective-permute-start | bytes 786440 | tf_op jit(solution)/shard_map/ppermute | solution.py:32
  184.3 34.7 %collective-permute-start.13 = (bf16[2,256,256]{2,1,0:T(8,128)(2,1)S(1)}, bf16[2,256,256]{2,1,0:T(8,128)(2,1)S(1)}, u32[]{:S(2)}, u32[]{:S(2)}) collective-permute-start(bf16[2,256,256]{2,1,0:T(8,128)(2,1)S(1)} %copy-done.32), channel_id=1, source_target_pairs={{0,1},{1,0},{2,3},{3,2},{4,5},{5,4},{6,7},{7,6},{8,9},{9,8},{10,11... | collective-permute-start | bytes 786440 | tf_op jit(solution)/shard_map/ppermute | solution.py:32
  201.6 22.5 %collective-permute-start.14 = (bf16[2,256,256]{2,1,0:T(8,128)(2,1)S(1)}, bf16[2,256,256]{2,1,0:T(8,128)(2,1)S(1)}, u32[]{:S(2)}, u32[]{:S(2)}) collective-permute-start(bf16[2,256,256]{2,1,0:T(8,128)(2,1)S(1)} %copy-done.31), channel_id=1, source_target_pairs={{0,2},{1,3},{2,0},{3,1},{4,6},{5,7},{6,4},{7,5},{8,10},{9,11},{10,... | collective-permute-start | bytes 786440 | tf_op jit(solution)/shard_map/ppermute | solution.py:32
  201.6 28.8 %collective-permute-start.15 = (bf16[2,256,256]{2,1,0:T(8,128)(2,1)S(1)}, bf16[2,256,256]{2,1,0:T(8,128)(2,1)S(1)}, u32[]{:S(2)}, u32[]{:S(2)}) collective-permute-start(bf16[2,256,256]{2,1,0:T(8,128)(2,1)S(1)} %copy-done.30), channel_id=1, source_target_pairs={{0,3},{1,2},{2,1},{3,0},{4,7},{5,6},{6,5},{7,4},{8,11},{9,10},{10,... | collective-permute-start | bytes 786440 | tf_op jit(solution)/shard_map/ppermute | solution.py:32
  202.7 30.5 %collective-permute-start.22 = (bf16[2,256,256]{2,1,0:T(8,128)(2,1)}, bf16[2,256,256]{2,1,0:T(8,128)(2,1)S(1)}, u32[]{:S(2)}, u32[]{:S(2)}) collective-permute-start(bf16[2,256,256]{2,1,0:T(8,128)(2,1)} %pad_maximum_fusion.24), channel_id=1, source_target_pairs={{0,1},{1,0},{2,3},{3,2},{4,5},{5,4},{6,7},{7,6},{8,9},{9,8},{10,11... | collective-permute-start | bytes 786440 | tf_op jit(solution)/shard_map/ppermute | solution.py:32
  219.0 27.6 %collective-permute-start.23 = (bf16[2,256,256]{2,1,0:T(8,128)(2,1)}, bf16[2,256,256]{2,1,0:T(8,128)(2,1)S(1)}, u32[]{:S(2)}, u32[]{:S(2)}) collective-permute-start(bf16[2,256,256]{2,1,0:T(8,128)(2,1)} %pad_maximum_fusion.25), channel_id=1, source_target_pairs={{0,2},{1,3},{2,0},{3,1},{4,6},{5,7},{6,4},{7,5},{8,10},{9,11},{10,... | collective-permute-start | bytes 786440 | tf_op jit(solution)/shard_map/ppermute | solution.py:32
  224.1 22.5 %collective-permute-start.24 = (bf16[2,256,256]{2,1,0:T(8,128)(2,1)}, bf16[2,256,256]{2,1,0:T(8,128)(2,1)S(1)}, u32[]{:S(2)}, u32[]{:S(2)}) collective-permute-start(bf16[2,256,256]{2,1,0:T(8,128)(2,1)} %pad_maximum_fusion.26), channel_id=1, source_target_pairs={{0,3},{1,2},{2,1},{3,0},{4,7},{5,6},{6,5},{7,4},{8,11},{9,10},{10,... | collective-permute-start | bytes 786440 | tf_op jit(solution)/shard_map/ppermute | solution.py:32
  230.4 43.1 %collective-permute-start.36 = (bf16[512,1152]{1,0:T(8,128)(2,1)}, bf16[512,1152]{1,0:T(8,128)(2,1)}, u32[]{:S(2)}, u32[]{:S(2)}) collective-permute-start(bf16[512,1152]{1,0:T(8,128)(2,1)} %get-tuple-element.77), channel_id=1, source_target_pairs={{0,4},{4,0},{8,12},{12,8},{16,20},{20,16},{24,28},{28,24},{1,5},{5... | collective-permute-start | bytes 3538952 | tf_op jit(solution)/shard_map/ppermute | solution.py:32
  233.3 58.3 %collective-permute-start.48 = (bf16[512,1152]{1,0:T(8,128)(2,1)}, bf16[512,1152]{1,0:T(8,128)(2,1)}, u32[]{:S(2)}, u32[]{:S(2)}) collective-permute-start(bf16[512,1152]{1,0:T(8,128)(2,1)} %get-tuple-element.83), channel_id=1, source_target_pairs={{0,4},{4,0},{8,12},{12,8},{16,20},{20,16},{24,28},{28,24},{1,5},{5... | collective-permute-start | bytes 3538952 | tf_op jit(solution)/shard_map/ppermute | solution.py:32
  254.9 46.4 %collective-permute-start.60 = (bf16[512,1024]{1,0:T(8,128)(2,1)}, bf16[512,1024]{1,0:T(8,128)(2,1)}, u32[]{:S(2)}, u32[]{:S(2)}) collective-permute-start(bf16[512,1024]{1,0:T(8,128)(2,1)} %slice.440), channel_id=1, source_target_pairs={{0,4},{4,0},{8,12},{12,8},{16,20},{20,16},{24,28},{28,24},{1,5},{5... | collective-permute-start | bytes 3145736 | tf_op jit(solution)/shard_map/ppermute | solution.py:32
  273.0 41.7 %collective-permute-start.25 = (bf16[512,1024]{1,0:T(8,128)(2,1)}, bf16[512,1024]{1,0:T(8,128)(2,1)}, u32[]{:S(2)}, u32[]{:S(2)}) collective-permute-start(bf16[512,1024]{1,0:T(8,128)(2,1)} %slice.385), channel_id=1, source_target_pairs={{0,4},{4,0},{8,12},{12,8},{16,20},{20,16},{24,28},{28,24},{1,5},{5... | collective-permute-start | bytes 3145736 | tf_op jit(solution)/shard_map/ppermute | solution.py:32
  291.6 26.3 %collective-permute-start.37 = (bf16[512,1024]{1,0:T(8,128)(2,1)}, bf16[512,1024]{1,0:T(8,128)(2,1)}, u32[]{:S(2)}, u32[]{:S(2)}) collective-permute-start(bf16[512,1024]{1,0:T(8,128)(2,1)} %slice.404), channel_id=1, source_target_pairs={{0,4},{4,0},{8,12},{12,8},{16,20},{20,16},{24,28},{28,24},{1,5},{5... | collective-permute-start | bytes 3145736 | tf_op jit(solution)/shard_map/ppermute | solution.py:32
  313.5 43.1 %collective-permute-start.62 = (bf16[128,512]{1,0:T(8,128)(2,1)S(1)}, bf16[128,512]{1,0:T(8,128)(2,1)S(1)}, u32[]{:S(2)}, u32[]{:S(2)}) collective-permute-start(bf16[128,512]{1,0:T(8,128)(2,1)S(1)} %get-tuple-element.35), channel_id=1, source_target_pairs={{0,16},{4,20},{8,24},{12,28},{16,0},{20,4},{24,8},{28,12},{1,17},{... | collective-permute-start | bytes 393224 | tf_op jit(solution)/shard_map/ppermute | solution.py:32
  331.4 25.2 %collective-permute-start.64 = (bf16[128,512]{1,0:T(8,128)(2,1)S(1)}, bf16[128,512]{1,0:T(8,128)(2,1)S(1)}, u32[]{:S(2)}, u32[]{:S(2)}) collective-permute-start(bf16[128,512]{1,0:T(8,128)(2,1)S(1)} %get-tuple-element.36), channel_id=1, source_target_pairs={{0,8},{4,12},{8,0},{12,4},{16,24},{20,28},{24,16},{28,20},{1,9},{5... | collective-permute-start | bytes 393224 | tf_op jit(solution)/shard_map/ppermute | solution.py:32
  346.4 14.1 %collective-permute-start.30 = (bf16[128,1024]{1,0:T(8,128)(2,1)S(1)}, bf16[128,1024]{1,0:T(8,128)(2,1)S(1)}, u32[]{:S(2)}, u32[]{:S(2)}) collective-permute-start(bf16[128,1024]{1,0:T(8,128)(2,1)S(1)} %pad_maximum_fusion.28), channel_id=1, source_target_pairs={{0,1},{1,0},{2,3},{3,2},{4,5},{5,4},{6,7},{7,6},{8,9},{9,8},{10,11... | collective-permute-start | bytes 786440 | tf_op jit(solution)/shard_map/ppermute | solution.py:32
  352.2 19.3 %collective-permute-start.42 = (bf16[128,1024]{1,0:T(8,128)(2,1)S(1)}, bf16[128,1024]{1,0:T(8,128)(2,1)S(1)}, u32[]{:S(2)}, u32[]{:S(2)}) collective-permute-start(bf16[128,1024]{1,0:T(8,128)(2,1)S(1)} %pad_maximum_fusion.30), channel_id=1, source_target_pairs={{0,2},{1,3},{2,0},{3,1},{4,6},{5,7},{6,4},{7,5},{8,10},{9,11},{10,... | collective-permute-start | bytes 786440 | tf_op jit(solution)/shard_map/ppermute | solution.py:32
  353.8 17.8 %collective-permute-start.54 = (bf16[128,1024]{1,0:T(8,128)(2,1)S(1)}, bf16[128,1024]{1,0:T(8,128)(2,1)S(1)}, u32[]{:S(2)}, u32[]{:S(2)}) collective-permute-start(bf16[128,1024]{1,0:T(8,128)(2,1)S(1)} %pad_maximum_fusion.32), channel_id=1, source_target_pairs={{0,3},{1,2},{2,1},{3,0},{4,7},{5,6},{6,5},{7,4},{8,11},{9,10},{10,... | collective-permute-start | bytes 786440 | tf_op jit(solution)/shard_map/ppermute | solution.py:32
  (70 other events, 756.1 us)

commit v2 on v0

--- a/solution.py
+++ b/solution.py
@@ -1,8 +1,11 @@
+import functools
 import math
 
 import jax
 import jax.numpy as jnp
 from jax import lax
+from jax.experimental import pallas as pl
+from jax.experimental.pallas import tpu as pltpu
 from jax.sharding import PartitionSpec as P
 
 CAP = 48
@@ -15,6 +18,427 @@
 def rms_scale(values, scale_gain):
     mean_square = jnp.mean(values * values, axis=-1, keepdims=True)
     return values * lax.rsqrt(mean_square + eps_norm) * scale_gain
+
+
+bf16 = jnp.bfloat16
+f32 = jnp.float32
+vmem_limit = 62 * 1024 * 1024
+tile_rows = 512
+chunks = ((0, 3), (3, 3), (6, 2))
+any_space = pl.BlockSpec(memory_space=pl.ANY)
+in_vmem = pl.BlockSpec(memory_space=pltpu.VMEM)
+in_smem = pl.BlockSpec(memory_space=pltpu.SMEM)
+
+
+def swap(value, axis, bits):
+    size = lax.axis_size(axis)
+    return lax.ppermute(value, axis, [(i, i ^ bits) for i in range(size)])
+
+
+def hit_table(routes, picks, column, row, places):
+    lanes = row.shape[1]
+    same = column == row
+    q = lax.broadcasted_iota(jnp.int32, same.shape, 0)
+    p = lax.broadcasted_iota(jnp.int32, same.shape, 1) % places
+    copies = jnp.sum(jnp.where(same & (q < places), 1.0, 0.0), axis=0, keepdims=True)
+    rank = jnp.sum(jnp.where(same & (q < p), 1.0, 0.0), axis=0, keepdims=True)
+    routes = jnp.transpose(routes.astype(f32))
+    rests = [jnp.transpose(lax.rem(picks, jnp.full_like(picks, count)).astype(f32)) for count in range(2, most_copies + 1)]
+    hits = jnp.zeros((routes.shape[0], lanes), f32)
+    for k in range(routes.shape[1]):
+        wanted = jnp.zeros(hits.shape, f32)
+        for count, rest in enumerate(rests, 2):
+            wanted = jnp.where(copies == count, rest[:, k:k + 1], wanted)
+        hits = jnp.where((routes[:, k:k + 1] == row) & (wanted == rank), 1.0, hits)
+    return hits
+
+
+def quarters_kernel(weights_ref, send_ref):
+    shards, _, columns = send_ref.shape
+    units = columns // 2
+    for q in range(shards):
+        for part in range(2):
+            at = (part * shards + q) * units
+            send_ref[q, :, part * units:(part + 1) * units] = weights_ref[0, :, at:at + units]
+
+
+def quarters(weights, first, slots, shards):
+    _, depth, columns = weights.shape
+    part = columns // shards
+    return pl.pallas_call(
+        quarters_kernel,
+        out_shape=jax.ShapeDtypeStruct((shards, depth, part * slots), bf16),
+        grid=(slots,),
+        in_specs=[pl.BlockSpec((1, depth, columns), lambda i: (first + i, 0, 0))],
+        out_specs=pl.BlockSpec((shards, depth, part), lambda i: (0, 0, i)),
+        compiler_params=pltpu.CompilerParams(vmem_limit_bytes=vmem_limit),
+        cost_estimate=pl.CostEstimate(flops=0, bytes_accessed=4 * depth * columns * slots, transcendentals=0),
+        name="quarters",
+    )(weights)
+
+
+class Loads:
+    def __init__(self, sems):
+        self.sems = sems
+        self.used = 0
+        self.waiting = {}
+
+    def start(self, name, source, target):
+        copy = pltpu.make_async_copy(source, target, self.sems.at[self.used])
+        copy.start()
+        self.used += 1
+        self.waiting.setdefault(name, []).append(copy)
+
+    def wait(self, name):
+        for copy in self.waiting.pop(name, []):
+            copy.wait()
+
+
+def project_kernel(
+    where_ref, heads_hbm, residual_hbm, gain_hbm, router_hbm, routes_hbm, picks_hbm, experts_hbm, *refs
+):
+    pieces = refs[:-11]
+    rows_ref, hidden_ref, weight, heads_ref, residual_ref, gain_ref, router_ref = refs[-11:-4]
+    routes_ref, picks_ref, experts_ref, sems = refs[-4:]
+    e = where_ref[0]
+    s = where_ref[1]
+    chips = len(pieces) // 2
+    shards, piece, _ = pieces[0].shape
+    depth = weight.shape[0] // shards
+    loads = Loads(sems)
+    for source, target in (
+        (routes_hbm, routes_ref), (picks_hbm, picks_ref), (experts_hbm, experts_ref), (router_hbm, router_ref),
+    ):
+        loads.start("routing", source, target)
+    for core in range(2):
+        for chip in range(chips):
+            for k in range(shards):
+                start = pl.multiple_of((s ^ k) * depth + (e ^ (2 * chip + core)) * piece, piece)
+                loads.start("weight", pieces[core * chips + chip].at[k], weight.at[pl.ds(start, piece), :])
+    for source, target in ((heads_hbm, heads_ref), (residual_hbm, residual_ref), (gain_hbm, gain_ref)):
+        loads.start("weight", source, target)
+    loads.wait("routing")
+    places = experts_ref.shape[1]
+    row = experts_ref[...].astype(f32)
+    row = jnp.concatenate([row, row], axis=1)
+    column = jnp.transpose(jnp.broadcast_to(row, (row.shape[1], row.shape[1])))
+    hits = hit_table(routes_ref[...], picks_ref[...], column, row, places)
+    count = router_ref.shape[0]
+    label = lax.broadcasted_iota(jnp.int32, (row.shape[1], count), 1).astype(f32)
+    chosen = jnp.where(column[:, :count] == label, 1.0, 0.0).astype(bf16)
+    router = jnp.dot(chosen, router_ref[...], preferred_element_type=f32).astype(bf16)
+    loads.wait("weight")
+    projected = jnp.dot(heads_ref[...], weight[...], preferred_element_type=f32)
+    hidden = (residual_ref[...].astype(f32) + projected).astype(bf16)
+    hidden_ref[...] = hidden
+    normed = rms_scale(hidden.astype(f32), gain_ref[...]).astype(bf16)
+    width = normed.shape[1]
+    rows_ref[:, :width] = normed
+    logits = lax.dot_general(normed, router, (((1,), (1,)), ((), ())), preferred_element_type=f32)
+    raised = jnp.where(hits > 0, jnp.exp(logits), 0.0)
+    total = jnp.sum(raised, axis=-1, keepdims=True) * 0.5
+    share = raised / total
+    high = share.astype(bf16)
+    low = (share - high.astype(f32)).astype(bf16)
+    lane = lax.broadcasted_iota(jnp.int32, share.shape, 1)
+    rows_ref[:, width:] = jnp.where(lane < places, high.astype(f32), low.astype(f32)).astype(bf16)
+
+
+def project(where, heads, residual, gain, router, routes, picks, placement, pieces):
+    rows, width = residual.shape
+    pairs = 2 * placement.shape[0]
+    places = placement.shape[0]
+    operands = (
+        heads, residual, gain.reshape(1, -1), router.T, routes.T, picks.T, placement.reshape(1, -1), *pieces,
+    )
+    count = len(operands) + len(pieces) * (pieces[0].shape[0] - 1)
+    return pl.pallas_call(
+        project_kernel,
+        out_shape=(
+            jax.ShapeDtypeStruct((rows, width + pairs), bf16),
+            jax.ShapeDtypeStruct((rows, width), bf16),
+        ),
+        in_specs=[in_smem] + [any_space] * len(operands),
+        out_specs=(in_vmem, in_vmem),
+        scratch_shapes=[
+            pltpu.VMEM((width, width), bf16),
+            pltpu.VMEM((rows, width), bf16),
+            pltpu.VMEM((rows, width), bf16),
+            pltpu.VMEM((1, width), f32),
+            pltpu.VMEM(router.shape[::-1], bf16),
+            pltpu.VMEM(routes.shape[::-1], jnp.int32),
+            pltpu.VMEM(picks.shape[::-1], jnp.int32),
+            pltpu.VMEM((1, places), jnp.int32),
+            pltpu.SemaphoreType.DMA((count,)),
+        ],
+        compiler_params=pltpu.CompilerParams(vmem_limit_bytes=vmem_limit),
+        cost_estimate=pl.CostEstimate(
+            flops=2 * rows * width * width, bytes_accessed=3 * width * width, transcendentals=rows * pairs
+        ),
+        name="project",
+    )(where, *operands)
+
+
+def activate(both, shares, first, slots):
+    units = shares.shape[1]
+    pairs = shares.shape[1]
+    place = lax.broadcasted_iota(jnp.int32, (pairs, slots * units), 0) % (pairs // 2)
+    lane = lax.broadcasted_iota(jnp.int32, (pairs, slots * units), 1) // units
+    spread = jnp.where(place == lane + first, 1.0, 0.0).astype(bf16)
+    factor = jnp.dot(shares, spread, preferred_element_type=f32)
+    parts = []
+    for slot in range(slots):
+        gate = both[:, 2 * slot * units:(2 * slot + 1) * units]
+        up = both[:, (2 * slot + 1) * units:(2 * slot + 2) * units]
+        act = gate / (1.0 + jnp.exp(-gate)) * up
+        parts.append((act * factor[:, slot * units:(slot + 1) * units]).astype(bf16))
+    return parts
+
+
+def slots_kernel(slot_sets, group_slots, block_count, has_sums, cut, where_ref, *refs):
+    refs = list(refs)
+
+    def take(count):
+        taken, refs[:] = refs[:count], refs[count:]
+        return taken
+
+    blocks = take(block_count)
+    sources = take(len(slot_sets))
+    downs = take(2)
+    earlier = take(1)[0] if has_sums else None
+    outs = take(4 if cut else 1)
+    x, total, weight, down, weight_sem, x_sems, sum_sems, out_sems = refs
+    tiles, tile_rows, _ = x.shape
+    width = weight.shape[0]
+    units = x.shape[2] - width
+
+    at = 0
+    for source in sources:
+        shards, depth, columns = source.shape
+        for q in range(shards):
+            rows = pl.ds(q * depth, depth)
+            pltpu.make_async_copy(source.at[q], weight.at[rows, pl.ds(at, columns)], weight_sem.at[0]).start()
+        at += columns
+
+    def load_tile(tile):
+        at = 0
+        for block in blocks:
+            rows = block.shape[0]
+            if at // tile_rows == tile:
+                target = x.at[tile, pl.ds(at % tile_rows, rows), :]
+                pltpu.make_async_copy(block, target, x_sems.at[tile]).start()
+            at += rows
+
+    load_tile(0)
+    at = 0
+    for flip, first, count in slot_sets:
+        source, target = downs[flip].at[pl.ds(first * units, count * units), :], down.at[pl.ds(at, count * units), :]
+        pltpu.make_async_copy(source, target, weight_sem.at[1]).start()
+        at += count * units
+    for tile in range(tiles):
+        if tile:
+            load_tile(tile)
+        if has_sums:
+            source = earlier.at[pl.ds(tile * tile_rows, tile_rows), :]
+            pltpu.make_async_copy(source, total.at[tile], sum_sems.at[tile]).start()
+    pltpu.make_async_copy(weight, weight, weight_sem.at[0]).wait()
+    pltpu.make_async_copy(down, down, weight_sem.at[1]).wait()
+
+    @pl.loop(0, tiles)
+    def _(tile):
+        pltpu.make_async_copy(x.at[tile], x.at[tile], x_sems.at[tile]).wait()
+        shares = x[tile, :, width:]
+        both = jnp.dot(x[tile, :, :width], weight[...], preferred_element_type=f32)
+        parts, at = [], 0
+        for flip, first, count in slot_sets:
+            place = (where_ref[0] ^ flip) * group_slots + first
+            parts += activate(both[:, at:at + 2 * count * units], shares, place, count)
+            at += 2 * count * units
+        added = jnp.dot(jnp.concatenate(parts, axis=1), down[...], preferred_element_type=f32)
+        if has_sums:
+            pltpu.make_async_copy(total.at[tile], total.at[tile], sum_sems.at[tile]).wait()
+            added = added + total[tile].astype(f32)
+        total[tile] = added.astype(bf16)
+        if not cut:
+            target = outs[0].at[pl.ds(tile * tile_rows, tile_rows), :]
+            pltpu.make_async_copy(total.at[tile], target, out_sems.at[tile]).start()
+
+    if cut:
+        rows, half = blocks[0].shape[0], width // 2
+        parts = block_count // 4
+        copies = []
+        for part in range(parts):
+            place = part if cut == "ordered" else part ^ (1 - where_ref[2])
+            for out, chips, column in zip(outs, ((1, 3), (2, 3), (0, 2), (0, 1)), (0, half, 0, half)):
+                for i, chip in enumerate(chips):
+                    tile, at = divmod((4 * part + chip) * rows, tile_rows)
+                    source = total.at[tile, pl.ds(at, rows), pl.ds(column, half)]
+                    target = out.at[i, place]
+                    copies.append(pltpu.make_async_copy(source, target, out_sems.at[len(copies)]))
+        for copy in copies:
+            copy.start()
+        for copy in copies:
+            copy.wait()
+    else:
+        @pl.loop(0, tiles)
+        def _(tile):
+            target = outs[0].at[pl.ds(tile * tile_rows, tile_rows), :]
+            pltpu.make_async_copy(total.at[tile], target, out_sems.at[tile]).wait()
+
+
+def slots_block(where, blocks, sources, slot_sets, downs, earlier, group_slots, cut=None):
+    rows = sum(block.shape[0] for block in blocks)
+    wide = blocks[0].shape[1]
+    shards, depth, _ = sources[0].shape
+    width = downs[0].shape[1]
+    columns = sum(source.shape[2] for source in sources)
+    tiles = rows // tile_rows
+    if cut:
+        out_shape = [jax.ShapeDtypeStruct((2, len(blocks) // 4, blocks[0].shape[0], width // 2), bf16)] * 4
+    else:
+        out_shape = [jax.ShapeDtypeStruct((rows, width), bf16)]
+    return pl.pallas_call(
+        functools.partial(slots_kernel, slot_sets, group_slots, len(blocks), bool(earlier), cut),
+        out_shape=out_shape,
+        in_specs=[in_smem] + [any_space] * (len(blocks) + len(sources) + 2 + len(earlier)),
+        out_specs=[any_space] * len(out_shape),
+        scratch_shapes=[
+            pltpu.VMEM((tiles, tile_rows, wide), bf16),
+            pltpu.VMEM((tiles, tile_rows, width), bf16),
+            pltpu.VMEM((depth * shards, columns), bf16),
+            pltpu.VMEM((columns // 2, width), bf16),
+            pltpu.SemaphoreType.DMA((2,)),
+            pltpu.SemaphoreType.DMA((tiles,)),
+            pltpu.SemaphoreType.DMA((tiles,)),
+            pltpu.SemaphoreType.DMA((max(tiles, 2 * len(blocks)),)),
+        ],
+        compiler_params=pltpu.CompilerParams(vmem_limit_bytes=vmem_limit),
+        cost_estimate=pl.CostEstimate(
+            flops=2 * rows * columns * (depth * shards + width // 2),
+            bytes_accessed=2 * (rows * (wide + 2 * width) + columns * (depth * shards + width // 2)),
+            transcendentals=rows * columns // 2,
+        ),
+        name="slots_block",
+    )(where, *blocks, *sources, *downs, *earlier)
+
+
+def after(value, *events):
+    return lax.optimization_barrier((value, *events))[0]
+
+
+def chip_gather(block):
+    return [block] + [swap(block, "expert", bits) for bits in (2, 4, 6)]
+
+
+def core_gather(chips):
+    return chips + [swap(chip, "expert", 1) for chip in chips]
+
+
+def stage(*values):
+    return lax.optimization_barrier(values)
+
+
+def add(left, right):
+    return (left.astype(f32) + right.astype(f32)).astype(bf16)
+
+
+def quarter_body(
+    head_outputs,
+    residual,
+    output_weight,
+    router,
+    norm_gain,
+    placed_gate_up,
+    placed_down,
+    routes,
+    replica_pick,
+    placement,
+    final_gain,
+):
+    rows, width = residual.shape
+    slots, depth, columns = placed_gate_up.shape
+    devices, shards = lax.axis_size("expert"), lax.axis_size("shard")
+    e, s = lax.axis_index("expert"), lax.axis_index("shard")
+    inner = (s == 1) | (s == 2)
+    where = jnp.stack([e, s, inner]).astype(jnp.int32)
+    hidden_units = columns // 2
+    units = hidden_units // shards
+
+    piece = output_weight.shape[0] // devices
+    own = lax.dynamic_slice_in_dim(output_weight, e * piece, piece, 0)
+    over_z = jnp.stack([own] + [swap(own, "shard", k) for k in range(1, shards)])
+
+    sends = [quarters(placed_gate_up, first, count, shards) for first, count in chunks]
+
+    def exchange(send):
+        return lax.all_to_all(send, "shard", split_axis=0, concat_axis=0, tiled=True)
+
+    over_z, send = stage(over_z, sends[0])
+    weights = [exchange(send)]
+    pieces = core_gather(chip_gather(over_z))
+    block, hidden = project(where, head_outputs, residual, norm_gain, router, routes, replica_pick, placement, pieces)
+
+    cross = [(1, 2), (2, 1)]
+    outward = [(1, 0), (2, 3)]
+
+    own_chips = chip_gather(block)
+    near = swap(block, "shard", 1)
+    first_in = lax.ppermute(block, "shard", cross)
+    near, first_in, send, sends[2], *own_chips = stage(near, first_in, sends[1], sends[2], *own_chips)
+
+    near_chips = chip_gather(near)
+    first_out = lax.ppermute(first_in, "shard", outward)
+    second_in = lax.ppermute(near, "shard", cross)
+    first_out, second_in, weights[0], *near_chips = stage(first_out, second_in, weights[0], *near_chips)
+
+    weights.append(exchange(after(send, weights[0])))
+    far_a = jnp.where(inner, first_in, first_out)
+    far_a_chips = chip_gather(far_a)
+    second_out = lax.ppermute(second_in, "shard", outward)
+
+    down = placed_down.reshape(slots * units, width)
+    downs = [down, swap(after(down, near), "expert", 1)]
+    others = [swap(weights[0], "expert", 1)]
+    def run(blocks, which, earlier, cut=None):
+        sources, sets = [], []
+        for chunk in range(len(chunks))[which]:
+            sources += [weights[chunk], others[chunk]]
+            sets += [(0, *chunks[chunk]), (1, *chunks[chunk])]
+        return slots_block(where, blocks, sources, tuple(sets), downs, earlier, slots, cut)
+
+    (early,) = run(near_chips + own_chips, slice(0, 1), [])
+    second_out, early, *far_a_chips = stage(second_out, early, *far_a_chips)
+
+    far_b = jnp.where(inner, second_in, second_out)
+    far_b_chips = chip_gather(far_b)
+    weights[1], *far_b_chips = stage(weights[1], *far_b_chips)
+
+    weights.append(exchange(after(sends[2], weights[1])))
+    others.append(swap(weights[1], "expert", 1))
+    (late,) = run(far_a_chips + far_b_chips, slice(0, 2), [])
+    weights[2], late = stage(weights[2], late)
+    others.append(swap(weights[2], "expert", 1))
+
+    sums = {}
+    far = run(far_a_chips + far_b_chips, slice(2, 3), [late], "labelled")
+    far_x, far_y = swap(far[0], "expert", 2), swap(far[1], "expert", 4)
+    close = run(near_chips + own_chips, slice(1, 3), [after(early, far[2])], "ordered")
+    far_x, far_y, *close = stage(far_x, far_y, *close)
+    close_x, close_y = swap(close[0], "expert", 2), swap(close[1], "expert", 4)
+    for pair, left, right, a_x, b_y in (
+        ((3, 2), far[2], far[3], far_x, far_y), ((1, 0), close[2], close[3], close_x, close_y)
+    ):
+        a_y = swap(add(left[1], a_x[1]), "expert", 4)
+        b_x = swap(add(right[1], b_y[1]), "expert", 2)
+        left = left[0].astype(f32) + a_x[0].astype(f32) + a_y.astype(f32)
+        right = right[0].astype(f32) + b_y[0].astype(f32) + b_x.astype(f32)
+        for i, k in enumerate(pair):
+            sums[k] = jnp.concatenate([left[i], right[i]], axis=1)
+    sent = [swap(sums[k].astype(bf16), "shard", k) for k in range(1, shards)]
+    total = hidden.astype(f32) + sums[0]
+    for part in sent:
+        total = total + part.astype(f32)
+    return rms_scale(total, final_gain).astype(bf16)
 
 
 def choose_slots(routes, replica_pick, placement, experts):
@@ -132,8 +556,9 @@
 
 
 def solution(mesh):
+    by_quarters = mesh.shape["expert"] == 8 and mesh.shape["shard"] == 4
     return jax.shard_map(
-        body,
+        quarter_body if by_quarters else body,
         mesh=mesh,
         in_specs=(
             P(("expert", "shard"), None),

time: 636 us -> 229 us (0.36)
  waiting for transfers between devices: 522 us -> 96.1 us
  Pallas kernels: 0 us -> 66.6 us
  starting transfers between devices: 9.97 us -> 55.4 us
  matrix products: 45 us -> 0 us
  local copies, waits for them, and re-layouts: 24 us -> 3.26 us
  other arithmetic: 21.4 us -> 6.52 us
  between operations: 13.3 us -> 0.52 us
    all_gather x3 -> x0, waiting for transfers between devices: 378 us -> none  [the longest x1 287 us: body(): lax.all_gather(placed_gate_up, 'shard', axis=1, tiled=True)]
    all_to_all x2 -> x3, waiting for transfers between devices: 143 us -> 8.88 us  [exchange(): lax.all_to_all(send, 'shard', split_axis=0, concat_axis=0, tiled=True)]
    ppermute x0 -> x42, waiting for transfers between devices: none -> 87.2 us  [the longest x38 69.9 us: swap(): return lax.ppermute(value, axis, [(i, i ^ bits) for i in range(size)])]
    pallas_call x0 -> x8, Pallas kernels: none -> 66.6 us  [the longest x4 52.9 us: slots_block(): pl.pallas_call(functools.partial(slots_kernel, slot_sets, group_slots, le...]
    dot_general x10 -> x0, matrix products: 45 us -> none  [the longest x4 36.6 us: apply_block(): jnp.einsum('bjmd,jdf->bjmf', block_part, gate_up, preferred_element_type=...]
    ppermute x0 -> x42, starting transfers between devices: none -> 43 us  [the longest x38 39.1 us: swap(): return lax.ppermute(value, axis, [(i, i ^ bits) for i in range(size)])]
    another operation x4, other arithmetic: 18.4 us -> 2.79 us
    scatter x1 -> x0, local copies, waits for them, and re-layouts: 9.22 us -> none  [body(): outbound = jnp.zeros((place_count * capacity, model_width), jnp.bfloat16)...]
  transfers between devices with their start and end apart: 5 -> 45, of which waited for: 5 -> 29; matrix products, arithmetic and copies ran while one was open for 5% -> 2% of each run, Pallas kernels for 0% -> 25%
where the time goes in v2:
time: 229 us; the launch traced here: 228 us
  waiting for transfers between devices  96.1 us (42%)
  Pallas kernels  66.6 us (29%)
  starting transfers between devices  55.4 us (24%)
  other arithmetic  6.52 us (3%)
  local copies, waits for them, and re-layouts  3.26 us (1%)
    ppermute x38, waiting for transfers between devices, swap(): return lax.ppermute(value, axis, [(i, i ^ bits) for i in range(size)])  69.9 us
    pallas_call x4, Pallas kernels, slots_block(): pl.pallas_call(functools.partial(slots_kernel, slot_sets, group_slots, le...  52.9 us
    ppermute x38, starting transfers between devices, swap(): return lax.ppermute(value, axis, [(i, i ^ bits) for i in range(size)])  39.1 us
    all_to_all x3, starting transfers between devices, exchange(): lax.all_to_all(send, 'shard', split_axis=0, concat_axis=0, tiled=True)  12.4 us
    ppermute x1, waiting for transfers between devices, quarter_body(): second_out = lax.ppermute(second_in, 'shard', outward)  11.5 us
    pallas_call x3, Pallas kernels, quarters(): pl.pallas_call(quarters_kernel, out_shape=jax.ShapeDtypeStruct((shards, d...  9.23 us
    all_to_all x3, waiting for transfers between devices, exchange(): lax.all_to_all(send, 'shard', split_axis=0, concat_axis=0, tiled=True)  8.88 us
    ppermute x1, waiting for transfers between devices, quarter_body(): first_out = lax.ppermute(first_in, 'shard', outward)  5.88 us
  transfers between devices with their start and end apart: 45, of which 29 were waited for; matrix products, arithmetic and copies ran while one was open for 2% of the time, Pallas kernels for 25%

profile of v2, /device:TPU:0, one launch (start us, length us, event | category | flops | bytes accessed | tf_op | source)
XLA Modules:
  0.0 228.4 jit_solution(11276403380908526258)
XLA Ops:
  1.0 4.0 %collective-permute-start.1 = (bf16[32,1024]{1,0:T(8,128)(2,1)S(1)}, bf16[32,1024]{1,0:T(8,128)(2,1)S(1)}, u32[]{:S(2)}, u32[]{:S(2)}) collective-permute-start(bf16[32,1024]{1,0:T(8,128)(2,1)S(1)} %constant_dynamic-slice_fusion), channel_id=1, source_target_pairs={{0,2},{1,3},{2,0},{3,1},{4,6},{5,7},{6,4},{7,5},{8,10},{9,11},{10,... | collective-permute-start | bytes 196616 | tf_op jit(solution)/shard_map/ppermute | solution.py:35
  6.7 3.5 %quarters.3 = bf16[4,256,768]{2,1,0:T(8,128)(2,1)} custom-call(bf16[8,256,1024]{2,1,0:T(8,128)(2,1)} %weights_ref.5), custom_call_target="tpu_custom_call" | custom-call | bytes 3145728 | tf_op jit(solution)/shard_map/quarters/pallas_call | solution.py:68
  10.2 2.5 %collective-permute-done.2 = bf16[32,1024]{1,0:T(8,128)(2,1)S(1)} collective-permute-done((bf16[32,1024]{1,0:T(8,128)(2,1)S(1)}, bf16[32,1024]{1,0:T(8,128)(2,1)S(1)}, u32[]{:S(2)}, u32[]{:S(2)}) %collective-permute-start.2) | collective-permute-done | bytes 65568 | tf_op jit(solution)/shard_map/ppermute | solution.py:35
  12.8 4.3 %all-to-all-start = ((bf16[4,256,768]{2,1,0:T(8,128)(2,1)}), bf16[4,256,768]{2,1,0:T(8,128)(2,1)}, u32[]{:S(2)}, u32[]{:S(2)}) async-start(bf16[4,256,768]{2,1,0:T(8,128)(2,1)} %quarters.3), calls=%async_computation | async-start | bytes 3145728 | tf_op jit(solution)/shard_map/all_to_all | solution.py:374
  17.1 2.5 %collective-permute-start.5 = (bf16[4,32,1024]{2,1,0:T(8,128)(2,1)S(1)}, bf16[4,32,1024]{2,1,0:T(8,128)(2,1)S(1)}, u32[]{:S(2)}, u32[]{:S(2)}) collective-permute-start(bf16[4,32,1024]{2,1,0:T(8,128)(2,1)S(1)} %pad_maximum_fusion.refs_0_), channel_id=1, source_target_pairs={{0,24},{4,28},{8,16},{12,20},{16,8},{20,12},{24,0},{28,4},{1,25},{... | collective-permute-start | bytes 786440 | tf_op jit(solution)/shard_map/ppermute | solution.py:35
  20.7 6.7 %collective-permute-done.5.refs_3_ = bf16[4,32,1024]{2,1,0:T(8,128)(2,1)S(1)} collective-permute-done((bf16[4,32,1024]{2,1,0:T(8,128)(2,1)S(1)}, bf16[4,32,1024]{2,1,0:T(8,128)(2,1)S(1)}, u32[]{:S(2)}, u32[]{:S(2)}) %collective-permute-start.5) | collective-permute-done | bytes 262176 | tf_op jit(solution)/shard_map/ppermute | solution.py:35
  27.4 2.8 %collective-permute-done.4.refs_2_ = bf16[4,32,1024]{2,1,0:T(8,128)(2,1)S(1)} collective-permute-done((bf16[4,32,1024]{2,1,0:T(8,128)(2,1)S(1)}, bf16[4,32,1024]{2,1,0:T(8,128)(2,1)S(1)}, u32[]{:S(2)}, u32[]{:S(2)}) %collective-permute-start.4) | collective-permute-done | bytes 262176 | tf_op jit(solution)/shard_map/ppermute | solution.py:35
  32.8 4.5 %project.1 = (bf16[128,1152]{1,0:T(8,128)(2,1)}, bf16[128,1024]{1,0:T(8,128)(2,1)}) custom-call(s32[3]{0:T(128)} %pad_add_fusion.where_ref, bf16[128,1024]{1,0:T(8,128)(2,1)} %heads_hbm.1, bf16[128,1024]{1,0:T(8,128)(2,1)} %residual_hbm.1, f32[1,1024]{1,0:T(1,128)} %bitcast.54, bf16[32,1024]{1,0:T(8,128)(2,1)} %bitcast.50, s32[8,128]{1,0:T(8,128)} %bitcast.55, ...), custom_call_target="tpu_custom_call" | custom-call | flops 268435456 | bytes 3145728 | tf_op jit(solution)/shard_map/project/pallas_call | solution.py:155
  41.5 4.6 %collective-permute-start.10 = (bf16[128,1152]{1,0:T(8,128)(2,1)}, bf16[128,1152]{1,0:T(8,128)(2,1)S(1)}, u32[]{:S(2)}, u32[]{:S(2)}) collective-permute-start(bf16[128,1152]{1,0:T(8,128)(2,1)} %get-tuple-element.66.refs_4_), channel_id=1, source_target_pairs={{0,1},{1,0},{2,3},{3,2},{4,5},{5,4},{6,7},{7,6},{8,9},{9,8},{10,11... | collective-permute-start | bytes 884744 | tf_op jit(solution)/shard_map/ppermute | solution.py:35
  46.1 2.2 quarters.5
  48.3 3.5 %quarters.4 = bf16[4,256,768]{2,1,0:T(8,128)(2,1)} custom-call(bf16[8,256,1024]{2,1,0:T(8,128)(2,1)} %weights_ref.5), custom_call_target="tpu_custom_call" | custom-call | bytes 3145728 | tf_op jit(solution)/shard_map/quarters/pallas_call | solution.py:68
  51.9 2.0 collective-permute-done.13.refs_6_
  54.0 5.2 %collective-permute-done.10.refs_0_ = bf16[128,1152]{1,0:T(8,128)(2,1)S(1)} collective-permute-done((bf16[128,1152]{1,0:T(8,128)(2,1)}, bf16[128,1152]{1,0:T(8,128)(2,1)S(1)}, u32[]{:S(2)}, u32[]{:S(2)}) %collective-permute-start.10) | collective-permute-done | bytes 294944 | tf_op jit(solution)/shard_map/ppermute | solution.py:35
  60.5 2.5 %collective-permute-start.19 = (bf16[128,1152]{1,0:T(8,128)(2,1)S(1)}, bf16[128,1152]{1,0:T(8,128)(2,1)S(1)}, u32[]{:S(2)}, u32[]{:S(2)}) collective-permute-start(bf16[128,1152]{1,0:T(8,128)(2,1)S(1)} %collective-permute-done.10.refs_0_), channel_id=1, source_target_pairs={{0,24},{4,28},{8,16},{12,20},{16,8},{20,12},{24,0},{28,4},{1,25},{... | collective-permute-start | bytes 884744 | tf_op jit(solution)/shard_map/ppermute | solution.py:35
  64.1 5.9 %collective-permute-done.15 = bf16[128,1152]{1,0:T(8,128)(2,1)S(1)} collective-permute-done((bf16[128,1152]{1,0:T(8,128)(2,1)S(1)}, bf16[128,1152]{1,0:T(8,128)(2,1)S(1)}, u32[]{:S(2)}, u32[]{:S(2)}) %collective-permute-start.15) | collective-permute-done | bytes 294944 | tf_op jit(solution)/shard_map/ppermute | solution.py:390
  71.4 5.8 %collective-permute-done.18.refs_2_ = bf16[128,1152]{1,0:T(8,128)(2,1)S(1)} collective-permute-done((bf16[128,1152]{1,0:T(8,128)(2,1)S(1)}, bf16[128,1152]{1,0:T(8,128)(2,1)S(1)}, u32[]{:S(2)}, u32[]{:S(2)}) %collective-permute-start.18) | collective-permute-done | bytes 294944 | tf_op jit(solution)/shard_map/ppermute | solution.py:35
  78.0 4.4 %all-to-all-start.1 = ((bf16[4,256,768]{2,1,0:T(8,128)(2,1)}), bf16[4,256,768]{2,1,0:T(8,128)(2,1)}, u32[]{:S(2)}, u32[]{:S(2)}) async-start(bf16[4,256,768]{2,1,0:T(8,128)(2,1)} %quarters.4), calls=%async_computation.1 | async-start | bytes 3145728 | tf_op jit(solution)/shard_map/all_to_all | solution.py:374
  87.3 10.4 %slots_block.4.refs_14_ = bf16[1024,1024]{1,0:T(8,128)(2,1)} custom-call(s32[3]{0:T(128)} %pad_add_fusion.where_ref, bf16[128,1152]{1,0:T(8,128)(2,1)} %copy-done.23, bf16[128,1152]{1,0:T(8,128)(2,1)} %copy-done.26, bf16[128,1152]{1,0:T(8,128)(2,1)} %copy-done.25, bf16[128,1152]{1,0:T(8,128)(2,1)} %copy-done.24, ...), custom_call_target="tpu_custom_call" | custom-call | flops 4831838208 | bytes 11272192 | tf_op jit(solution)/shard_map/slots_block/pallas_call | solution.py:300
  98.9 11.5 %collective-permute-done.20 = bf16[128,1152]{1,0:T(8,128)(2,1)S(1)} collective-permute-done((bf16[128,1152]{1,0:T(8,128)(2,1)S(1)}, bf16[128,1152]{1,0:T(8,128)(2,1)S(1)}, u32[]{:S(2)}, u32[]{:S(2)}) %collective-permute-start.20) | collective-permute-done | bytes 294944 | tf_op jit(solution)/shard_map/ppermute | solution.py:397
  114.0 7.4 %collective-permute-done.28.refs_7_ = bf16[128,1152]{1,0:T(8,128)(2,1)S(1)} collective-permute-done((bf16[128,1152]{1,0:T(8,128)(2,1)S(1)}, bf16[128,1152]{1,0:T(8,128)(2,1)S(1)}, u32[]{:S(2)}, u32[]{:S(2)}) %collective-permute-start.28) | collective-permute-done | bytes 294944 | tf_op jit(solution)/shard_map/ppermute | solution.py:35
  121.3 4.9 %collective-permute-done.27.refs_6_ = bf16[128,1152]{1,0:T(8,128)(2,1)S(1)} collective-permute-done((bf16[128,1152]{1,0:T(8,128)(2,1)S(1)}, bf16[128,1152]{1,0:T(8,128)(2,1)S(1)}, u32[]{:S(2)}, u32[]{:S(2)}) %collective-permute-start.27) | collective-permute-done | bytes 294944 | tf_op jit(solution)/shard_map/ppermute | solution.py:35
  127.0 3.7 %all-to-all-start.2 = ((bf16[4,256,512]{2,1,0:T(8,128)(2,1)}), bf16[4,256,512]{2,1,0:T(8,128)(2,1)S(1)}, u32[]{:S(2)}, u32[]{:S(2)}) async-start(bf16[4,256,512]{2,1,0:T(8,128)(2,1)} %quarters.5), calls=%async_computation.2 | async-start | bytes 2097152 | tf_op jit(solution)/shard_map/all_to_all | solution.py:374
  130.8 17.1 %slots_block.5.refs_12_ = bf16[1024,1024]{1,0:T(8,128)(2,1)} custom-call(s32[3]{0:T(128)} %pad_add_fusion.where_ref, bf16[128,1152]{1,0:T(8,128)(2,1)} %copy-done.8, bf16[128,1152]{1,0:T(8,128)(2,1)} %collective-permute-done.23.refs_1_, bf16[128,1152]{1,0:T(8,128)(2,1)} %copy-done.28, bf16[128,1152]{1,0:T(8,128)(2,1)} %copy-done.27, ...), custom_call_target="tpu_custom_call" | custom-call | flops 9663676416 | bytes 15990784 | tf_op jit(solution)/shard_map/slots_block/pallas_call | solution.py:300
  147.8 8.9 %all-to-all-done.2.refs_8_.refs_10_ = bf16[4,256,512]{2,1,0:T(8,128)(2,1)S(1)} async-done(((bf16[4,256,512]{2,1,0:T(8,128)(2,1)}), bf16[4,256,512]{2,1,0:T(8,128)(2,1)S(1)}, u32[]{:S(2)}, u32[]{:S(2)}) %all-to-all-start.2) | async-done | bytes 1048608 | tf_op jit(solution)/shard_map/all_to_all | solution.py:374
  156.7 2.8 %collective-permute-done.30.refs_9_.refs_11_ = bf16[4,256,512]{2,1,0:T(8,128)(2,1)} collective-permute-done((bf16[4,256,512]{2,1,0:T(8,128)(2,1)S(1)}, bf16[4,256,512]{2,1,0:T(8,128)(2,1)}, u32[]{:S(2)}, u32[]{:S(2)}) %collective-permute-start.30) | collective-permute-done | bytes 1048608 | tf_op jit(solution)/shard_map/ppermute | solution.py:35
  159.5 9.3 %slots_block.6 = (bf16[2,2,128,512]{3,2,1,0:T(8,128)(2,1)}, bf16[2,2,128,512]{3,2,1,0:T(8,128)(2,1)}, bf16[2,2,128,512]{3,2,1,0:T(8,128)(2,1)}, bf16[2,2,128,512]{3,2,1,0:T(8,128)(2,1)}) custom-call(s32[3]{0:T(128)} %pad_add_fusion.where_ref, bf16[128,1152]{1,0:T(8,128)(2,1)} %copy-done.8, bf16[128,1152]{1,0:T(8,128)(2,1)} %collective-permute-done.23.refs_1_, ...), custom_call_target="tpu_custom_call" | custom-call | flops 3221225472 | bytes 9699328 | tf_op jit(solution)/shard_map/slots_block/pallas_call | solution.py:300
  171.1 16.1 %slots_block.7 = (bf16[2,2,128,512]{3,2,1,0:T(8,128)(2,1)}, bf16[2,2,128,512]{3,2,1,0:T(8,128)(2,1)}, bf16[2,2,128,512]{3,2,1,0:T(8,128)(2,1)}, bf16[2,2,128,512]{3,2,1,0:T(8,128)(2,1)}) custom-call(s32[3]{0:T(128)} %pad_add_fusion.where_ref, bf16[128,1152]{1,0:T(8,128)(2,1)} %copy-done.23, bf16[128,1152]{1,0:T(8,128)(2,1)} %copy-done.26, ...), custom_call_target="tpu_custom_call" | custom-call | flops 8053063680 | bytes 14417920 | tf_op jit(solution)/shard_map/slots_block/pallas_call | solution.py:300
  193.6 4.1 %collective-permute-done.39 = bf16[2,128,512]{2,1,0:T(8,128)(2,1)S(1)} collective-permute-done((bf16[2,128,512]{2,1,0:T(8,128)(2,1)S(1)}, bf16[2,128,512]{2,1,0:T(8,128)(2,1)S(1)}, u32[]{:S(2)}, u32[]{:S(2)}) %collective-permute-start.39) | collective-permute-done | bytes 262176 | tf_op jit(solution)/shard_map/ppermute | solution.py:35
  202.8 4.7 %collective-permute-done.33 = bf16[2,2,128,512]{3,2,1,0:T(8,128)(2,1)S(1)} collective-permute-done((bf16[2,2,128,512]{3,2,1,0:T(8,128)(2,1)S(1)}, bf16[2,2,128,512]{3,2,1,0:T(8,128)(2,1)S(1)}, u32[]{:S(2)}, u32[]{:S(2)}) %collective-permute-start.33) | collective-permute-done | bytes 524320 | tf_op jit(solution)/shard_map/ppermute | solution.py:35
  210.6 4.7 %collective-permute-done.34 = bf16[2,128,512]{2,1,0:T(8,128)(2,1)S(1)} collective-permute-done((bf16[2,128,512]{2,1,0:T(8,128)(2,1)S(1)}, bf16[2,128,512]{2,1,0:T(8,128)(2,1)S(1)}, u32[]{:S(2)}, u32[]{:S(2)}) %collective-permute-start.34) | collective-permute-done | bytes 262176 | tf_op jit(solution)/shard_map/ppermute | solution.py:35
  217.8 4.3 %collective-permute-done.40 = bf16[128,1024]{1,0:T(8,128)(2,1)S(1)} collective-permute-done((bf16[128,1024]{1,0:T(8,128)(2,1)S(1)}, bf16[128,1024]{1,0:T(8,128)(2,1)S(1)}, u32[]{:S(2)}, u32[]{:S(2)}) %collective-permute-start.40) | collective-permute-done | bytes 262176 | tf_op jit(solution)/shard_map/ppermute | solution.py:35
  222.1 5.2 %collective-permute-done.37 = bf16[128,1024]{1,0:T(8,128)(2,1)S(1)} collective-permute-done((bf16[128,1024]{1,0:T(8,128)(2,1)S(1)}, bf16[128,1024]{1,0:T(8,128)(2,1)S(1)}, u32[]{:S(2)}, u32[]{:S(2)}) %collective-permute-start.37) | collective-permute-done | bytes 262176 | tf_op jit(solution)/shard_map/ppermute | solution.py:35
  (156 shorter events, 46.0 us)
Async XLA Ops:
  12.8 64.5 %all-to-all-start = ((bf16[4,256,768]{2,1,0:T(8,128)(2,1)}), bf16[4,256,768]{2,1,0:T(8,128)(2,1)}, u32[]{:S(2)}, u32[]{:S(2)}) async-start(bf16[4,256,768]{2,1,0:T(8,128)(2,1)} %quarters.3), calls=%async_computation | async-start | bytes 3145728 | tf_op jit(solution)/shard_map/all_to_all | solution.py:374
  17.1 10.2 %collective-permute-start.5 = (bf16[4,32,1024]{2,1,0:T(8,128)(2,1)S(1)}, bf16[4,32,1024]{2,1,0:T(8,128)(2,1)S(1)}, u32[]{:S(2)}, u32[]{:S(2)}) collective-permute-start(bf16[4,32,1024]{2,1,0:T(8,128)(2,1)S(1)} %pad_maximum_fusion.refs_0_), channel_id=1, source_target_pairs={{0,24},{4,28},{8,16},{12,20},{16,8},{20,12},{24,0},{28,4},{1,25},{... | collective-permute-start | bytes 786440 | tf_op jit(solution)/shard_map/ppermute | solution.py:35
  19.6 10.5 %collective-permute-start.4 = (bf16[4,32,1024]{2,1,0:T(8,128)(2,1)S(1)}, bf16[4,32,1024]{2,1,0:T(8,128)(2,1)S(1)}, u32[]{:S(2)}, u32[]{:S(2)}) collective-permute-start(bf16[4,32,1024]{2,1,0:T(8,128)(2,1)S(1)} %pad_maximum_fusion.refs_0_), channel_id=1, source_target_pairs={{0,16},{4,20},{8,24},{12,28},{16,0},{20,4},{24,8},{28,12},{1,17},{... | collective-permute-start | bytes 786440 | tf_op jit(solution)/shard_map/ppermute | solution.py:35
  20.2 10.1 %collective-permute-start.3 = (bf16[4,32,1024]{2,1,0:T(8,128)(2,1)S(1)}, bf16[4,32,1024]{2,1,0:T(8,128)(2,1)S(1)}, u32[]{:S(2)}, u32[]{:S(2)}) collective-permute-start(bf16[4,32,1024]{2,1,0:T(8,128)(2,1)S(1)} %pad_maximum_fusion.refs_0_), channel_id=1, source_target_pairs={{0,8},{4,12},{8,0},{12,4},{16,24},{20,28},{24,16},{28,20},{1,9},{5... | collective-permute-start | bytes 786440 | tf_op jit(solution)/shard_map/ppermute | solution.py:35
  20.7 10.6 %collective-permute-start.6 = (bf16[4,32,1024]{2,1,0:T(8,128)(2,1)S(1)}, bf16[4,32,1024]{2,1,0:T(8,128)(2,1)S(1)}, u32[]{:S(2)}, u32[]{:S(2)}) collective-permute-start(bf16[4,32,1024]{2,1,0:T(8,128)(2,1)S(1)} %pad_maximum_fusion.refs_0_), channel_id=1, source_target_pairs={{0,4},{4,0},{8,12},{12,8},{16,20},{20,16},{24,28},{28,24},{1,5},{5... | collective-permute-start | bytes 786440 | tf_op jit(solution)/shard_map/ppermute | solution.py:35
  37.3 14.6 %collective-permute-start.14 = (bf16[128,1152]{1,0:T(8,128)(2,1)}, bf16[128,1152]{1,0:T(8,128)(2,1)S(1)}, u32[]{:S(2)}, u32[]{:S(2)}) collective-permute-start(bf16[128,1152]{1,0:T(8,128)(2,1)} %get-tuple-element.66.refs_4_), channel_id=1, source_target_pairs={{0,24},{4,28},{8,16},{12,20},{16,8},{20,12},{24,0},{28,4},{1,25},{... | collective-permute-start | bytes 884744 | tf_op jit(solution)/shard_map/ppermute | solution.py:35
  39.1 14.7 %collective-permute-start.13 = (bf16[128,1152]{1,0:T(8,128)(2,1)}, bf16[128,1152]{1,0:T(8,128)(2,1)S(1)}, u32[]{:S(2)}, u32[]{:S(2)}) collective-permute-start(bf16[128,1152]{1,0:T(8,128)(2,1)} %get-tuple-element.66.refs_4_), channel_id=1, source_target_pairs={{0,16},{4,20},{8,24},{12,28},{16,0},{20,4},{24,8},{28,12},{1,17},{... | collective-permute-start | bytes 884744 | tf_op jit(solution)/shard_map/ppermute | solution.py:35
  40.3 13.6 %collective-permute-start.12 = (bf16[128,1152]{1,0:T(8,128)(2,1)}, bf16[128,1152]{1,0:T(8,128)(2,1)S(1)}, u32[]{:S(2)}, u32[]{:S(2)}) collective-permute-start(bf16[128,1152]{1,0:T(8,128)(2,1)} %get-tuple-element.66.refs_4_), channel_id=1, source_target_pairs={{0,8},{4,12},{8,0},{12,4},{16,24},{20,28},{24,16},{28,20},{1,9},{5... | collective-permute-start | bytes 884744 | tf_op jit(solution)/shard_map/ppermute | solution.py:35
  40.9 13.1 %collective-permute-start.11 = (bf16[128,1152]{1,0:T(8,128)(2,1)}, bf16[128,1152]{1,0:T(8,128)(2,1)S(1)}, u32[]{:S(2)}, u32[]{:S(2)}) collective-permute-start(bf16[128,1152]{1,0:T(8,128)(2,1)} %get-tuple-element.66.refs_4_), channel_id=1, source_target_pairs={{1,2},{2,1},{5,6},{6,5},{9,10},{10,9},{13,14},{14,13},{17,18},{18,... | collective-permute-start | bytes 884744 | tf_op jit(solution)/shard_map/ppermute | solution.py:386
  41.5 17.6 %collective-permute-start.10 = (bf16[128,1152]{1,0:T(8,128)(2,1)}, bf16[128,1152]{1,0:T(8,128)(2,1)S(1)}, u32[]{:S(2)}, u32[]{:S(2)}) collective-permute-start(bf16[128,1152]{1,0:T(8,128)(2,1)} %get-tuple-element.66.refs_4_), channel_id=1, source_target_pairs={{0,1},{1,0},{2,3},{3,2},{4,5},{5,4},{6,7},{7,6},{8,9},{9,8},{10,11... | collective-permute-start | bytes 884744 | tf_op jit(solution)/shard_map/ppermute | solution.py:35
  59.2 10.8 %collective-permute-start.15 = (bf16[128,1152]{1,0:T(8,128)(2,1)S(1)}, bf16[128,1152]{1,0:T(8,128)(2,1)S(1)}, u32[]{:S(2)}, u32[]{:S(2)}) collective-permute-start(bf16[128,1152]{1,0:T(8,128)(2,1)S(1)} %collective-permute-done.11), channel_id=1, source_target_pairs={{1,0},{2,3},{5,4},{6,7},{9,8},{10,11},{13,12},{14,15},{17,16},{18,... | collective-permute-start | bytes 884744 | tf_op jit(solution)/shard_map/ppermute | solution.py:390
  60.5 25.5 %collective-permute-start.22 = (bf16[1024,1024]{1,0:T(8,128)(2,1)}, bf16[1024,1024]{1,0:T(8,128)(2,1)}, u32[]{:S(2)}, u32[]{:S(2)}) collective-permute-start(bf16[1024,1024]{1,0:T(8,128)(2,1)} %bitcast.58), channel_id=1, source_target_pairs={{0,4},{4,0},{8,12},{12,8},{16,20},{20,16},{24,28},{28,24},{1,5},{5... | collective-permute-start | bytes 6291464 | tf_op jit(solution)/shard_map/ppermute | solution.py:35
  60.5 10.8 %collective-permute-start.19 = (bf16[128,1152]{1,0:T(8,128)(2,1)S(1)}, bf16[128,1152]{1,0:T(8,128)(2,1)S(1)}, u32[]{:S(2)}, u32[]{:S(2)}) collective-permute-start(bf16[128,1152]{1,0:T(8,128)(2,1)S(1)} %collective-permute-done.10.refs_0_), channel_id=1, source_target_pairs={{0,24},{4,28},{8,16},{12,20},{16,8},{20,12},{24,0},{28,4},{1,25},{... | collective-permute-start | bytes 884744 | tf_op jit(solution)/shard_map/ppermute | solution.py:35
  63.1 14.1 %collective-permute-start.18 = (bf16[128,1152]{1,0:T(8,128)(2,1)S(1)}, bf16[128,1152]{1,0:T(8,128)(2,1)S(1)}, u32[]{:S(2)}, u32[]{:S(2)}) collective-permute-start(bf16[128,1152]{1,0:T(8,128)(2,1)S(1)} %collective-permute-done.10.refs_0_), channel_id=1, source_target_pairs={{0,16},{4,20},{8,24},{12,28},{16,0},{20,4},{24,8},{28,12},{1,17},{... | collective-permute-start | bytes 884744 | tf_op jit(solution)/shard_map/ppermute | solution.py:35
  63.6 13.7 %collective-permute-start.17 = (bf16[128,1152]{1,0:T(8,128)(2,1)S(1)}, bf16[128,1152]{1,0:T(8,128)(2,1)S(1)}, u32[]{:S(2)}, u32[]{:S(2)}) collective-permute-start(bf16[128,1152]{1,0:T(8,128)(2,1)S(1)} %collective-permute-done.10.refs_0_), channel_id=1, source_target_pairs={{0,8},{4,12},{8,0},{12,4},{16,24},{20,28},{24,16},{28,20},{1,9},{5... | collective-permute-start | bytes 884744 | tf_op jit(solution)/shard_map/ppermute | solution.py:35
  77.3 10.0 %collective-permute-start.21 = (bf16[4,256,768]{2,1,0:T(8,128)(2,1)}, bf16[4,256,768]{2,1,0:T(8,128)(2,1)}, u32[]{:S(2)}, u32[]{:S(2)}) collective-permute-start(bf16[4,256,768]{2,1,0:T(8,128)(2,1)} %all-to-all-done.refs_8_), channel_id=1, source_target_pairs={{0,4},{4,0},{8,12},{12,8},{16,20},{20,16},{24,28},{28,24},{1,5},{5... | collective-permute-start | bytes 4718600 | tf_op jit(solution)/shard_map/ppermute | solution.py:35
  78.0 48.3 %all-to-all-start.1 = ((bf16[4,256,768]{2,1,0:T(8,128)(2,1)}), bf16[4,256,768]{2,1,0:T(8,128)(2,1)}, u32[]{:S(2)}, u32[]{:S(2)}) async-start(bf16[4,256,768]{2,1,0:T(8,128)(2,1)} %quarters.4), calls=%async_computation.1 | async-start | bytes 3145728 | tf_op jit(solution)/shard_map/all_to_all | solution.py:374
  82.4 15.3 %collective-permute-start.25 = (bf16[128,1152]{1,0:T(8,128)(2,1)S(1)}, bf16[128,1152]{1,0:T(8,128)(2,1)S(1)}, u32[]{:S(2)}, u32[]{:S(2)}) collective-permute-start(bf16[128,1152]{1,0:T(8,128)(2,1)S(1)} %broadcast_select_fusion.1.refs_0_), channel_id=1, source_target_pairs={{0,24},{4,28},{8,16},{12,20},{16,8},{20,12},{24,0},{28,4},{1,25},{... | collective-permute-start | bytes 884744 | tf_op jit(solution)/shard_map/ppermute | solution.py:35
  84.2 14.4 %collective-permute-start.24 = (bf16[128,1152]{1,0:T(8,128)(2,1)S(1)}, bf16[128,1152]{1,0:T(8,128)(2,1)S(1)}, u32[]{:S(2)}, u32[]{:S(2)}) collective-permute-start(bf16[128,1152]{1,0:T(8,128)(2,1)S(1)} %broadcast_select_fusion.1.refs_0_), channel_id=1, source_target_pairs={{0,16},{4,20},{8,24},{12,28},{16,0},{20,4},{24,8},{28,12},{1,17},{... | collective-permute-start | bytes 884744 | tf_op jit(solution)/shard_map/ppermute | solution.py:35
  85.5 13.4 %collective-permute-start.23 = (bf16[128,1152]{1,0:T(8,128)(2,1)S(1)}, bf16[128,1152]{1,0:T(8,128)(2,1)}, u32[]{:S(2)}, u32[]{:S(2)}) collective-permute-start(bf16[128,1152]{1,0:T(8,128)(2,1)S(1)} %broadcast_select_fusion.1.refs_0_), channel_id=1, source_target_pairs={{0,8},{4,12},{8,0},{12,4},{16,24},{20,28},{24,16},{28,20},{1,9},{5... | collective-permute-start | bytes 884744 | tf_op jit(solution)/shard_map/ppermute | solution.py:35
  86.0 24.4 %collective-permute-start.20 = (bf16[128,1152]{1,0:T(8,128)(2,1)S(1)}, bf16[128,1152]{1,0:T(8,128)(2,1)S(1)}, u32[]{:S(2)}, u32[]{:S(2)}) collective-permute-start(bf16[128,1152]{1,0:T(8,128)(2,1)S(1)} %collective-permute-done.16), channel_id=1, source_target_pairs={{1,0},{2,3},{5,4},{6,7},{9,8},{10,11},{13,12},{14,15},{17,16},{18,... | collective-permute-start | bytes 884744 | tf_op jit(solution)/shard_map/ppermute | solution.py:397
  110.4 10.9 %collective-permute-start.28 = (bf16[128,1152]{1,0:T(8,128)(2,1)S(1)}, bf16[128,1152]{1,0:T(8,128)(2,1)S(1)}, u32[]{:S(2)}, u32[]{:S(2)}) collective-permute-start(bf16[128,1152]{1,0:T(8,128)(2,1)S(1)} %broadcast_select_fusion.refs_4_), channel_id=1, source_target_pairs={{0,24},{4,28},{8,16},{12,20},{16,8},{20,12},{24,0},{28,4},{1,25},{... | collective-permute-start | bytes 884744 | tf_op jit(solution)/shard_map/ppermute | solution.py:35
  112.2 14.0 %collective-permute-start.27 = (bf16[128,1152]{1,0:T(8,128)(2,1)S(1)}, bf16[128,1152]{1,0:T(8,128)(2,1)S(1)}, u32[]{:S(2)}, u32[]{:S(2)}) collective-permute-start(bf16[128,1152]{1,0:T(8,128)(2,1)S(1)} %broadcast_select_fusion.refs_4_), channel_id=1, source_target_pairs={{0,16},{4,20},{8,24},{12,28},{16,0},{20,4},{24,8},{28,12},{1,17},{... | collective-permute-start | bytes 884744 | tf_op jit(solution)/shard_map/ppermute | solution.py:35
  113.4 12.9 %collective-permute-start.26 = (bf16[128,1152]{1,0:T(8,128)(2,1)S(1)}, bf16[128,1152]{1,0:T(8,128)(2,1)S(1)}, u32[]{:S(2)}, u32[]{:S(2)}) collective-permute-start(bf16[128,1152]{1,0:T(8,128)(2,1)S(1)} %broadcast_select_fusion.refs_4_), channel_id=1, source_target_pairs={{0,8},{4,12},{8,0},{12,4},{16,24},{20,28},{24,16},{28,20},{1,9},{5... | collective-permute-start | bytes 884744 | tf_op jit(solution)/shard_map/ppermute | solution.py:35
  127.0 29.7 %all-to-all-start.2 = ((bf16[4,256,512]{2,1,0:T(8,128)(2,1)}), bf16[4,256,512]{2,1,0:T(8,128)(2,1)S(1)}, u32[]{:S(2)}, u32[]{:S(2)}) async-start(bf16[4,256,512]{2,1,0:T(8,128)(2,1)} %quarters.5), calls=%async_computation.2 | async-start | bytes 2097152 | tf_op jit(solution)/shard_map/all_to_all | solution.py:374
  168.8 18.5 %collective-permute-start.31 = (bf16[2,2,128,512]{3,2,1,0:T(8,128)(2,1)}, bf16[2,2,128,512]{3,2,1,0:T(8,128)(2,1)}, u32[]{:S(2)}, u32[]{:S(2)}) collective-permute-start(bf16[2,2,128,512]{3,2,1,0:T(8,128)(2,1)} %get-tuple-element.89), channel_id=1, source_target_pairs={{0,8},{4,12},{8,0},{12,4},{16,24},{20,28},{24,16},{28,20},{1,9},{5... | collective-permute-start | bytes 1572872 | tf_op jit(solution)/shard_map/ppermute | solution.py:35
  170.4 16.9 %collective-permute-start.32 = (bf16[2,2,128,512]{3,2,1,0:T(8,128)(2,1)}, bf16[2,2,128,512]{3,2,1,0:T(8,128)(2,1)}, u32[]{:S(2)}, u32[]{:S(2)}) collective-permute-start(bf16[2,2,128,512]{3,2,1,0:T(8,128)(2,1)} %get-tuple-element.90), channel_id=1, source_target_pairs={{0,16},{4,20},{8,24},{12,28},{16,0},{20,4},{24,8},{28,12},{1,17},{... | collective-permute-start | bytes 1572872 | tf_op jit(solution)/shard_map/ppermute | solution.py:35
  191.4 16.1 %collective-permute-start.33 = (bf16[2,2,128,512]{3,2,1,0:T(8,128)(2,1)S(1)}, bf16[2,2,128,512]{3,2,1,0:T(8,128)(2,1)S(1)}, u32[]{:S(2)}, u32[]{:S(2)}) collective-permute-start(bf16[2,2,128,512]{3,2,1,0:T(8,128)(2,1)S(1)} %copy-done.19), channel_id=1, source_target_pairs={{0,8},{4,12},{8,0},{12,4},{16,24},{20,28},{24,16},{28,20},{1,9},{5... | collective-permute-start | bytes 1572872 | tf_op jit(solution)/shard_map/ppermute | solution.py:35
  192.9 17.4 %collective-permute-start.35 = (bf16[2,2,128,512]{3,2,1,0:T(8,128)(2,1)S(1)}, bf16[2,2,128,512]{3,2,1,0:T(8,128)(2,1)S(1)}, u32[]{:S(2)}, u32[]{:S(2)}) collective-permute-start(bf16[2,2,128,512]{3,2,1,0:T(8,128)(2,1)S(1)} %copy-done.18), channel_id=1, source_target_pairs={{0,16},{4,20},{8,24},{12,28},{16,0},{20,4},{24,8},{28,12},{1,17},{... | collective-permute-start | bytes 1572872 | tf_op jit(solution)/shard_map/ppermute | solution.py:35
  201.2 16.6 %collective-permute-start.41 = (bf16[128,1024]{1,0:T(8,128)(2,1)S(1)}, bf16[128,1024]{1,0:T(8,128)(2,1)S(1)}, u32[]{:S(2)}, u32[]{:S(2)}) collective-permute-start(bf16[128,1024]{1,0:T(8,128)(2,1)S(1)} %pad_maximum_fusion.3), channel_id=1, source_target_pairs={{0,3},{1,2},{2,1},{3,0},{4,7},{5,6},{6,5},{7,4},{8,11},{9,10},{10,... | collective-permute-start | bytes 786440 | tf_op jit(solution)/shard_map/ppermute | solution.py:35
  208.9 13.2 %collective-permute-start.40 = (bf16[128,1024]{1,0:T(8,128)(2,1)S(1)}, bf16[128,1024]{1,0:T(8,128)(2,1)S(1)}, u32[]{:S(2)}, u32[]{:S(2)}) collective-permute-start(bf16[128,1024]{1,0:T(8,128)(2,1)S(1)} %pad_maximum_fusion.2), channel_id=1, source_target_pairs={{0,2},{1,3},{2,0},{3,1},{4,6},{5,7},{6,4},{7,5},{8,10},{9,11},{10,... | collective-permute-start | bytes 786440 | tf_op jit(solution)/shard_map/ppermute | solution.py:35
  216.9 10.3 %collective-permute-start.37 = (bf16[128,1024]{1,0:T(8,128)(2,1)S(1)}, bf16[128,1024]{1,0:T(8,128)(2,1)S(1)}, u32[]{:S(2)}, u32[]{:S(2)}) collective-permute-start(bf16[128,1024]{1,0:T(8,128)(2,1)S(1)} %pad_maximum_fusion.1), channel_id=1, source_target_pairs={{0,1},{1,0},{2,3},{3,2},{4,5},{5,4},{6,7},{7,6},{8,9},{9,8},{10,11... | collective-permute-start | bytes 786440 | tf_op jit(solution)/shard_map/ppermute | solution.py:35
  (45 other events, 343.0 us)

commit v3 on v2

--- a/solution.py
+++ b/solution.py
@@ -24,7 +24,7 @@
 f32 = jnp.float32
 vmem_limit = 62 * 1024 * 1024
 tile_rows = 512
-chunks = ((0, 3), (3, 3), (6, 2))
+chunks = ((0, 4), (4, 4))
 any_space = pl.BlockSpec(memory_space=pl.ANY)
 in_vmem = pl.BlockSpec(memory_space=pltpu.VMEM)
 in_smem = pl.BlockSpec(memory_space=pltpu.SMEM)
@@ -207,18 +207,18 @@
     downs = take(2)
     earlier = take(1)[0] if has_sums else None
     outs = take(4 if cut else 1)
-    x, total, weight, down, weight_sem, x_sems, sum_sems, out_sems = refs
+    sets = len(slot_sets)
+    weights = take(sets)
+    x, total, act, down, weight_sems, x_sems, sum_sems, out_sems = refs
     tiles, tile_rows, _ = x.shape
-    width = weight.shape[0]
+    width = weights[0].shape[0]
     units = x.shape[2] - width
 
-    at = 0
-    for source in sources:
-        shards, depth, columns = source.shape
+    def load_weights(i):
+        shards, depth, _ = sources[i].shape
         for q in range(shards):
-            rows = pl.ds(q * depth, depth)
-            pltpu.make_async_copy(source.at[q], weight.at[rows, pl.ds(at, columns)], weight_sem.at[0]).start()
-        at += columns
+            target = weights[i].at[pl.ds(q * depth, depth), :]
+            pltpu.make_async_copy(sources[i].at[q], target, weight_sems.at[i]).start()
 
     def load_tile(tile):
         at = 0
@@ -229,32 +229,40 @@
                 pltpu.make_async_copy(block, target, x_sems.at[tile]).start()
             at += rows
 
-    load_tile(0)
+    load_weights(0)
+    for tile in range(tiles):
+        load_tile(tile)
+    for i in range(1, sets):
+        load_weights(i)
     at = 0
     for flip, first, count in slot_sets:
         source, target = downs[flip].at[pl.ds(first * units, count * units), :], down.at[pl.ds(at, count * units), :]
-        pltpu.make_async_copy(source, target, weight_sem.at[1]).start()
+        pltpu.make_async_copy(source, target, weight_sems.at[sets]).start()
         at += count * units
     for tile in range(tiles):
-        if tile:
-            load_tile(tile)
         if has_sums:
             source = earlier.at[pl.ds(tile * tile_rows, tile_rows), :]
             pltpu.make_async_copy(source, total.at[tile], sum_sems.at[tile]).start()
-    pltpu.make_async_copy(weight, weight, weight_sem.at[0]).wait()
-    pltpu.make_async_copy(down, down, weight_sem.at[1]).wait()
+
+    at = 0
+    for i, (flip, first, count) in enumerate(slot_sets):
+        pltpu.make_async_copy(weights[i], weights[i], weight_sems.at[i]).wait()
+        place = (where_ref[0] ^ flip) * group_slots + first
+
+        @pl.loop(0, tiles)
+        def _(tile, i=i, at=at, count=count, place=place):
+            if i == 0:
+                pltpu.make_async_copy(x.at[tile], x.at[tile], x_sems.at[tile]).wait()
+            both = jnp.dot(x[tile, :, :width], weights[i][...], preferred_element_type=f32)
+            parts = activate(both, x[tile, :, width:], place, count)
+            act[tile, :, at:at + count * units] = jnp.concatenate(parts, axis=1)
+
+        at += count * units
+    pltpu.make_async_copy(down, down, weight_sems.at[sets]).wait()
 
     @pl.loop(0, tiles)
     def _(tile):
-        pltpu.make_async_copy(x.at[tile], x.at[tile], x_sems.at[tile]).wait()
-        shares = x[tile, :, width:]
-        both = jnp.dot(x[tile, :, :width], weight[...], preferred_element_type=f32)
-        parts, at = [], 0
-        for flip, first, count in slot_sets:
-            place = (where_ref[0] ^ flip) * group_slots + first
-            parts += activate(both[:, at:at + 2 * count * units], shares, place, count)
-            at += 2 * count * units
-        added = jnp.dot(jnp.concatenate(parts, axis=1), down[...], preferred_element_type=f32)
+        added = jnp.dot(act[tile], down[...], preferred_element_type=f32)
         if has_sums:
             pltpu.make_async_copy(total.at[tile], total.at[tile], sum_sems.at[tile]).wait()
             added = added + total[tile].astype(f32)
@@ -302,12 +310,13 @@
         out_shape=out_shape,
         in_specs=[in_smem] + [any_space] * (len(blocks) + len(sources) + 2 + len(earlier)),
         out_specs=[any_space] * len(out_shape),
-        scratch_shapes=[
+        scratch_shapes=[pltpu.VMEM((depth * shards, source.shape[2]), bf16) for source in sources]
+        + [
             pltpu.VMEM((tiles, tile_rows, wide), bf16),
             pltpu.VMEM((tiles, tile_rows, width), bf16),
-            pltpu.VMEM((depth * shards, columns), bf16),
+            pltpu.VMEM((tiles, tile_rows, columns // 2), bf16),
             pltpu.VMEM((columns // 2, width), bf16),
-            pltpu.SemaphoreType.DMA((2,)),
+            pltpu.SemaphoreType.DMA((len(sources) + 1,)),
             pltpu.SemaphoreType.DMA((tiles,)),
             pltpu.SemaphoreType.DMA((tiles,)),
             pltpu.SemaphoreType.DMA((max(tiles, 2 * len(blocks)),)),
@@ -384,17 +393,17 @@
     own_chips = chip_gather(block)
     near = swap(block, "shard", 1)
     first_in = lax.ppermute(block, "shard", cross)
-    near, first_in, send, sends[2], *own_chips = stage(near, first_in, sends[1], sends[2], *own_chips)
+    second_in = lax.ppermute(near, "shard", cross)
+    near, first_in, second_in, send, *own_chips = stage(near, first_in, second_in, sends[1], *own_chips)
 
     near_chips = chip_gather(near)
     first_out = lax.ppermute(first_in, "shard", outward)
-    second_in = lax.ppermute(near, "shard", cross)
-    first_out, second_in, weights[0], *near_chips = stage(first_out, second_in, weights[0], *near_chips)
+    second_out = lax.ppermute(second_in, "shard", outward)
+    first_out, second_out, weights[0], *near_chips = stage(first_out, second_out, weights[0], *near_chips)
 
     weights.append(exchange(after(send, weights[0])))
     far_a = jnp.where(inner, first_in, first_out)
     far_a_chips = chip_gather(far_a)
-    second_out = lax.ppermute(second_in, "shard", outward)
 
     down = placed_down.reshape(slots * units, width)
     downs = [down, swap(after(down, near), "expert", 1)]
@@ -407,22 +416,19 @@
         return slots_block(where, blocks, sources, tuple(sets), downs, earlier, slots, cut)
 
     (early,) = run(near_chips + own_chips, slice(0, 1), [])
-    second_out, early, *far_a_chips = stage(second_out, early, *far_a_chips)
+    early, *far_a_chips = stage(early, *far_a_chips)
 
     far_b = jnp.where(inner, second_in, second_out)
     far_b_chips = chip_gather(far_b)
-    weights[1], *far_b_chips = stage(weights[1], *far_b_chips)
-
-    weights.append(exchange(after(sends[2], weights[1])))
+    far_b_chips = stage(*far_b_chips)
+    (late,) = run(list(far_a_chips) + list(far_b_chips), slice(0, 1), [])
+    weights[1], late = stage(weights[1], late)
     others.append(swap(weights[1], "expert", 1))
-    (late,) = run(far_a_chips + far_b_chips, slice(0, 2), [])
-    weights[2], late = stage(weights[2], late)
-    others.append(swap(weights[2], "expert", 1))
 
     sums = {}
-    far = run(far_a_chips + far_b_chips, slice(2, 3), [late], "labelled")
+    far = run(list(far_a_chips) + list(far_b_chips), slice(1, 2), [late], "labelled")
     far_x, far_y = swap(far[0], "expert", 2), swap(far[1], "expert", 4)
-    close = run(near_chips + own_chips, slice(1, 3), [after(early, far[2])], "ordered")
+    close = run(near_chips + own_chips, slice(1, 2), [after(early, far[2])], "ordered")
     far_x, far_y, *close = stage(far_x, far_y, *close)
     close_x, close_y = swap(close[0], "expert", 2), swap(close[1], "expert", 4)
     for pair, left, right, a_x, b_y in (

time: 229 us -> 221 us (0.965)
  Pallas kernels: 66.6 us -> 62 us
    ppermute x1, waiting for transfers between devices: 5.88 us -> 19.5 us  [quarter_body(): first_out = lax.ppermute(first_in, 'shard', outward)]
    ppermute x1, waiting for transfers between devices: 11.5 us -> 4.74 us  [quarter_body(): second_out = lax.ppermute(second_in, 'shard', outward)]
    all_to_all x3 -> x2, waiting for transfers between devices: 8.88 us -> 4.6 us  [exchange(): lax.all_to_all(send, 'shard', split_axis=0, concat_axis=0, tiled=True)]
    ppermute x38 -> x37, waiting for transfers between devices: 69.9 us -> 65.7 us  [swap(): return lax.ppermute(value, axis, [(i, i ^ bits) for i in range(size)])]
    pallas_call x4, Pallas kernels: 52.9 us -> 49.4 us  [slots_block(): pl.pallas_call(functools.partial(slots_kernel, slot_sets, group_slots, le...]
    all_to_all x3 -> x2, starting transfers between devices: 12.4 us -> 9.78 us  [exchange(): lax.all_to_all(send, 'shard', split_axis=0, concat_axis=0, tiled=True)]
    pallas_call x3 -> x2, Pallas kernels: 9.23 us -> 8.03 us  [quarters(): pl.pallas_call(quarters_kernel, out_shape=jax.ShapeDtypeStruct((shards, d...]
    ppermute x38 -> x37, starting transfers between devices: 39.1 us -> 39.7 us  [swap(): return lax.ppermute(value, axis, [(i, i ^ bits) for i in range(size)])]
  transfers between devices with their start and end apart: 45 -> 43, of which waited for: 29 -> 22; matrix products, arithmetic and copies ran while one was open for 2% -> 2% of each run, Pallas kernels for 25% -> 22%
where the time goes in v3:
time: 221 us; the launch traced here: 220 us
  waiting for transfers between devices  94.5 us (43%)
  Pallas kernels  62 us (28%)
  starting transfers between devices  53.4 us (24%)
  other arithmetic  6.45 us (3%)
  local copies, waits for them, and re-layouts  3.36 us (2%)
    ppermute x37, waiting for transfers between devices, swap(): return lax.ppermute(value, axis, [(i, i ^ bits) for i in range(size)])  65.7 us
    pallas_call x4, Pallas kernels, slots_block(): pl.pallas_call(functools.partial(slots_kernel, slot_sets, group_slots, le...  49.4 us
    ppermute x37, starting transfers between devices, swap(): return lax.ppermute(value, axis, [(i, i ^ bits) for i in range(size)])  39.7 us
    ppermute x1, waiting for transfers between devices, quarter_body(): first_out = lax.ppermute(first_in, 'shard', outward)  19.5 us
    all_to_all x2, starting transfers between devices, exchange(): lax.all_to_all(send, 'shard', split_axis=0, concat_axis=0, tiled=True)  9.78 us
    pallas_call x2, Pallas kernels, quarters(): pl.pallas_call(quarters_kernel, out_shape=jax.ShapeDtypeStruct((shards, d...  8.03 us
    ppermute x1, waiting for transfers between devices, quarter_body(): second_out = lax.ppermute(second_in, 'shard', outward)  4.74 us
    all_to_all x2, waiting for transfers between devices, exchange(): lax.all_to_all(send, 'shard', split_axis=0, concat_axis=0, tiled=True)  4.6 us
  transfers between devices with their start and end apart: 43, of which 22 were waited for; matrix products, arithmetic and copies ran while one was open for 2% of the time, Pallas kernels for 22%

profile of v3, /device:TPU:0, one launch (start us, length us, event | category | flops | bytes accessed | tf_op | source)
XLA Modules:
  0.0 220.1 jit_solution(5106585335389424543)
XLA Ops:
  1.0 4.0 %collective-permute-start.1 = (bf16[32,1024]{1,0:T(8,128)(2,1)S(1)}, bf16[32,1024]{1,0:T(8,128)(2,1)S(1)}, u32[]{:S(2)}, u32[]{:S(2)}) collective-permute-start(bf16[32,1024]{1,0:T(8,128)(2,1)S(1)} %constant_dynamic-slice_fusion), channel_id=1, source_target_pairs={{0,2},{1,3},{2,0},{3,1},{4,6},{5,7},{6,4},{7,5},{8,10},{9,11},{10,... | collective-permute-start | bytes 196616 | tf_op jit(solution)/shard_map/ppermute | solution.py:35
  6.7 4.0 %quarters.2 = bf16[4,256,1024]{2,1,0:T(8,128)(2,1)} custom-call(bf16[8,256,1024]{2,1,0:T(8,128)(2,1)} %weights_ref.3), custom_call_target="tpu_custom_call" | custom-call | bytes 4194304 | tf_op jit(solution)/shard_map/quarters/pallas_call | solution.py:68
  10.7 2.0 collective-permute-done.2
  12.8 4.5 %all-to-all-start = ((bf16[4,256,1024]{2,1,0:T(8,128)(2,1)}), bf16[4,256,1024]{2,1,0:T(8,128)(2,1)}, u32[]{:S(2)}, u32[]{:S(2)}) async-start(bf16[4,256,1024]{2,1,0:T(8,128)(2,1)} %quarters.2), calls=%async_computation | async-start | bytes 4194304 | tf_op jit(solution)/shard_map/all_to_all | solution.py:383
  17.2 2.5 %collective-permute-start.5 = (bf16[4,32,1024]{2,1,0:T(8,128)(2,1)S(1)}, bf16[4,32,1024]{2,1,0:T(8,128)(2,1)S(1)}, u32[]{:S(2)}, u32[]{:S(2)}) collective-permute-start(bf16[4,32,1024]{2,1,0:T(8,128)(2,1)S(1)} %pad_maximum_fusion.refs_0_), channel_id=1, source_target_pairs={{0,24},{4,28},{8,16},{12,20},{16,8},{20,12},{24,0},{28,4},{1,25},{... | collective-permute-start | bytes 786440 | tf_op jit(solution)/shard_map/ppermute | solution.py:35
  20.8 6.7 %collective-permute-done.5.refs_3_ = bf16[4,32,1024]{2,1,0:T(8,128)(2,1)S(1)} collective-permute-done((bf16[4,32,1024]{2,1,0:T(8,128)(2,1)S(1)}, bf16[4,32,1024]{2,1,0:T(8,128)(2,1)S(1)}, u32[]{:S(2)}, u32[]{:S(2)}) %collective-permute-start.5) | collective-permute-done | bytes 262176 | tf_op jit(solution)/shard_map/ppermute | solution.py:35
  27.5 2.8 %collective-permute-done.4.refs_2_ = bf16[4,32,1024]{2,1,0:T(8,128)(2,1)S(1)} collective-permute-done((bf16[4,32,1024]{2,1,0:T(8,128)(2,1)S(1)}, bf16[4,32,1024]{2,1,0:T(8,128)(2,1)S(1)}, u32[]{:S(2)}, u32[]{:S(2)}) %collective-permute-start.4) | collective-permute-done | bytes 262176 | tf_op jit(solution)/shard_map/ppermute | solution.py:35
  32.9 4.5 %project.1 = (bf16[128,1152]{1,0:T(8,128)(2,1)}, bf16[128,1024]{1,0:T(8,128)(2,1)}) custom-call(s32[3]{0:T(128)} %pad_add_fusion.where_ref, bf16[128,1024]{1,0:T(8,128)(2,1)} %heads_hbm.1, bf16[128,1024]{1,0:T(8,128)(2,1)} %residual_hbm.1, f32[1,1024]{1,0:T(1,128)} %bitcast.54, bf16[32,1024]{1,0:T(8,128)(2,1)} %bitcast.50, s32[8,128]{1,0:T(8,128)} %bitcast.55, ...), custom_call_target="tpu_custom_call" | custom-call | flops 268435456 | bytes 3145728 | tf_op jit(solution)/shard_map/project/pallas_call | solution.py:155
  39.1 1.7 collective-permute-start.15
  43.3 12.9 %collective-permute-done.10.refs_0_ = bf16[128,1152]{1,0:T(8,128)(2,1)S(1)} collective-permute-done((bf16[128,1152]{1,0:T(8,128)(2,1)}, bf16[128,1152]{1,0:T(8,128)(2,1)S(1)}, u32[]{:S(2)}, u32[]{:S(2)}) %collective-permute-start.10) | collective-permute-done | bytes 294944 | tf_op jit(solution)/shard_map/ppermute | solution.py:35
  56.9 4.0 %quarters.3 = bf16[4,256,1024]{2,1,0:T(8,128)(2,1)} custom-call(bf16[8,256,1024]{2,1,0:T(8,128)(2,1)} %weights_ref.3), custom_call_target="tpu_custom_call" | custom-call | bytes 4194304 | tf_op jit(solution)/shard_map/quarters/pallas_call | solution.py:68
  63.6 2.5 %collective-permute-start.20 = (bf16[128,1152]{1,0:T(8,128)(2,1)S(1)}, bf16[128,1152]{1,0:T(8,128)(2,1)S(1)}, u32[]{:S(2)}, u32[]{:S(2)}) collective-permute-start(bf16[128,1152]{1,0:T(8,128)(2,1)S(1)} %collective-permute-done.10.refs_0_), channel_id=1, source_target_pairs={{0,24},{4,28},{8,16},{12,20},{16,8},{20,12},{24,0},{28,4},{1,25},{... | collective-permute-start | bytes 884744 | tf_op jit(solution)/shard_map/ppermute | solution.py:35
  67.1 19.5 %collective-permute-done.16 = bf16[128,1152]{1,0:T(8,128)(2,1)S(1)} collective-permute-done((bf16[128,1152]{1,0:T(8,128)(2,1)S(1)}, bf16[128,1152]{1,0:T(8,128)(2,1)S(1)}, u32[]{:S(2)}, u32[]{:S(2)}) %collective-permute-start.16) | collective-permute-done | bytes 294944 | tf_op jit(solution)/shard_map/ppermute | solution.py:400
  86.6 4.7 %collective-permute-done.17 = bf16[128,1152]{1,0:T(8,128)(2,1)S(1)} collective-permute-done((bf16[128,1152]{1,0:T(8,128)(2,1)S(1)}, bf16[128,1152]{1,0:T(8,128)(2,1)S(1)}, u32[]{:S(2)}, u32[]{:S(2)}) %collective-permute-start.17) | collective-permute-done | bytes 294944 | tf_op jit(solution)/shard_map/ppermute | solution.py:401
  91.5 5.3 %all-to-all-start.1 = ((bf16[4,256,1024]{2,1,0:T(8,128)(2,1)}), bf16[4,256,1024]{2,1,0:T(8,128)(2,1)}, u32[]{:S(2)}, u32[]{:S(2)}) async-start(bf16[4,256,1024]{2,1,0:T(8,128)(2,1)} %quarters.3), calls=%async_computation.1 | async-start | bytes 4194304 | tf_op jit(solution)/shard_map/all_to_all | solution.py:383
  96.9 1.9 collective-permute-start.28
  100.5 7.3 %collective-permute-done.28.refs_7_ = bf16[128,1152]{1,0:T(8,128)(2,1)S(1)} collective-permute-done((bf16[128,1152]{1,0:T(8,128)(2,1)S(1)}, bf16[128,1152]{1,0:T(8,128)(2,1)S(1)}, u32[]{:S(2)}, u32[]{:S(2)}) %collective-permute-start.28) | collective-permute-done | bytes 294944 | tf_op jit(solution)/shard_map/ppermute | solution.py:35
  107.7 1.8 collective-permute-start.25
  109.5 4.5 %collective-permute-done.27.refs_6_ = bf16[128,1152]{1,0:T(8,128)(2,1)S(1)} collective-permute-done((bf16[128,1152]{1,0:T(8,128)(2,1)S(1)}, bf16[128,1152]{1,0:T(8,128)(2,1)S(1)}, u32[]{:S(2)}, u32[]{:S(2)}) %collective-permute-start.27) | collective-permute-done | bytes 294944 | tf_op jit(solution)/shard_map/ppermute | solution.py:35
  116.4 12.0 %slots_block.4.refs_12_ = bf16[1024,1024]{1,0:T(8,128)(2,1)} custom-call(s32[3]{0:T(128)} %pad_add_fusion.where_ref, bf16[128,1152]{1,0:T(8,128)(2,1)} %copy-done.17, bf16[128,1152]{1,0:T(8,128)(2,1)} %copy-done.21, bf16[128,1152]{1,0:T(8,128)(2,1)} %copy-done.20, bf16[128,1152]{1,0:T(8,128)(2,1)} %copy-done.19, ...), custom_call_target="tpu_custom_call" | custom-call | flops 6442450944 | bytes 12845056 | tf_op jit(solution)/shard_map/slots_block/pallas_call | solution.py:308
  129.1 12.0 %slots_block.5.refs_12_ = bf16[1024,1024]{1,0:T(8,128)(2,1)} custom-call(s32[3]{0:T(128)} %pad_add_fusion.where_ref, bf16[128,1152]{1,0:T(8,128)(2,1)} %copy-done.8, bf16[128,1152]{1,0:T(8,128)(2,1)} %collective-permute-done.23.refs_1_, bf16[128,1152]{1,0:T(8,128)(2,1)} %collective-permute-done.24.refs_2_, bf16[128,1152]{1,0:T(8,128)(2,1)} %copy-done.25, ...), custom_call_target="tpu_custom_call" | custom-call | flops 6442450944 | bytes 12845056 | tf_op jit(solution)/shard_map/slots_block/pallas_call | solution.py:308
  141.1 4.6 %all-to-all-done.1.refs_8_ = bf16[4,256,1024]{2,1,0:T(8,128)(2,1)} async-done(((bf16[4,256,1024]{2,1,0:T(8,128)(2,1)}), bf16[4,256,1024]{2,1,0:T(8,128)(2,1)}, u32[]{:S(2)}, u32[]{:S(2)}) %all-to-all-start.1) | async-done | bytes 2097184 | tf_op jit(solution)/shard_map/all_to_all | solution.py:383
  145.7 4.5 %collective-permute-done.29.refs_9_ = bf16[4,256,1024]{2,1,0:T(8,128)(2,1)} collective-permute-done((bf16[4,256,1024]{2,1,0:T(8,128)(2,1)}, bf16[4,256,1024]{2,1,0:T(8,128)(2,1)}, u32[]{:S(2)}, u32[]{:S(2)}) %collective-permute-start.29) | collective-permute-done | bytes 2097184 | tf_op jit(solution)/shard_map/ppermute | solution.py:35
  150.2 12.7 %slots_block.6 = (bf16[2,2,128,512]{3,2,1,0:T(8,128)(2,1)}, bf16[2,2,128,512]{3,2,1,0:T(8,128)(2,1)}, bf16[2,2,128,512]{3,2,1,0:T(8,128)(2,1)}, bf16[2,2,128,512]{3,2,1,0:T(8,128)(2,1)}) custom-call(s32[3]{0:T(128)} %pad_add_fusion.where_ref, bf16[128,1152]{1,0:T(8,128)(2,1)} %copy-done.8, bf16[128,1152]{1,0:T(8,128)(2,1)} %collective-permute-done.23.refs_1_, ...), custom_call_target="tpu_custom_call" | custom-call | flops 6442450944 | bytes 12845056 | tf_op jit(solution)/shard_map/slots_block/pallas_call | solution.py:308
  165.4 12.7 %slots_block.7 = (bf16[2,2,128,512]{3,2,1,0:T(8,128)(2,1)}, bf16[2,2,128,512]{3,2,1,0:T(8,128)(2,1)}, bf16[2,2,128,512]{3,2,1,0:T(8,128)(2,1)}, bf16[2,2,128,512]{3,2,1,0:T(8,128)(2,1)}) custom-call(s32[3]{0:T(128)} %pad_add_fusion.where_ref, bf16[128,1152]{1,0:T(8,128)(2,1)} %copy-done.17, bf16[128,1152]{1,0:T(8,128)(2,1)} %copy-done.21, ...), custom_call_target="tpu_custom_call" | custom-call | flops 6442450944 | bytes 12845056 | tf_op jit(solution)/shard_map/slots_block/pallas_call | solution.py:308
  184.7 4.1 %collective-permute-done.38 = bf16[2,128,512]{2,1,0:T(8,128)(2,1)S(1)} collective-permute-done((bf16[2,128,512]{2,1,0:T(8,128)(2,1)S(1)}, bf16[2,128,512]{2,1,0:T(8,128)(2,1)S(1)}, u32[]{:S(2)}, u32[]{:S(2)}) %collective-permute-start.38) | collective-permute-done | bytes 262176 | tf_op jit(solution)/shard_map/ppermute | solution.py:35
  191.9 3.4 %collective-permute-start.40 = (bf16[128,1024]{1,0:T(8,128)(2,1)S(1)}, bf16[128,1024]{1,0:T(8,128)(2,1)S(1)}, u32[]{:S(2)}, u32[]{:S(2)}) collective-permute-start(bf16[128,1024]{1,0:T(8,128)(2,1)S(1)} %pad_maximum_fusion.3), channel_id=1, source_target_pairs={{0,3},{1,2},{2,1},{3,0},{4,7},{5,6},{6,5},{7,4},{8,11},{9,10},{10,... | collective-permute-start | bytes 786440 | tf_op jit(solution)/shard_map/ppermute | solution.py:35
  195.2 3.1 %collective-permute-done.32 = bf16[2,2,128,512]{3,2,1,0:T(8,128)(2,1)S(1)} collective-permute-done((bf16[2,2,128,512]{3,2,1,0:T(8,128)(2,1)}, bf16[2,2,128,512]{3,2,1,0:T(8,128)(2,1)S(1)}, u32[]{:S(2)}, u32[]{:S(2)}) %collective-permute-start.32) | collective-permute-done | bytes 524320 | tf_op jit(solution)/shard_map/ppermute | solution.py:35
  201.5 4.3 %collective-permute-done.33 = bf16[2,128,512]{2,1,0:T(8,128)(2,1)S(1)} collective-permute-done((bf16[2,128,512]{2,1,0:T(8,128)(2,1)S(1)}, bf16[2,128,512]{2,1,0:T(8,128)(2,1)S(1)}, u32[]{:S(2)}, u32[]{:S(2)}) %collective-permute-start.33) | collective-permute-done | bytes 262176 | tf_op jit(solution)/shard_map/ppermute | solution.py:35
  207.7 2.6 %collective-permute-start.36 = (bf16[128,1024]{1,0:T(8,128)(2,1)S(1)}, bf16[128,1024]{1,0:T(8,128)(2,1)S(1)}, u32[]{:S(2)}, u32[]{:S(2)}) collective-permute-start(bf16[128,1024]{1,0:T(8,128)(2,1)S(1)} %pad_maximum_fusion.1), channel_id=1, source_target_pairs={{0,1},{1,0},{2,3},{3,2},{4,5},{5,4},{6,7},{7,6},{8,9},{9,8},{10,11... | collective-permute-start | bytes 786440 | tf_op jit(solution)/shard_map/ppermute | solution.py:35
  210.3 3.3 %collective-permute-done.39 = bf16[128,1024]{1,0:T(8,128)(2,1)S(1)} collective-permute-done((bf16[128,1024]{1,0:T(8,128)(2,1)S(1)}, bf16[128,1024]{1,0:T(8,128)(2,1)S(1)}, u32[]{:S(2)}, u32[]{:S(2)}) %collective-permute-start.39) | collective-permute-done | bytes 262176 | tf_op jit(solution)/shard_map/ppermute | solution.py:35
  213.6 5.3 %collective-permute-done.36 = bf16[128,1024]{1,0:T(8,128)(2,1)S(1)} collective-permute-done((bf16[128,1024]{1,0:T(8,128)(2,1)S(1)}, bf16[128,1024]{1,0:T(8,128)(2,1)S(1)}, u32[]{:S(2)}, u32[]{:S(2)}) %collective-permute-start.36) | collective-permute-done | bytes 262176 | tf_op jit(solution)/shard_map/ppermute | solution.py:35
  (139 shorter events, 38.0 us)
Async XLA Ops:
  1.0 9.6 %collective-permute-start.1 = (bf16[32,1024]{1,0:T(8,128)(2,1)S(1)}, bf16[32,1024]{1,0:T(8,128)(2,1)S(1)}, u32[]{:S(2)}, u32[]{:S(2)}) collective-permute-start(bf16[32,1024]{1,0:T(8,128)(2,1)S(1)} %constant_dynamic-slice_fusion), channel_id=1, source_target_pairs={{0,2},{1,3},{2,0},{3,1},{4,6},{5,7},{6,4},{7,5},{8,10},{9,11},{10,... | collective-permute-start | bytes 196616 | tf_op jit(solution)/shard_map/ppermute | solution.py:35
  12.8 78.6 %all-to-all-start = ((bf16[4,256,1024]{2,1,0:T(8,128)(2,1)}), bf16[4,256,1024]{2,1,0:T(8,128)(2,1)}, u32[]{:S(2)}, u32[]{:S(2)}) async-start(bf16[4,256,1024]{2,1,0:T(8,128)(2,1)} %quarters.2), calls=%async_computation | async-start | bytes 4194304 | tf_op jit(solution)/shard_map/all_to_all | solution.py:383
  17.2 10.2 %collective-permute-start.5 = (bf16[4,32,1024]{2,1,0:T(8,128)(2,1)S(1)}, bf16[4,32,1024]{2,1,0:T(8,128)(2,1)S(1)}, u32[]{:S(2)}, u32[]{:S(2)}) collective-permute-start(bf16[4,32,1024]{2,1,0:T(8,128)(2,1)S(1)} %pad_maximum_fusion.refs_0_), channel_id=1, source_target_pairs={{0,24},{4,28},{8,16},{12,20},{16,8},{20,12},{24,0},{28,4},{1,25},{... | collective-permute-start | bytes 786440 | tf_op jit(solution)/shard_map/ppermute | solution.py:35
  19.8 10.5 %collective-permute-start.4 = (bf16[4,32,1024]{2,1,0:T(8,128)(2,1)S(1)}, bf16[4,32,1024]{2,1,0:T(8,128)(2,1)S(1)}, u32[]{:S(2)}, u32[]{:S(2)}) collective-permute-start(bf16[4,32,1024]{2,1,0:T(8,128)(2,1)S(1)} %pad_maximum_fusion.refs_0_), channel_id=1, source_target_pairs={{0,16},{4,20},{8,24},{12,28},{16,0},{20,4},{24,8},{28,12},{1,17},{... | collective-permute-start | bytes 786440 | tf_op jit(solution)/shard_map/ppermute | solution.py:35
  20.3 10.1 %collective-permute-start.3 = (bf16[4,32,1024]{2,1,0:T(8,128)(2,1)S(1)}, bf16[4,32,1024]{2,1,0:T(8,128)(2,1)S(1)}, u32[]{:S(2)}, u32[]{:S(2)}) collective-permute-start(bf16[4,32,1024]{2,1,0:T(8,128)(2,1)S(1)} %pad_maximum_fusion.refs_0_), channel_id=1, source_target_pairs={{0,8},{4,12},{8,0},{12,4},{16,24},{20,28},{24,16},{28,20},{1,9},{5... | collective-permute-start | bytes 786440 | tf_op jit(solution)/shard_map/ppermute | solution.py:35
  20.8 10.6 %collective-permute-start.6 = (bf16[4,32,1024]{2,1,0:T(8,128)(2,1)S(1)}, bf16[4,32,1024]{2,1,0:T(8,128)(2,1)S(1)}, u32[]{:S(2)}, u32[]{:S(2)}) collective-permute-start(bf16[4,32,1024]{2,1,0:T(8,128)(2,1)S(1)} %pad_maximum_fusion.refs_0_), channel_id=1, source_target_pairs={{0,4},{4,0},{8,12},{12,8},{16,20},{20,16},{24,28},{28,24},{1,5},{5... | collective-permute-start | bytes 786440 | tf_op jit(solution)/shard_map/ppermute | solution.py:35
  37.4 18.8 %collective-permute-start.10 = (bf16[128,1152]{1,0:T(8,128)(2,1)}, bf16[128,1152]{1,0:T(8,128)(2,1)S(1)}, u32[]{:S(2)}, u32[]{:S(2)}) collective-permute-start(bf16[128,1152]{1,0:T(8,128)(2,1)} %get-tuple-element.63.refs_4_), channel_id=1, source_target_pairs={{0,1},{1,0},{2,3},{3,2},{4,5},{5,4},{6,7},{7,6},{8,9},{9,8},{10,11... | collective-permute-start | bytes 884744 | tf_op jit(solution)/shard_map/ppermute | solution.py:35
  39.1 21.8 %collective-permute-start.15 = (bf16[128,1152]{1,0:T(8,128)(2,1)}, bf16[128,1152]{1,0:T(8,128)(2,1)S(1)}, u32[]{:S(2)}, u32[]{:S(2)}) collective-permute-start(bf16[128,1152]{1,0:T(8,128)(2,1)} %get-tuple-element.63.refs_4_), channel_id=1, source_target_pairs={{0,24},{4,28},{8,16},{12,20},{16,8},{20,12},{24,0},{28,4},{1,25},{... | collective-permute-start | bytes 884744 | tf_op jit(solution)/shard_map/ppermute | solution.py:35
  40.9 20.0 %collective-permute-start.14 = (bf16[128,1152]{1,0:T(8,128)(2,1)}, bf16[128,1152]{1,0:T(8,128)(2,1)}, u32[]{:S(2)}, u32[]{:S(2)}) collective-permute-start(bf16[128,1152]{1,0:T(8,128)(2,1)} %get-tuple-element.63.refs_4_), channel_id=1, source_target_pairs={{0,16},{4,20},{8,24},{12,28},{16,0},{20,4},{24,8},{28,12},{1,17},{... | collective-permute-start | bytes 884744 | tf_op jit(solution)/shard_map/ppermute | solution.py:35
  42.1 18.8 %collective-permute-start.13 = (bf16[128,1152]{1,0:T(8,128)(2,1)}, bf16[128,1152]{1,0:T(8,128)(2,1)}, u32[]{:S(2)}, u32[]{:S(2)}) collective-permute-start(bf16[128,1152]{1,0:T(8,128)(2,1)} %get-tuple-element.63.refs_4_), channel_id=1, source_target_pairs={{0,8},{4,12},{8,0},{12,4},{16,24},{20,28},{24,16},{28,20},{1,9},{5... | collective-permute-start | bytes 884744 | tf_op jit(solution)/shard_map/ppermute | solution.py:35
  42.6 18.3 %collective-permute-start.11 = (bf16[128,1152]{1,0:T(8,128)(2,1)}, bf16[128,1152]{1,0:T(8,128)(2,1)S(1)}, u32[]{:S(2)}, u32[]{:S(2)}) collective-permute-start(bf16[128,1152]{1,0:T(8,128)(2,1)} %get-tuple-element.63.refs_4_), channel_id=1, source_target_pairs={{1,2},{2,1},{5,6},{6,5},{9,10},{10,9},{13,14},{14,13},{17,18},{18,... | collective-permute-start | bytes 884744 | tf_op jit(solution)/shard_map/ppermute | solution.py:395
  61.0 25.6 %collective-permute-start.16 = (bf16[128,1152]{1,0:T(8,128)(2,1)S(1)}, bf16[128,1152]{1,0:T(8,128)(2,1)S(1)}, u32[]{:S(2)}, u32[]{:S(2)}) collective-permute-start(bf16[128,1152]{1,0:T(8,128)(2,1)S(1)} %collective-permute-done.11), channel_id=1, source_target_pairs={{1,0},{2,3},{5,4},{6,7},{9,8},{10,11},{13,12},{14,15},{17,16},{18,... | collective-permute-start | bytes 884744 | tf_op jit(solution)/shard_map/ppermute | solution.py:400
  62.3 29.1 %collective-permute-start.17 = (bf16[128,1152]{1,0:T(8,128)(2,1)S(1)}, bf16[128,1152]{1,0:T(8,128)(2,1)S(1)}, u32[]{:S(2)}, u32[]{:S(2)}) collective-permute-start(bf16[128,1152]{1,0:T(8,128)(2,1)S(1)} %collective-permute-done.12), channel_id=1, source_target_pairs={{1,0},{2,3},{5,4},{6,7},{9,8},{10,11},{13,12},{14,15},{17,16},{18,... | collective-permute-start | bytes 884744 | tf_op jit(solution)/shard_map/ppermute | solution.py:401
  63.6 27.8 %collective-permute-start.20 = (bf16[128,1152]{1,0:T(8,128)(2,1)S(1)}, bf16[128,1152]{1,0:T(8,128)(2,1)S(1)}, u32[]{:S(2)}, u32[]{:S(2)}) collective-permute-start(bf16[128,1152]{1,0:T(8,128)(2,1)S(1)} %collective-permute-done.10.refs_0_), channel_id=1, source_target_pairs={{0,24},{4,28},{8,16},{12,20},{16,8},{20,12},{24,0},{28,4},{1,25},{... | collective-permute-start | bytes 884744 | tf_op jit(solution)/shard_map/ppermute | solution.py:35
  66.1 25.3 %collective-permute-start.19 = (bf16[128,1152]{1,0:T(8,128)(2,1)S(1)}, bf16[128,1152]{1,0:T(8,128)(2,1)S(1)}, u32[]{:S(2)}, u32[]{:S(2)}) collective-permute-start(bf16[128,1152]{1,0:T(8,128)(2,1)S(1)} %collective-permute-done.10.refs_0_), channel_id=1, source_target_pairs={{0,16},{4,20},{8,24},{12,28},{16,0},{20,4},{24,8},{28,12},{1,17},{... | collective-permute-start | bytes 884744 | tf_op jit(solution)/shard_map/ppermute | solution.py:35
  66.6 24.8 %collective-permute-start.18 = (bf16[128,1152]{1,0:T(8,128)(2,1)S(1)}, bf16[128,1152]{1,0:T(8,128)(2,1)S(1)}, u32[]{:S(2)}, u32[]{:S(2)}) collective-permute-start(bf16[128,1152]{1,0:T(8,128)(2,1)S(1)} %collective-permute-done.10.refs_0_), channel_id=1, source_target_pairs={{0,8},{4,12},{8,0},{12,4},{16,24},{20,28},{24,16},{28,20},{1,9},{5... | collective-permute-start | bytes 884744 | tf_op jit(solution)/shard_map/ppermute | solution.py:35
  86.6 29.8 %collective-permute-start.22 = (bf16[1024,1024]{1,0:T(8,128)(2,1)}, bf16[1024,1024]{1,0:T(8,128)(2,1)}, u32[]{:S(2)}, u32[]{:S(2)}) collective-permute-start(bf16[1024,1024]{1,0:T(8,128)(2,1)} %bitcast.58), channel_id=1, source_target_pairs={{0,4},{4,0},{8,12},{12,8},{16,20},{20,16},{24,28},{28,24},{1,5},{5... | collective-permute-start | bytes 6291464 | tf_op jit(solution)/shard_map/ppermute | solution.py:35
  91.4 25.0 %collective-permute-start.21 = (bf16[4,256,1024]{2,1,0:T(8,128)(2,1)}, bf16[4,256,1024]{2,1,0:T(8,128)(2,1)}, u32[]{:S(2)}, u32[]{:S(2)}) collective-permute-start(bf16[4,256,1024]{2,1,0:T(8,128)(2,1)} %all-to-all-done.refs_8_), channel_id=1, source_target_pairs={{0,4},{4,0},{8,12},{12,8},{16,20},{20,16},{24,28},{28,24},{1,5},{5... | collective-permute-start | bytes 6291464 | tf_op jit(solution)/shard_map/ppermute | solution.py:35
  91.5 54.3 %all-to-all-start.1 = ((bf16[4,256,1024]{2,1,0:T(8,128)(2,1)}), bf16[4,256,1024]{2,1,0:T(8,128)(2,1)}, u32[]{:S(2)}, u32[]{:S(2)}) async-start(bf16[4,256,1024]{2,1,0:T(8,128)(2,1)} %quarters.3), calls=%async_computation.1 | async-start | bytes 4194304 | tf_op jit(solution)/shard_map/all_to_all | solution.py:383
  96.9 10.9 %collective-permute-start.28 = (bf16[128,1152]{1,0:T(8,128)(2,1)S(1)}, bf16[128,1152]{1,0:T(8,128)(2,1)S(1)}, u32[]{:S(2)}, u32[]{:S(2)}) collective-permute-start(bf16[128,1152]{1,0:T(8,128)(2,1)S(1)} %broadcast_select_fusion.refs_4_), channel_id=1, source_target_pairs={{0,24},{4,28},{8,16},{12,20},{16,8},{20,12},{24,0},{28,4},{1,25},{... | collective-permute-start | bytes 884744 | tf_op jit(solution)/shard_map/ppermute | solution.py:35
  98.7 15.2 %collective-permute-start.27 = (bf16[128,1152]{1,0:T(8,128)(2,1)S(1)}, bf16[128,1152]{1,0:T(8,128)(2,1)S(1)}, u32[]{:S(2)}, u32[]{:S(2)}) collective-permute-start(bf16[128,1152]{1,0:T(8,128)(2,1)S(1)} %broadcast_select_fusion.refs_4_), channel_id=1, source_target_pairs={{0,16},{4,20},{8,24},{12,28},{16,0},{20,4},{24,8},{28,12},{1,17},{... | collective-permute-start | bytes 884744 | tf_op jit(solution)/shard_map/ppermute | solution.py:35
  99.9 15.6 %collective-permute-start.26 = (bf16[128,1152]{1,0:T(8,128)(2,1)S(1)}, bf16[128,1152]{1,0:T(8,128)(2,1)S(1)}, u32[]{:S(2)}, u32[]{:S(2)}) collective-permute-start(bf16[128,1152]{1,0:T(8,128)(2,1)S(1)} %broadcast_select_fusion.refs_4_), channel_id=1, source_target_pairs={{0,8},{4,12},{8,0},{12,4},{16,24},{20,28},{24,16},{28,20},{1,9},{5... | collective-permute-start | bytes 884744 | tf_op jit(solution)/shard_map/ppermute | solution.py:35
  107.7 20.7 %collective-permute-start.25 = (bf16[128,1152]{1,0:T(8,128)(2,1)S(1)}, bf16[128,1152]{1,0:T(8,128)(2,1)S(1)}, u32[]{:S(2)}, u32[]{:S(2)}) collective-permute-start(bf16[128,1152]{1,0:T(8,128)(2,1)S(1)} %broadcast_select_fusion.1.refs_0_), channel_id=1, source_target_pairs={{0,24},{4,28},{8,16},{12,20},{16,8},{20,12},{24,0},{28,4},{1,25},{... | collective-permute-start | bytes 884744 | tf_op jit(solution)/shard_map/ppermute | solution.py:35
  114.0 14.5 %collective-permute-start.24 = (bf16[128,1152]{1,0:T(8,128)(2,1)S(1)}, bf16[128,1152]{1,0:T(8,128)(2,1)}, u32[]{:S(2)}, u32[]{:S(2)}) collective-permute-start(bf16[128,1152]{1,0:T(8,128)(2,1)S(1)} %broadcast_select_fusion.1.refs_0_), channel_id=1, source_target_pairs={{0,16},{4,20},{8,24},{12,28},{16,0},{20,4},{24,8},{28,12},{1,17},{... | collective-permute-start | bytes 884744 | tf_op jit(solution)/shard_map/ppermute | solution.py:35
  116.2 12.3 %collective-permute-start.23 = (bf16[128,1152]{1,0:T(8,128)(2,1)S(1)}, bf16[128,1152]{1,0:T(8,128)(2,1)}, u32[]{:S(2)}, u32[]{:S(2)}) collective-permute-start(bf16[128,1152]{1,0:T(8,128)(2,1)S(1)} %broadcast_select_fusion.1.refs_0_), channel_id=1, source_target_pairs={{0,8},{4,12},{8,0},{12,4},{16,24},{20,28},{24,16},{28,20},{1,9},{5... | collective-permute-start | bytes 884744 | tf_op jit(solution)/shard_map/ppermute | solution.py:35
  162.9 15.2 %collective-permute-start.30 = (bf16[2,2,128,512]{3,2,1,0:T(8,128)(2,1)}, bf16[2,2,128,512]{3,2,1,0:T(8,128)(2,1)}, u32[]{:S(2)}, u32[]{:S(2)}) collective-permute-start(bf16[2,2,128,512]{3,2,1,0:T(8,128)(2,1)} %get-tuple-element.83), channel_id=1, source_target_pairs={{0,8},{4,12},{8,0},{12,4},{16,24},{20,28},{24,16},{28,20},{1,9},{5... | collective-permute-start | bytes 1572872 | tf_op jit(solution)/shard_map/ppermute | solution.py:35
  164.5 14.0 %collective-permute-start.31 = (bf16[2,2,128,512]{3,2,1,0:T(8,128)(2,1)}, bf16[2,2,128,512]{3,2,1,0:T(8,128)(2,1)}, u32[]{:S(2)}, u32[]{:S(2)}) collective-permute-start(bf16[2,2,128,512]{3,2,1,0:T(8,128)(2,1)} %get-tuple-element.84), channel_id=1, source_target_pairs={{0,16},{4,20},{8,24},{12,28},{16,0},{20,4},{24,8},{28,12},{1,17},{... | collective-permute-start | bytes 1572872 | tf_op jit(solution)/shard_map/ppermute | solution.py:35
  182.7 15.6 %collective-permute-start.32 = (bf16[2,2,128,512]{3,2,1,0:T(8,128)(2,1)}, bf16[2,2,128,512]{3,2,1,0:T(8,128)(2,1)S(1)}, u32[]{:S(2)}, u32[]{:S(2)}) collective-permute-start(bf16[2,2,128,512]{3,2,1,0:T(8,128)(2,1)} %get-tuple-element.93), channel_id=1, source_target_pairs={{0,8},{4,12},{8,0},{12,4},{16,24},{20,28},{24,16},{28,20},{1,9},{5... | collective-permute-start | bytes 1572872 | tf_op jit(solution)/shard_map/ppermute | solution.py:35
  183.6 17.4 %collective-permute-start.34 = (bf16[2,2,128,512]{3,2,1,0:T(8,128)(2,1)}, bf16[2,2,128,512]{3,2,1,0:T(8,128)(2,1)S(1)}, u32[]{:S(2)}, u32[]{:S(2)}) collective-permute-start(bf16[2,2,128,512]{3,2,1,0:T(8,128)(2,1)} %get-tuple-element.95), channel_id=1, source_target_pairs={{0,16},{4,20},{8,24},{12,28},{16,0},{20,4},{24,8},{28,12},{1,17},{... | collective-permute-start | bytes 1572872 | tf_op jit(solution)/shard_map/ppermute | solution.py:35
  191.9 18.4 %collective-permute-start.40 = (bf16[128,1024]{1,0:T(8,128)(2,1)S(1)}, bf16[128,1024]{1,0:T(8,128)(2,1)S(1)}, u32[]{:S(2)}, u32[]{:S(2)}) collective-permute-start(bf16[128,1024]{1,0:T(8,128)(2,1)S(1)} %pad_maximum_fusion.3), channel_id=1, source_target_pairs={{0,3},{1,2},{2,1},{3,0},{4,7},{5,6},{6,5},{7,4},{8,11},{9,10},{10,... | collective-permute-start | bytes 786440 | tf_op jit(solution)/shard_map/ppermute | solution.py:35
  199.6 14.1 %collective-permute-start.39 = (bf16[128,1024]{1,0:T(8,128)(2,1)S(1)}, bf16[128,1024]{1,0:T(8,128)(2,1)S(1)}, u32[]{:S(2)}, u32[]{:S(2)}) collective-permute-start(bf16[128,1024]{1,0:T(8,128)(2,1)S(1)} %pad_maximum_fusion.2), channel_id=1, source_target_pairs={{0,2},{1,3},{2,0},{3,1},{4,6},{5,7},{6,4},{7,5},{8,10},{9,11},{10,... | collective-permute-start | bytes 786440 | tf_op jit(solution)/shard_map/ppermute | solution.py:35
  207.7 11.3 %collective-permute-start.36 = (bf16[128,1024]{1,0:T(8,128)(2,1)S(1)}, bf16[128,1024]{1,0:T(8,128)(2,1)S(1)}, u32[]{:S(2)}, u32[]{:S(2)}) collective-permute-start(bf16[128,1024]{1,0:T(8,128)(2,1)S(1)} %pad_maximum_fusion.1), channel_id=1, source_target_pairs={{0,1},{1,0},{2,3},{3,2},{4,5},{5,4},{6,7},{7,6},{8,9},{9,8},{10,11... | collective-permute-start | bytes 786440 | tf_op jit(solution)/shard_map/ppermute | solution.py:35
  (37 other events, 338.3 us)

commit v4 on v3

--- a/solution.py
+++ b/solution.py
@@ -24,7 +24,7 @@
 f32 = jnp.float32
 vmem_limit = 62 * 1024 * 1024
 tile_rows = 512
-chunks = ((0, 4), (4, 4))
+chunks = ((0, 3), (3, 5))
 any_space = pl.BlockSpec(memory_space=pl.ANY)
 in_vmem = pl.BlockSpec(memory_space=pltpu.VMEM)
 in_smem = pl.BlockSpec(memory_space=pltpu.SMEM)
@@ -195,17 +195,18 @@
     return parts
 
 
-def slots_kernel(slot_sets, group_slots, block_count, has_sums, cut, where_ref, *refs):
+def slots_kernel(slot_sets, group_slots, block_rows, source_counts, sum_rows, cut, where_ref, *refs):
     refs = list(refs)
 
     def take(count):
         taken, refs[:] = refs[:count], refs[count:]
         return taken
 
+    block_count, has_sums = len(block_rows), bool(sum_rows)
     blocks = take(block_count)
-    sources = take(len(slot_sets))
+    sources = [take(count) for count in source_counts]
     downs = take(2)
-    earlier = take(1)[0] if has_sums else None
+    earlier = take(len(sum_rows))
     outs = take(4 if cut else 1)
     sets = len(slot_sets)
     weights = take(sets)
@@ -215,19 +216,22 @@
     units = x.shape[2] - width
 
     def load_weights(i):
-        shards, depth, _ = sources[i].shape
-        for q in range(shards):
-            target = weights[i].at[pl.ds(q * depth, depth), :]
-            pltpu.make_async_copy(sources[i].at[q], target, weight_sems.at[i]).start()
+        if len(sources[i]) == 1:
+            blocks = [sources[i][0].at[q] for q in range(sources[i][0].shape[0])]
+        else:
+            blocks = sources[i]
+        for k, block in enumerate(blocks):
+            depth = block.shape[0]
+            q = k if len(sources[i]) == 1 else where_ref[1] ^ k
+            target = weights[i].at[pl.ds(pl.multiple_of(q * depth, depth), depth), :]
+            pltpu.make_async_copy(block, target, weight_sems.at[i]).start()
 
     def load_tile(tile):
-        at = 0
-        for block in blocks:
-            rows = block.shape[0]
-            if at // tile_rows == tile:
-                target = x.at[tile, pl.ds(at % tile_rows, rows), :]
-                pltpu.make_async_copy(block, target, x_sems.at[tile]).start()
-            at += rows
+        rows = tiles * tile_rows // block_count
+        for i, (block, first) in enumerate(zip(blocks, block_rows)):
+            if i * rows // tile_rows == tile:
+                target = x.at[tile, pl.ds(i * rows % tile_rows, rows), :]
+                pltpu.make_async_copy(block.at[pl.ds(first, rows), :], target, x_sems.at[tile]).start()
 
     load_weights(0)
     for tile in range(tiles):
@@ -241,7 +245,7 @@
         at += count * units
     for tile in range(tiles):
         if has_sums:
-            source = earlier.at[pl.ds(tile * tile_rows, tile_rows), :]
+            source = earlier[tile].at[pl.ds(sum_rows[tile], tile_rows), :]
             pltpu.make_async_copy(source, total.at[tile], sum_sems.at[tile]).start()
 
     at = 0
@@ -272,7 +276,7 @@
             pltpu.make_async_copy(total.at[tile], target, out_sems.at[tile]).start()
 
     if cut:
-        rows, half = blocks[0].shape[0], width // 2
+        rows, half = tiles * tile_rows // block_count, width // 2
         parts = block_count // 4
         copies = []
         for part in range(parts):
@@ -294,37 +298,41 @@
             pltpu.make_async_copy(total.at[tile], target, out_sems.at[tile]).wait()
 
 
-def slots_block(where, blocks, sources, slot_sets, downs, earlier, group_slots, cut=None):
-    rows = sum(block.shape[0] for block in blocks)
-    wide = blocks[0].shape[1]
-    shards, depth, _ = sources[0].shape
+def slots_block(where, tokens, blocks, sources, slot_sets, downs, earlier, group_slots, cut=None):
+    block_rows = tuple(first for _, first in blocks)
+    sum_rows = tuple(first for _, first in earlier)
+    blocks, earlier = [block for block, _ in blocks], [total for total, _ in earlier]
+    rows, wide = len(blocks) * tokens, blocks[0].shape[1]
     width = downs[0].shape[1]
-    columns = sum(source.shape[2] for source in sources)
+    wides = [source[0].shape[-1] for source in sources]
+    columns = sum(wides)
+    source_counts = tuple(len(source) for source in sources)
+    sources = [block for source in sources for block in source]
     tiles = rows // tile_rows
     if cut:
-        out_shape = [jax.ShapeDtypeStruct((2, len(blocks) // 4, blocks[0].shape[0], width // 2), bf16)] * 4
+        out_shape = [jax.ShapeDtypeStruct((2, len(blocks) // 4, tokens, width // 2), bf16)] * 4
     else:
         out_shape = [jax.ShapeDtypeStruct((rows, width), bf16)]
     return pl.pallas_call(
-        functools.partial(slots_kernel, slot_sets, group_slots, len(blocks), bool(earlier), cut),
+        functools.partial(slots_kernel, slot_sets, group_slots, block_rows, source_counts, sum_rows, cut),
         out_shape=out_shape,
         in_specs=[in_smem] + [any_space] * (len(blocks) + len(sources) + 2 + len(earlier)),
         out_specs=[any_space] * len(out_shape),
-        scratch_shapes=[pltpu.VMEM((depth * shards, source.shape[2]), bf16) for source in sources]
+        scratch_shapes=[pltpu.VMEM((width, columns), bf16) for columns in wides]
         + [
             pltpu.VMEM((tiles, tile_rows, wide), bf16),
             pltpu.VMEM((tiles, tile_rows, width), bf16),
             pltpu.VMEM((tiles, tile_rows, columns // 2), bf16),
             pltpu.VMEM((columns // 2, width), bf16),
-            pltpu.SemaphoreType.DMA((len(sources) + 1,)),
+            pltpu.SemaphoreType.DMA((len(wides) + 1,)),
             pltpu.SemaphoreType.DMA((tiles,)),
             pltpu.SemaphoreType.DMA((tiles,)),
             pltpu.SemaphoreType.DMA((max(tiles, 2 * len(blocks)),)),
         ],
         compiler_params=pltpu.CompilerParams(vmem_limit_bytes=vmem_limit),
         cost_estimate=pl.CostEstimate(
-            flops=2 * rows * columns * (depth * shards + width // 2),
-            bytes_accessed=2 * (rows * (wide + 2 * width) + columns * (depth * shards + width // 2)),
+            flops=3 * rows * columns * width,
+            bytes_accessed=2 * rows * (wide + 2 * width) + 3 * columns * width,
             transcendentals=rows * columns // 2,
         ),
         name="slots_block",
@@ -377,14 +385,19 @@
     own = lax.dynamic_slice_in_dim(output_weight, e * piece, piece, 0)
     over_z = jnp.stack([own] + [swap(own, "shard", k) for k in range(1, shards)])
 
-    sends = [quarters(placed_gate_up, first, count, shards) for first, count in chunks]
+    sends = [quarters(placed_gate_up, *chunks[0], shards)]
 
     def exchange(send):
         return lax.all_to_all(send, "shard", split_axis=0, concat_axis=0, tiled=True)
 
     over_z, send = stage(over_z, sends[0])
     weights = [exchange(send)]
-    pieces = core_gather(chip_gather(over_z))
+    down = placed_down.reshape(slots * units, width)
+    pieces = chip_gather(over_z)
+    sends.append(quarters(after(placed_gate_up, pieces[1]), *chunks[1], shards))
+    *pieces, other_down, sends[1] = stage(*pieces, swap(after(down, over_z), "expert", 1), sends[1])
+    pieces = core_gather(pieces)
+    downs = [down, other_down]
     block, hidden = project(where, head_outputs, residual, norm_gain, router, routes, replica_pick, placement, pieces)
 
     cross = [(1, 2), (2, 1)]
@@ -394,41 +407,52 @@
     near = swap(block, "shard", 1)
     first_in = lax.ppermute(block, "shard", cross)
     second_in = lax.ppermute(near, "shard", cross)
-    near, first_in, second_in, send, *own_chips = stage(near, first_in, second_in, sends[1], *own_chips)
-
-    near_chips = chip_gather(near)
+    parts = [lax.dynamic_index_in_dim(sends[1], s ^ k, 0, keepdims=False) for k in range(shards)]
+    near, first_in, second_in, *rest = stage(near, first_in, second_in, *parts, *own_chips)
+    parts, own_chips = rest[:4], rest[4:]
+
+    near_chips = [near, swap(near, "expert", 2), swap(near, "expert", 4)]
     first_out = lax.ppermute(first_in, "shard", outward)
     second_out = lax.ppermute(second_in, "shard", outward)
-    first_out, second_out, weights[0], *near_chips = stage(first_out, second_out, weights[0], *near_chips)
-
-    weights.append(exchange(after(send, weights[0])))
-    far_a = jnp.where(inner, first_in, first_out)
-    far_a_chips = chip_gather(far_a)
-
-    down = placed_down.reshape(slots * units, width)
-    downs = [down, swap(after(down, near), "expert", 1)]
-    others = [swap(weights[0], "expert", 1)]
+    part_in = lax.ppermute(parts[3], "shard", cross)
+    first_out, second_out, weights[0], part_in, *rest = stage(
+        first_out, second_out, weights[0], part_in, *parts, *near_chips
+    )
+    parts, near_chips = list(rest[:4]), list(rest[4:])
+
+    parts[1] = swap(parts[1], "shard", 1)
+    parts[2] = swap(parts[2], "shard", 2)
+    far = jnp.concatenate([jnp.where(inner, first_in, first_out), jnp.where(inner, second_in, second_out)])
+    far_chips = chip_gather(far)
+
+    weights = [[weights[0]]]
+    others = [[swap(weights[0][0], "expert", 1)]]
     def run(blocks, which, earlier, cut=None):
         sources, sets = [], []
         for chunk in range(len(chunks))[which]:
             sources += [weights[chunk], others[chunk]]
             sets += [(0, *chunks[chunk]), (1, *chunks[chunk])]
-        return slots_block(where, blocks, sources, tuple(sets), downs, earlier, slots, cut)
-
-    (early,) = run(near_chips + own_chips, slice(0, 1), [])
-    early, *far_a_chips = stage(early, *far_a_chips)
-
-    far_b = jnp.where(inner, second_in, second_out)
-    far_b_chips = chip_gather(far_b)
-    far_b_chips = stage(*far_b_chips)
-    (late,) = run(list(far_a_chips) + list(far_b_chips), slice(0, 1), [])
-    weights[1], late = stage(weights[1], late)
-    others.append(swap(weights[1], "expert", 1))
+        return slots_block(where, rows, blocks, sources, tuple(sets), downs, earlier, slots, cut)
+
+    own_blocks = [(chip, 0) for chip in own_chips]
+    (early,) = run(own_blocks, slice(0, 1), [])
+    early, *rest = stage(early, *parts[1:], near_chips[0], *far_chips)
+    parts[1:], near_chips[0], far_chips = rest[:3], rest[3], rest[4:]
+
+    part_out = lax.ppermute(parts[3], "shard", [(0, 3), (3, 0)])
+    near_blocks = [(chip, 0) for chip in near_chips + [swap(near_chips[0], "expert", 6)]]
+    far_blocks = [(chip, first) for first in (0, rows) for chip in far_chips]
+    (late,) = run(far_blocks, slice(0, 1), [])
+    (middle,) = run(near_blocks, slice(0, 1), [])
+    part_out, late, middle = stage(part_out, late, middle)
+    parts[3] = jnp.where(inner, part_in, part_out)
+    weights.append(parts)
+    others.append([swap(part, "expert", 1) for part in parts])
 
     sums = {}
-    far = run(list(far_a_chips) + list(far_b_chips), slice(1, 2), [late], "labelled")
+    far = run(far_blocks, slice(1, 2), [(late, 0), (late, tile_rows)], "labelled")
     far_x, far_y = swap(far[0], "expert", 2), swap(far[1], "expert", 4)
-    close = run(near_chips + own_chips, slice(1, 2), [after(early, far[2])], "ordered")
+    close = run(near_blocks + own_blocks, slice(1, 2), [(middle, 0), (after(early, far[2]), 0)], "ordered")
     far_x, far_y, *close = stage(far_x, far_y, *close)
     close_x, close_y = swap(close[0], "expert", 2), swap(close[1], "expert", 4)
     for pair, left, right, a_x, b_y in (

time: 221 us -> 218 us (0.986)
  waiting for transfers between devices: 94.5 us -> 82.7 us
  Pallas kernels: 62 us -> 69 us
  other arithmetic: 6.45 us -> 9.56 us
  starting transfers between devices: 53.4 us -> 50.7 us
    pallas_call x4 -> x5, Pallas kernels: 49.4 us -> 55.9 us  [slots_block(): pl.pallas_call(functools.partial(slots_kernel, slot_sets, group_slots, bl...]
    all_to_all x2 -> x1, starting transfers between devices: 9.78 us -> 4.36 us  [exchange(): lax.all_to_all(send, 'shard', split_axis=0, concat_axis=0, tiled=True)]
    ppermute x0 -> x2, starting transfers between devices: none -> 5.11 us  [the longest x1 4.4 us: quarter_body(): part_out = lax.ppermute(parts[3], 'shard', [(0, 3), (3, 0)])]
    all_to_all x2 -> x1, waiting for transfers between devices: 4.6 us -> 0.01 us  [exchange(): lax.all_to_all(send, 'shard', split_axis=0, concat_axis=0, tiled=True)]
    ppermute x1, waiting for transfers between devices: 19.5 us -> 14.9 us  [quarter_body(): first_out = lax.ppermute(first_in, 'shard', outward)]
    ppermute x37 -> x39, starting transfers between devices: 39.7 us -> 35.9 us  [swap(): return lax.ppermute(value, axis, [(i, i ^ bits) for i in range(size)])]
    squeeze x0 -> x1, local copies, waits for them, and re-layouts: none -> 2.92 us  [quarter_body(): lax.dynamic_index_in_dim(sends[1], s ^ k, 0, keepdims=False)]
    select_n x2, other arithmetic: 0.07 us -> 2.29 us  [the longest x1 1.17 us: quarter_body(): parts[3] = jnp.where(inner, part_in, part_out)]
  transfers between devices with their start and end apart: 43 -> 46, of which waited for: 22 -> 20; matrix products, arithmetic and copies ran while one was open for 2% -> 5% of each run, Pallas kernels for 22% -> 25%
where the time goes in v4:
time: 218 us; the launch traced here: 217 us
  waiting for transfers between devices  82.7 us (38%)
  Pallas kernels  69 us (32%)
  starting transfers between devices  50.7 us (23%)
  other arithmetic  9.56 us (4%)
  local copies, waits for them, and re-layouts  4.9 us (2%)
    ppermute x39, waiting for transfers between devices, swap(): return lax.ppermute(value, axis, [(i, i ^ bits) for i in range(size)])  64.1 us
    pallas_call x5, Pallas kernels, slots_block(): pl.pallas_call(functools.partial(slots_kernel, slot_sets, group_slots, bl...  55.9 us
    ppermute x39, starting transfers between devices, swap(): return lax.ppermute(value, axis, [(i, i ^ bits) for i in range(size)])  35.9 us
    ppermute x1, waiting for transfers between devices, quarter_body(): first_out = lax.ppermute(first_in, 'shard', outward)  14.9 us
    pallas_call x2, Pallas kernels, quarters(): pl.pallas_call(quarters_kernel, out_shape=jax.ShapeDtypeStruct((shards, d...  8.56 us
    pallas_call x1, Pallas kernels, project(): pl.pallas_call(project_kernel, out_shape=(jax.ShapeDtypeStruct((rows, wid...  4.5 us
    ppermute x1, starting transfers between devices, quarter_body(): part_out = lax.ppermute(parts[3], 'shard', [(0, 3), (3, 0)])  4.4 us
    all_to_all x1, starting transfers between devices, exchange(): lax.all_to_all(send, 'shard', split_axis=0, concat_axis=0, tiled=True)  4.36 us
  transfers between devices with their start and end apart: 46, of which 20 were waited for; matrix products, arithmetic and copies ran while one was open for 5% of the time, Pallas kernels for 25%

profile of v4, /device:TPU:0, one launch (start us, length us, event | category | flops | bytes accessed | tf_op | source)
XLA Modules:
  0.0 217.4 jit_solution(17175737636352172980)
XLA Ops:
  1.0 4.0 %collective-permute-start.1 = (bf16[32,1024]{1,0:T(8,128)(2,1)S(1)}, bf16[32,1024]{1,0:T(8,128)(2,1)S(1)}, u32[]{:S(2)}, u32[]{:S(2)}) collective-permute-start(bf16[32,1024]{1,0:T(8,128)(2,1)S(1)} %constant_dynamic-slice_fusion), channel_id=1, source_target_pairs={{0,2},{1,3},{2,0},{3,1},{4,6},{5,7},{6,4},{7,5},{8,10},{9,11},{10,... | collective-permute-start | bytes 196616 | tf_op jit(solution)/shard_map/ppermute | solution.py:35
  6.7 3.5 %quarters.2 = bf16[4,256,768]{2,1,0:T(8,128)(2,1)} custom-call(bf16[8,256,1024]{2,1,0:T(8,128)(2,1)} %weights_ref.2), custom_call_target="tpu_custom_call" | custom-call | bytes 3145728 | tf_op jit(solution)/shard_map/quarters/pallas_call | solution.py:68
  11.5 4.4 %all-to-all-start = ((bf16[4,256,768]{2,1,0:T(8,128)(2,1)}), bf16[4,256,768]{2,1,0:T(8,128)(2,1)}, u32[]{:S(2)}, u32[]{:S(2)}) async-start(bf16[4,256,768]{2,1,0:T(8,128)(2,1)} %quarters.2), calls=%async_computation | async-start | bytes 3145728 | tf_op jit(solution)/shard_map/all_to_all | solution.py:391
  15.9 1.6 collective-permute-start.3
  17.5 1.5 collective-permute-start.4
  19.5 5.6 %collective-permute-done.3.refs_1_ = bf16[4,32,1024]{2,1,0:T(8,128)(2,1)S(1)} collective-permute-done((bf16[4,32,1024]{2,1,0:T(8,128)(2,1)S(1)}, bf16[4,32,1024]{2,1,0:T(8,128)(2,1)S(1)}, u32[]{:S(2)}, u32[]{:S(2)}) %collective-permute-start.3) | collective-permute-done | bytes 262176 | tf_op jit(solution)/shard_map/ppermute | solution.py:35
  25.1 5.0 %quarters.3 = bf16[4,256,1280]{2,1,0:T(8,128)(2,1)} custom-call(bf16[8,256,1024]{2,1,0:T(8,128)(2,1)} %weights_ref.2), custom_call_target="tpu_custom_call" | custom-call | bytes 5242880 | tf_op jit(solution)/shard_map/quarters/pallas_call | solution.py:68
  35.0 4.5 %project.1 = (bf16[128,1152]{1,0:T(8,128)(2,1)}, bf16[128,1024]{1,0:T(8,128)(2,1)}) custom-call(s32[3]{0:T(128)} %pad_add_fusion.where_ref, bf16[128,1024]{1,0:T(8,128)(2,1)} %heads_hbm.1, bf16[128,1024]{1,0:T(8,128)(2,1)} %residual_hbm.1, f32[1,1024]{1,0:T(1,128)} %bitcast.68, bf16[32,1024]{1,0:T(8,128)(2,1)} %bitcast.64, s32[8,128]{1,0:T(8,128)} %bitcast.69, ...), custom_call_target="tpu_custom_call" | custom-call | flops 268435456 | bytes 3145728 | tf_op jit(solution)/shard_map/project/pallas_call | solution.py:155
  39.5 1.7 collective-permute-start.11
  46.0 10.2 %collective-permute-done.11.refs_0_ = bf16[128,1152]{1,0:T(8,128)(2,1)S(1)} collective-permute-done((bf16[128,1152]{1,0:T(8,128)(2,1)}, bf16[128,1152]{1,0:T(8,128)(2,1)S(1)}, u32[]{:S(2)}, u32[]{:S(2)}) %collective-permute-start.11) | collective-permute-done | bytes 294944 | tf_op jit(solution)/shard_map/ppermute | solution.py:35
  57.7 2.9 %dynamic-slice_bitcast_fusion = (bf16[256,1280]{1,0:T(8,128)(2,1)S(1)}, bf16[256,1280]{1,0:T(8,128)(2,1)}, bf16[256,1280]{1,0:T(8,128)(2,1)}, bf16[256,1280]{1,0:T(8,128)(2,1)S(1)}) fusion(bf16[4,256,1280]{2,1,0:T(8,128)(2,1)} %quarters.3, s32[]{:T(128)S(6)} %select_n.40, s32[]{:T(128)S(6)} %select_n.39, s32[]{:T(128)S(6)} %select_n.38, s32[]{:T(128)S(6)} %select_n.37), kind=kLoop, calls=%fused_computation | loop fusion | bytes 5242896 | tf_op jit(solution)/shard_map/jit(dynamic_index_in_dim)/squeeze | solution.py:410
  66.1 14.9 %collective-permute-done.17 = bf16[128,1152]{1,0:T(8,128)(2,1)} collective-permute-done((bf16[128,1152]{1,0:T(8,128)(2,1)}, bf16[128,1152]{1,0:T(8,128)(2,1)}, u32[]{:S(2)}, u32[]{:S(2)}) %collective-permute-start.17) | collective-permute-done | bytes 294944 | tf_op jit(solution)/shard_map/ppermute | solution.py:415
  81.0 3.7 %collective-permute-done.18 = bf16[128,1152]{1,0:T(8,128)(2,1)} collective-permute-done((bf16[128,1152]{1,0:T(8,128)(2,1)}, bf16[128,1152]{1,0:T(8,128)(2,1)}, u32[]{:S(2)}, u32[]{:S(2)}) %collective-permute-start.18) | collective-permute-done | bytes 294944 | tf_op jit(solution)/shard_map/ppermute | solution.py:416
  85.1 1.8 collective-permute-start.24
  90.0 1.6 collective-permute-start.26
  92.5 7.7 %slots_block.5.refs_19_ = bf16[512,1024]{1,0:T(8,128)(2,1)} custom-call(s32[3]{0:T(128)} %pad_add_fusion.where_ref, bf16[128,1152]{1,0:T(8,128)(2,1)} %get-tuple-element.76.refs_0_.refs_4_, bf16[128,1152]{1,0:T(8,128)(2,1)} %copy-done.11, bf16[128,1152]{1,0:T(8,128)(2,1)} %copy-done.12, bf16[128,1152]{1,0:T(8,128)(2,1)} %copy-done.13, ...), custom_call_target="tpu_custom_call" | custom-call | flops 2415919104 | bytes 7995392 | tf_op jit(solution)/shard_map/slots_block/pallas_call | solution.py:316
  100.2 5.3 %collective-permute-done.25.refs_1_.refs_5_ = bf16[256,1152]{1,0:T(8,128)(2,1)} collective-permute-done((bf16[256,1152]{1,0:T(8,128)(2,1)}, bf16[256,1152]{1,0:T(8,128)(2,1)}, u32[]{:S(2)}, u32[]{:S(2)}) %collective-permute-start.25) | collective-permute-done | bytes 589856 | tf_op jit(solution)/shard_map/ppermute | solution.py:35
  105.5 11.4 %collective-permute-done.26.refs_2_.refs_6_ = bf16[256,1152]{1,0:T(8,128)(2,1)} collective-permute-done((bf16[256,1152]{1,0:T(8,128)(2,1)}, bf16[256,1152]{1,0:T(8,128)(2,1)}, u32[]{:S(2)}, u32[]{:S(2)}) %collective-permute-start.26) | collective-permute-done | bytes 589856 | tf_op jit(solution)/shard_map/ppermute | solution.py:35
  118.0 1.8 collective-permute-start.29
  119.8 4.4 %collective-permute-start.28 = (bf16[256,1280]{1,0:T(8,128)(2,1)S(1)}, bf16[256,1280]{1,0:T(8,128)(2,1)}, u32[]{:S(2)}, u32[]{:S(2)}) collective-permute-start(bf16[256,1280]{1,0:T(8,128)(2,1)S(1)} %get-tuple-element.104), channel_id=1, source_target_pairs={{0,3},{3,0},{4,7},{7,4},{8,11},{11,8},{12,15},{15,12},{16,19},{19,... | collective-permute-start | bytes 1966088 | tf_op jit(solution)/shard_map/ppermute | solution.py:442
  124.8 10.0 %slots_block.6.refs_18_.refs_19_ = bf16[1024,1024]{1,0:T(8,128)(2,1)} custom-call(s32[3]{0:T(128)} %pad_add_fusion.where_ref, bf16[256,1152]{1,0:T(8,128)(2,1)} %pad_maximum_fusion.refs_0_.refs_4_, bf16[256,1152]{1,0:T(8,128)(2,1)} %collective-permute-done.25.refs_1_.refs_5_, bf16[256,1152]{1,0:T(8,128)(2,1)} %collective-permute-done.26.refs_2_.refs_6_, ...), custom_call_target="tpu_custom_call" | custom-call | flops 4831838208 | bytes 11272192 | tf_op jit(solution)/shard_map/slots_block/pallas_call | solution.py:316
  134.9 7.7 %slots_block.7.refs_18_ = bf16[512,1024]{1,0:T(8,128)(2,1)} custom-call(s32[3]{0:T(128)} %pad_add_fusion.where_ref, bf16[128,1152]{1,0:T(8,128)(2,1)} %copy-done.10, bf16[128,1152]{1,0:T(8,128)(2,1)} %collective-permute-done.20.refs_1_, bf16[128,1152]{1,0:T(8,128)(2,1)} %collective-permute-done.21.refs_2_, ...), custom_call_target="tpu_custom_call" | custom-call | flops 2415919104 | bytes 7995392 | tf_op jit(solution)/shard_map/slots_block/pallas_call | solution.py:316
  144.0 2.1 collective-permute-done.33.refs_15_
  146.1 15.0 %slots_block.8 = (bf16[2,2,128,512]{3,2,1,0:T(8,128)(2,1)}, bf16[2,2,128,512]{3,2,1,0:T(8,128)(2,1)}, bf16[2,2,128,512]{3,2,1,0:T(8,128)(2,1)}, bf16[2,2,128,512]{3,2,1,0:T(8,128)(2,1)}) custom-call(s32[3]{0:T(128)} %pad_add_fusion.where_ref, bf16[256,1152]{1,0:T(8,128)(2,1)} %pad_maximum_fusion.refs_0_.refs_4_, ...), custom_call_target="tpu_custom_call" | custom-call | flops 8053063680 | bytes 14417920 | tf_op jit(solution)/shard_map/slots_block/pallas_call | solution.py:316
  162.9 15.4 %slots_block.9 = (bf16[2,2,128,512]{3,2,1,0:T(8,128)(2,1)}, bf16[2,2,128,512]{3,2,1,0:T(8,128)(2,1)}, bf16[2,2,128,512]{3,2,1,0:T(8,128)(2,1)}, bf16[2,2,128,512]{3,2,1,0:T(8,128)(2,1)}) custom-call(s32[3]{0:T(128)} %pad_add_fusion.where_ref, bf16[128,1152]{1,0:T(8,128)(2,1)} %copy-done.10, bf16[128,1152]{1,0:T(8,128)(2,1)} %collective-permute-done.20.refs_1_, ...), custom_call_target="tpu_custom_call" | custom-call | flops 8053063680 | bytes 14417920 | tf_op jit(solution)/shard_map/slots_block/pallas_call | solution.py:316
  181.3 1.6 collective-permute-start.42
  184.6 4.0 %collective-permute-done.41 = bf16[2,128,512]{2,1,0:T(8,128)(2,1)S(1)} collective-permute-done((bf16[2,128,512]{2,1,0:T(8,128)(2,1)S(1)}, bf16[2,128,512]{2,1,0:T(8,128)(2,1)S(1)}, u32[]{:S(2)}, u32[]{:S(2)}) %collective-permute-start.41) | collective-permute-done | bytes 262176 | tf_op jit(solution)/shard_map/ppermute | solution.py:35
  191.9 8.3 %collective-permute-done.36 = bf16[2,2,128,512]{3,2,1,0:T(8,128)(2,1)S(1)} collective-permute-done((bf16[2,2,128,512]{3,2,1,0:T(8,128)(2,1)}, bf16[2,2,128,512]{3,2,1,0:T(8,128)(2,1)S(1)}, u32[]{:S(2)}, u32[]{:S(2)}) %collective-permute-start.36) | collective-permute-done | bytes 524320 | tf_op jit(solution)/shard_map/ppermute | solution.py:35
  201.5 1.6 collective-permute-start.44
  204.3 2.6 %collective-permute-done.37 = bf16[2,128,512]{2,1,0:T(8,128)(2,1)S(1)} collective-permute-done((bf16[2,128,512]{2,1,0:T(8,128)(2,1)S(1)}, bf16[2,128,512]{2,1,0:T(8,128)(2,1)S(1)}, u32[]{:S(2)}, u32[]{:S(2)}) %collective-permute-start.37) | collective-permute-done | bytes 262176 | tf_op jit(solution)/shard_map/ppermute | solution.py:35
  207.0 2.6 %collective-permute-done.39 = bf16[2,128,512]{2,1,0:T(8,128)(2,1)S(1)} collective-permute-done((bf16[2,128,512]{2,1,0:T(8,128)(2,1)S(1)}, bf16[2,128,512]{2,1,0:T(8,128)(2,1)S(1)}, u32[]{:S(2)}, u32[]{:S(2)}) %collective-permute-start.39) | collective-permute-done | bytes 262176 | tf_op jit(solution)/shard_map/ppermute | solution.py:35
  209.9 6.3 %collective-permute-done.40 = bf16[128,1024]{1,0:T(8,128)(2,1)S(1)} collective-permute-done((bf16[128,1024]{1,0:T(8,128)(2,1)S(1)}, bf16[128,1024]{1,0:T(8,128)(2,1)S(1)}, u32[]{:S(2)}, u32[]{:S(2)}) %collective-permute-start.40) | collective-permute-done | bytes 262176 | tf_op jit(solution)/shard_map/ppermute | solution.py:35
  (140 shorter events, 41.9 us)
Async XLA Ops:
  11.5 20.1 %collective-permute-start.6 = (bf16[1024,1024]{1,0:T(8,128)(2,1)}, bf16[1024,1024]{1,0:T(8,128)(2,1)}, u32[]{:S(2)}, u32[]{:S(2)}) collective-permute-start(bf16[1024,1024]{1,0:T(8,128)(2,1)} %bitcast.58), channel_id=1, source_target_pairs={{0,4},{4,0},{8,12},{12,8},{16,20},{20,16},{24,28},{28,24},{1,5},{5... | collective-permute-start | bytes 6291464 | tf_op jit(solution)/shard_map/ppermute | solution.py:35
  11.5 54.6 %all-to-all-start = ((bf16[4,256,768]{2,1,0:T(8,128)(2,1)}), bf16[4,256,768]{2,1,0:T(8,128)(2,1)}, u32[]{:S(2)}, u32[]{:S(2)}) async-start(bf16[4,256,768]{2,1,0:T(8,128)(2,1)} %quarters.2), calls=%async_computation | async-start | bytes 3145728 | tf_op jit(solution)/shard_map/all_to_all | solution.py:391
  15.9 9.2 %collective-permute-start.3 = (bf16[4,32,1024]{2,1,0:T(8,128)(2,1)S(1)}, bf16[4,32,1024]{2,1,0:T(8,128)(2,1)S(1)}, u32[]{:S(2)}, u32[]{:S(2)}) collective-permute-start(bf16[4,32,1024]{2,1,0:T(8,128)(2,1)S(1)} %pad_maximum_fusion.1.refs_0_), channel_id=1, source_target_pairs={{0,8},{4,12},{8,0},{12,4},{16,24},{20,28},{24,16},{28,20},{1,9},{5... | collective-permute-start | bytes 786440 | tf_op jit(solution)/shard_map/ppermute | solution.py:35
  17.5 14.0 %collective-permute-start.4 = (bf16[4,32,1024]{2,1,0:T(8,128)(2,1)S(1)}, bf16[4,32,1024]{2,1,0:T(8,128)(2,1)S(1)}, u32[]{:S(2)}, u32[]{:S(2)}) collective-permute-start(bf16[4,32,1024]{2,1,0:T(8,128)(2,1)S(1)} %pad_maximum_fusion.1.refs_0_), channel_id=1, source_target_pairs={{0,16},{4,20},{8,24},{12,28},{16,0},{20,4},{24,8},{28,12},{1,17},{... | collective-permute-start | bytes 786440 | tf_op jit(solution)/shard_map/ppermute | solution.py:35
  19.0 12.5 %collective-permute-start.5 = (bf16[4,32,1024]{2,1,0:T(8,128)(2,1)S(1)}, bf16[4,32,1024]{2,1,0:T(8,128)(2,1)S(1)}, u32[]{:S(2)}, u32[]{:S(2)}) collective-permute-start(bf16[4,32,1024]{2,1,0:T(8,128)(2,1)S(1)} %pad_maximum_fusion.1.refs_0_), channel_id=1, source_target_pairs={{0,24},{4,28},{8,16},{12,20},{16,8},{20,12},{24,0},{28,4},{1,25},{... | collective-permute-start | bytes 786440 | tf_op jit(solution)/shard_map/ppermute | solution.py:35
  39.5 16.8 %collective-permute-start.11 = (bf16[128,1152]{1,0:T(8,128)(2,1)}, bf16[128,1152]{1,0:T(8,128)(2,1)S(1)}, u32[]{:S(2)}, u32[]{:S(2)}) collective-permute-start(bf16[128,1152]{1,0:T(8,128)(2,1)} %get-tuple-element.76.refs_0_.refs_4_), channel_id=1, source_target_pairs={{0,1},{1,0},{2,3},{3,2},{4,5},{5,4},{6,7},{7,6},{8,9},{9,8},{10,11... | collective-permute-start | bytes 884744 | tf_op jit(solution)/shard_map/ppermute | solution.py:35
  41.2 19.4 %collective-permute-start.12 = (bf16[128,1152]{1,0:T(8,128)(2,1)}, bf16[128,1152]{1,0:T(8,128)(2,1)}, u32[]{:S(2)}, u32[]{:S(2)}) collective-permute-start(bf16[128,1152]{1,0:T(8,128)(2,1)} %get-tuple-element.76.refs_0_.refs_4_), channel_id=1, source_target_pairs={{1,2},{2,1},{5,6},{6,5},{9,10},{10,9},{13,14},{14,13},{17,18},{18,... | collective-permute-start | bytes 884744 | tf_op jit(solution)/shard_map/ppermute | solution.py:408
  42.5 18.0 %collective-permute-start.14 = (bf16[128,1152]{1,0:T(8,128)(2,1)}, bf16[128,1152]{1,0:T(8,128)(2,1)S(1)}, u32[]{:S(2)}, u32[]{:S(2)}) collective-permute-start(bf16[128,1152]{1,0:T(8,128)(2,1)} %get-tuple-element.76.refs_0_.refs_4_), channel_id=1, source_target_pairs={{0,8},{4,12},{8,0},{12,4},{16,24},{20,28},{24,16},{28,20},{1,9},{5... | collective-permute-start | bytes 884744 | tf_op jit(solution)/shard_map/ppermute | solution.py:35
  43.7 16.9 %collective-permute-start.15 = (bf16[128,1152]{1,0:T(8,128)(2,1)}, bf16[128,1152]{1,0:T(8,128)(2,1)S(1)}, u32[]{:S(2)}, u32[]{:S(2)}) collective-permute-start(bf16[128,1152]{1,0:T(8,128)(2,1)} %get-tuple-element.76.refs_0_.refs_4_), channel_id=1, source_target_pairs={{0,16},{4,20},{8,24},{12,28},{16,0},{20,4},{24,8},{28,12},{1,17},{... | collective-permute-start | bytes 884744 | tf_op jit(solution)/shard_map/ppermute | solution.py:35
  44.6 16.0 %collective-permute-start.16 = (bf16[128,1152]{1,0:T(8,128)(2,1)}, bf16[128,1152]{1,0:T(8,128)(2,1)S(1)}, u32[]{:S(2)}, u32[]{:S(2)}) collective-permute-start(bf16[128,1152]{1,0:T(8,128)(2,1)} %get-tuple-element.76.refs_0_.refs_4_), channel_id=1, source_target_pairs={{0,24},{4,28},{8,16},{12,20},{16,8},{20,12},{24,0},{28,4},{1,25},{... | collective-permute-start | bytes 884744 | tf_op jit(solution)/shard_map/ppermute | solution.py:35
  60.6 24.1 %collective-permute-start.19 = (bf16[256,1280]{1,0:T(8,128)(2,1)S(1)}, bf16[256,1280]{1,0:T(8,128)(2,1)S(1)}, u32[]{:S(2)}, u32[]{:S(2)}) collective-permute-start(bf16[256,1280]{1,0:T(8,128)(2,1)S(1)} %get-tuple-element.104), channel_id=1, source_target_pairs={{1,2},{2,1},{5,6},{6,5},{9,10},{10,9},{13,14},{14,13},{17,18},{18,... | collective-permute-start | bytes 1966088 | tf_op jit(solution)/shard_map/ppermute | solution.py:417
  61.4 19.6 %collective-permute-start.17 = (bf16[128,1152]{1,0:T(8,128)(2,1)}, bf16[128,1152]{1,0:T(8,128)(2,1)}, u32[]{:S(2)}, u32[]{:S(2)}) collective-permute-start(bf16[128,1152]{1,0:T(8,128)(2,1)} %collective-permute-done.12), channel_id=1, source_target_pairs={{1,0},{2,3},{5,4},{6,7},{9,8},{10,11},{13,12},{14,15},{17,16},{18,... | collective-permute-start | bytes 884744 | tf_op jit(solution)/shard_map/ppermute | solution.py:415
  62.7 22.1 %collective-permute-start.18 = (bf16[128,1152]{1,0:T(8,128)(2,1)}, bf16[128,1152]{1,0:T(8,128)(2,1)}, u32[]{:S(2)}, u32[]{:S(2)}) collective-permute-start(bf16[128,1152]{1,0:T(8,128)(2,1)} %collective-permute-done.13), channel_id=1, source_target_pairs={{1,0},{2,3},{5,4},{6,7},{9,8},{10,11},{13,12},{14,15},{17,16},{18,... | collective-permute-start | bytes 884744 | tf_op jit(solution)/shard_map/ppermute | solution.py:416
  64.0 20.8 %collective-permute-start.20 = (bf16[128,1152]{1,0:T(8,128)(2,1)S(1)}, bf16[128,1152]{1,0:T(8,128)(2,1)}, u32[]{:S(2)}, u32[]{:S(2)}) collective-permute-start(bf16[128,1152]{1,0:T(8,128)(2,1)S(1)} %collective-permute-done.11.refs_0_), channel_id=1, source_target_pairs={{0,8},{4,12},{8,0},{12,4},{16,24},{20,28},{24,16},{28,20},{1,9},{5... | collective-permute-start | bytes 884744 | tf_op jit(solution)/shard_map/ppermute | solution.py:35
  65.2 19.6 %collective-permute-start.21 = (bf16[128,1152]{1,0:T(8,128)(2,1)S(1)}, bf16[128,1152]{1,0:T(8,128)(2,1)}, u32[]{:S(2)}, u32[]{:S(2)}) collective-permute-start(bf16[128,1152]{1,0:T(8,128)(2,1)S(1)} %collective-permute-done.11.refs_0_), channel_id=1, source_target_pairs={{0,16},{4,20},{8,24},{12,28},{16,0},{20,4},{24,8},{28,12},{1,17},{... | collective-permute-start | bytes 884744 | tf_op jit(solution)/shard_map/ppermute | solution.py:35
  84.9 33.2 %collective-permute-start.23 = (bf16[256,1280]{1,0:T(8,128)(2,1)}, bf16[256,1280]{1,0:T(8,128)(2,1)}, u32[]{:S(2)}, u32[]{:S(2)}) collective-permute-start(bf16[256,1280]{1,0:T(8,128)(2,1)} %get-tuple-element.90), channel_id=1, source_target_pairs={{0,1},{1,0},{2,3},{3,2},{4,5},{5,4},{6,7},{7,6},{8,9},{9,8},{10,11... | collective-permute-start | bytes 1966088 | tf_op jit(solution)/shard_map/ppermute | solution.py:35
  85.1 32.9 %collective-permute-start.24 = (bf16[256,1280]{1,0:T(8,128)(2,1)}, bf16[256,1280]{1,0:T(8,128)(2,1)}, u32[]{:S(2)}, u32[]{:S(2)}) collective-permute-start(bf16[256,1280]{1,0:T(8,128)(2,1)} %get-tuple-element.91), channel_id=1, source_target_pairs={{0,2},{1,3},{2,0},{3,1},{4,6},{5,7},{6,4},{7,5},{8,10},{9,11},{10,... | collective-permute-start | bytes 1966088 | tf_op jit(solution)/shard_map/ppermute | solution.py:35
  89.0 16.5 %collective-permute-start.25 = (bf16[256,1152]{1,0:T(8,128)(2,1)}, bf16[256,1152]{1,0:T(8,128)(2,1)}, u32[]{:S(2)}, u32[]{:S(2)}) collective-permute-start(bf16[256,1152]{1,0:T(8,128)(2,1)} %pad_maximum_fusion.refs_0_.refs_4_), channel_id=1, source_target_pairs={{0,8},{4,12},{8,0},{12,4},{16,24},{20,28},{24,16},{28,20},{1,9},{5... | collective-permute-start | bytes 1769480 | tf_op jit(solution)/shard_map/ppermute | solution.py:35
  90.0 26.9 %collective-permute-start.26 = (bf16[256,1152]{1,0:T(8,128)(2,1)}, bf16[256,1152]{1,0:T(8,128)(2,1)}, u32[]{:S(2)}, u32[]{:S(2)}) collective-permute-start(bf16[256,1152]{1,0:T(8,128)(2,1)} %pad_maximum_fusion.refs_0_.refs_4_), channel_id=1, source_target_pairs={{0,16},{4,20},{8,24},{12,28},{16,0},{20,4},{24,8},{28,12},{1,17},{... | collective-permute-start | bytes 1769480 | tf_op jit(solution)/shard_map/ppermute | solution.py:35
  91.6 26.4 %collective-permute-start.27 = (bf16[256,1152]{1,0:T(8,128)(2,1)}, bf16[256,1152]{1,0:T(8,128)(2,1)}, u32[]{:S(2)}, u32[]{:S(2)}) collective-permute-start(bf16[256,1152]{1,0:T(8,128)(2,1)} %pad_maximum_fusion.refs_0_.refs_4_), channel_id=1, source_target_pairs={{0,24},{4,28},{8,16},{12,20},{16,8},{20,12},{24,0},{28,4},{1,25},{... | collective-permute-start | bytes 1769480 | tf_op jit(solution)/shard_map/ppermute | solution.py:35
  105.5 38.4 %collective-permute-start.30 = (bf16[256,1280]{1,0:T(8,128)(2,1)S(1)}, bf16[256,1280]{1,0:T(8,128)(2,1)}, u32[]{:S(2)}, u32[]{:S(2)}) collective-permute-start(bf16[256,1280]{1,0:T(8,128)(2,1)S(1)} %get-tuple-element.100.refs_8_), channel_id=1, source_target_pairs={{0,4},{4,0},{8,12},{12,8},{16,20},{20,16},{24,28},{28,24},{1,5},{5... | collective-permute-start | bytes 1966088 | tf_op jit(solution)/shard_map/ppermute | solution.py:35
  118.0 16.9 %collective-permute-start.29 = (bf16[128,1152]{1,0:T(8,128)(2,1)}, bf16[128,1152]{1,0:T(8,128)(2,1)}, u32[]{:S(2)}, u32[]{:S(2)}) collective-permute-start(bf16[128,1152]{1,0:T(8,128)(2,1)} %copy-done.10), channel_id=1, source_target_pairs={{0,24},{4,28},{8,16},{12,20},{16,8},{20,12},{24,0},{28,4},{1,25},{... | collective-permute-start | bytes 884744 | tf_op jit(solution)/shard_map/ppermute | solution.py:35
  119.8 22.8 %collective-permute-start.28 = (bf16[256,1280]{1,0:T(8,128)(2,1)S(1)}, bf16[256,1280]{1,0:T(8,128)(2,1)}, u32[]{:S(2)}, u32[]{:S(2)}) collective-permute-start(bf16[256,1280]{1,0:T(8,128)(2,1)S(1)} %get-tuple-element.104), channel_id=1, source_target_pairs={{0,3},{3,0},{4,7},{7,4},{8,11},{11,8},{12,15},{15,12},{16,19},{19,... | collective-permute-start | bytes 1966088 | tf_op jit(solution)/shard_map/ppermute | solution.py:442
  124.2 19.7 %collective-permute-start.31 = (bf16[256,1280]{1,0:T(8,128)(2,1)}, bf16[256,1280]{1,0:T(8,128)(2,1)}, u32[]{:S(2)}, u32[]{:S(2)}) collective-permute-start(bf16[256,1280]{1,0:T(8,128)(2,1)} %collective-permute-done.23.refs_9_), channel_id=1, source_target_pairs={{0,4},{4,0},{8,12},{12,8},{16,20},{20,16},{24,28},{28,24},{1,5},{5... | collective-permute-start | bytes 1966088 | tf_op jit(solution)/shard_map/ppermute | solution.py:35
  124.3 19.6 %collective-permute-start.32 = (bf16[256,1280]{1,0:T(8,128)(2,1)}, bf16[256,1280]{1,0:T(8,128)(2,1)}, u32[]{:S(2)}, u32[]{:S(2)}) collective-permute-start(bf16[256,1280]{1,0:T(8,128)(2,1)} %collective-permute-done.24.refs_10_), channel_id=1, source_target_pairs={{0,4},{4,0},{8,12},{12,8},{16,20},{20,16},{24,28},{28,24},{1,5},{5... | collective-permute-start | bytes 1966088 | tf_op jit(solution)/shard_map/ppermute | solution.py:35
  161.1 17.2 %collective-permute-start.34 = (bf16[2,2,128,512]{3,2,1,0:T(8,128)(2,1)}, bf16[2,2,128,512]{3,2,1,0:T(8,128)(2,1)}, u32[]{:S(2)}, u32[]{:S(2)}) collective-permute-start(bf16[2,2,128,512]{3,2,1,0:T(8,128)(2,1)} %get-tuple-element.110), channel_id=1, source_target_pairs={{0,8},{4,12},{8,0},{12,4},{16,24},{20,28},{24,16},{28,20},{1,9},{5... | collective-permute-start | bytes 1572872 | tf_op jit(solution)/shard_map/ppermute | solution.py:35
  161.6 16.7 %collective-permute-start.35 = (bf16[2,2,128,512]{3,2,1,0:T(8,128)(2,1)}, bf16[2,2,128,512]{3,2,1,0:T(8,128)(2,1)}, u32[]{:S(2)}, u32[]{:S(2)}) collective-permute-start(bf16[2,2,128,512]{3,2,1,0:T(8,128)(2,1)} %get-tuple-element.111), channel_id=1, source_target_pairs={{0,16},{4,20},{8,24},{12,28},{16,0},{20,4},{24,8},{28,12},{1,17},{... | collective-permute-start | bytes 1572872 | tf_op jit(solution)/shard_map/ppermute | solution.py:35
  179.4 9.3 %collective-permute-start.41 = (bf16[2,128,512]{2,1,0:T(8,128)(2,1)S(1)}, bf16[2,128,512]{2,1,0:T(8,128)(2,1)S(1)}, u32[]{:S(2)}, u32[]{:S(2)}) collective-permute-start(bf16[2,128,512]{2,1,0:T(8,128)(2,1)S(1)} %fusion.7), channel_id=1, source_target_pairs={{0,16},{4,20},{8,24},{12,28},{16,0},{20,4},{24,8},{28,12},{1,17},{... | collective-permute-start | bytes 786440 | tf_op jit(solution)/shard_map/ppermute | solution.py:35
  181.3 9.3 %collective-permute-start.42 = (bf16[2,128,512]{2,1,0:T(8,128)(2,1)S(1)}, bf16[2,128,512]{2,1,0:T(8,128)(2,1)S(1)}, u32[]{:S(2)}, u32[]{:S(2)}) collective-permute-start(bf16[2,128,512]{2,1,0:T(8,128)(2,1)S(1)} %fusion.8), channel_id=1, source_target_pairs={{0,8},{4,12},{8,0},{12,4},{16,24},{20,28},{24,16},{28,20},{1,9},{5... | collective-permute-start | bytes 786440 | tf_op jit(solution)/shard_map/ppermute | solution.py:35
  183.0 17.2 %collective-permute-start.36 = (bf16[2,2,128,512]{3,2,1,0:T(8,128)(2,1)}, bf16[2,2,128,512]{3,2,1,0:T(8,128)(2,1)S(1)}, u32[]{:S(2)}, u32[]{:S(2)}) collective-permute-start(bf16[2,2,128,512]{3,2,1,0:T(8,128)(2,1)} %get-tuple-element.121), channel_id=1, source_target_pairs={{0,8},{4,12},{8,0},{12,4},{16,24},{20,28},{24,16},{28,20},{1,9},{5... | collective-permute-start | bytes 1572872 | tf_op jit(solution)/shard_map/ppermute | solution.py:35
  183.4 19.7 %collective-permute-start.38 = (bf16[2,2,128,512]{3,2,1,0:T(8,128)(2,1)}, bf16[2,2,128,512]{3,2,1,0:T(8,128)(2,1)S(1)}, u32[]{:S(2)}, u32[]{:S(2)}) collective-permute-start(bf16[2,2,128,512]{3,2,1,0:T(8,128)(2,1)} %get-tuple-element.123), channel_id=1, source_target_pairs={{0,16},{4,20},{8,24},{12,28},{16,0},{20,4},{24,8},{28,12},{1,17},{... | collective-permute-start | bytes 1572872 | tf_op jit(solution)/shard_map/ppermute | solution.py:35
  191.8 18.1 %collective-permute-start.43 = (bf16[128,1024]{1,0:T(8,128)(2,1)S(1)}, bf16[128,1024]{1,0:T(8,128)(2,1)S(1)}, u32[]{:S(2)}, u32[]{:S(2)}) collective-permute-start(bf16[128,1024]{1,0:T(8,128)(2,1)S(1)} %pad_maximum_fusion.3), channel_id=1, source_target_pairs={{0,2},{1,3},{2,0},{3,1},{4,6},{5,7},{6,4},{7,5},{8,10},{9,11},{10,... | collective-permute-start | bytes 786440 | tf_op jit(solution)/shard_map/ppermute | solution.py:35
  (36 other events, 297.0 us)

commit v5 on v4

--- a/solution.py
+++ b/solution.py
@@ -222,9 +222,14 @@
             blocks = sources[i]
         for k, block in enumerate(blocks):
             depth = block.shape[0]
-            q = k if len(sources[i]) == 1 else where_ref[1] ^ k
+            last = min(k, 3)
+            q = k if len(sources[i]) == 1 else where_ref[1] ^ last
             target = weights[i].at[pl.ds(pl.multiple_of(q * depth, depth), depth), :]
-            pltpu.make_async_copy(block, target, weight_sems.at[i]).start()
+            copy = pltpu.make_async_copy(block, target, weight_sems.at[i])
+            if len(sources[i]) == 1 or k < 3:
+                copy.start()
+            else:
+                pl.when(where_ref[2] == (1 if k == 3 else 0))(copy.start)
 
     def load_tile(tile):
         rows = tiles * tile_rows // block_count
@@ -445,7 +450,7 @@
     (late,) = run(far_blocks, slice(0, 1), [])
     (middle,) = run(near_blocks, slice(0, 1), [])
     part_out, late, middle = stage(part_out, late, middle)
-    parts[3] = jnp.where(inner, part_in, part_out)
+    parts[3:] = [part_in, part_out]
     weights.append(parts)
     others.append([swap(part, "expert", 1) for part in parts])
 

time: 218 us -> 218 us (level)
    ppermute x39 -> x40, waiting for transfers between devices: 64.1 us -> 64.3 us  [swap(): return lax.ppermute(value, axis, [(i, i ^ bits) for i in range(size)])]
    ppermute x39 -> x40, starting transfers between devices: 35.9 us -> 35.9 us  [swap(): return lax.ppermute(value, axis, [(i, i ^ bits) for i in range(size)])]
  transfers between devices with their start and end apart: 46 -> 47, of which waited for: 20 -> 20; matrix products, arithmetic and copies ran while one was open for 5% -> 4% of each run, Pallas kernels for 25% -> 25%
where the time goes in v5:
time: 218 us; the launch traced here: 217 us
  waiting for transfers between devices  82.2 us (38%)
  Pallas kernels  69.2 us (32%)
  starting transfers between devices  51.5 us (24%)
  other arithmetic  8.35 us (4%)
  local copies, waits for them, and re-layouts  5.75 us (3%)
    ppermute x40, waiting for transfers between devices, swap(): return lax.ppermute(value, axis, [(i, i ^ bits) for i in range(size)])  64.3 us
    pallas_call x5, Pallas kernels, slots_block(): pl.pallas_call(functools.partial(slots_kernel, slot_sets, group_slots, bl...  56.1 us
    ppermute x40, starting transfers between devices, swap(): return lax.ppermute(value, axis, [(i, i ^ bits) for i in range(size)])  35.9 us
    ppermute x1, waiting for transfers between devices, quarter_body(): first_out = lax.ppermute(first_in, 'shard', outward)  14.1 us
    pallas_call x2, Pallas kernels, quarters(): pl.pallas_call(quarters_kernel, out_shape=jax.ShapeDtypeStruct((shards, d...  8.56 us
    pallas_call x1, Pallas kernels, project(): pl.pallas_call(project_kernel, out_shape=(jax.ShapeDtypeStruct((rows, wid...  4.51 us
    ppermute x1, starting transfers between devices, quarter_body(): part_out = lax.ppermute(parts[3], 'shard', [(0, 3), (3, 0)])  4.41 us
    all_to_all x1, starting transfers between devices, exchange(): lax.all_to_all(send, 'shard', split_axis=0, concat_axis=0, tiled=True)  4.36 us
  transfers between devices with their start and end apart: 47, of which 20 were waited for; matrix products, arithmetic and copies ran while one was open for 4% of the time, Pallas kernels for 25%

profile of v5, /device:TPU:0, one launch (start us, length us, event | category | flops | bytes accessed | tf_op | source)
XLA Modules:
  0.0 217.4 jit_solution(17693994980233378951)
XLA Ops:
  1.0 4.0 %collective-permute-start.1 = (bf16[32,1024]{1,0:T(8,128)(2,1)S(1)}, bf16[32,1024]{1,0:T(8,128)(2,1)S(1)}, u32[]{:S(2)}, u32[]{:S(2)}) collective-permute-start(bf16[32,1024]{1,0:T(8,128)(2,1)S(1)} %constant_dynamic-slice_fusion), channel_id=1, source_target_pairs={{0,2},{1,3},{2,0},{3,1},{4,6},{5,7},{6,4},{7,5},{8,10},{9,11},{10,... | collective-permute-start | bytes 196616 | tf_op jit(solution)/shard_map/ppermute | solution.py:35
  6.7 3.5 %quarters.2 = bf16[4,256,768]{2,1,0:T(8,128)(2,1)} custom-call(bf16[8,256,1024]{2,1,0:T(8,128)(2,1)} %weights_ref.2), custom_call_target="tpu_custom_call" | custom-call | bytes 3145728 | tf_op jit(solution)/shard_map/quarters/pallas_call | solution.py:68
  11.5 4.4 %all-to-all-start = ((bf16[4,256,768]{2,1,0:T(8,128)(2,1)}), bf16[4,256,768]{2,1,0:T(8,128)(2,1)}, u32[]{:S(2)}, u32[]{:S(2)}) async-start(bf16[4,256,768]{2,1,0:T(8,128)(2,1)} %quarters.2), calls=%async_computation | async-start | bytes 3145728 | tf_op jit(solution)/shard_map/all_to_all | solution.py:396
  15.9 1.6 collective-permute-start.3
  17.5 1.5 collective-permute-start.4
  19.5 5.6 %collective-permute-done.3.refs_1_ = bf16[4,32,1024]{2,1,0:T(8,128)(2,1)S(1)} collective-permute-done((bf16[4,32,1024]{2,1,0:T(8,128)(2,1)S(1)}, bf16[4,32,1024]{2,1,0:T(8,128)(2,1)S(1)}, u32[]{:S(2)}, u32[]{:S(2)}) %collective-permute-start.3) | collective-permute-done | bytes 262176 | tf_op jit(solution)/shard_map/ppermute | solution.py:35
  25.1 5.0 %quarters.3 = bf16[4,256,1280]{2,1,0:T(8,128)(2,1)} custom-call(bf16[8,256,1024]{2,1,0:T(8,128)(2,1)} %weights_ref.2), custom_call_target="tpu_custom_call" | custom-call | bytes 5242880 | tf_op jit(solution)/shard_map/quarters/pallas_call | solution.py:68
  35.0 4.5 %project.1 = (bf16[128,1152]{1,0:T(8,128)(2,1)}, bf16[128,1024]{1,0:T(8,128)(2,1)}) custom-call(s32[3]{0:T(128)} %pad_add_fusion.where_ref, bf16[128,1024]{1,0:T(8,128)(2,1)} %heads_hbm.1, bf16[128,1024]{1,0:T(8,128)(2,1)} %residual_hbm.1, f32[1,1024]{1,0:T(1,128)} %bitcast.68, bf16[32,1024]{1,0:T(8,128)(2,1)} %bitcast.64, s32[8,128]{1,0:T(8,128)} %bitcast.69, ...), custom_call_target="tpu_custom_call" | custom-call | flops 268435456 | bytes 3145728 | tf_op jit(solution)/shard_map/project/pallas_call | solution.py:155
  39.5 1.7 collective-permute-start.11
  46.0 10.2 %collective-permute-done.11.refs_0_ = bf16[128,1152]{1,0:T(8,128)(2,1)S(1)} collective-permute-done((bf16[128,1152]{1,0:T(8,128)(2,1)}, bf16[128,1152]{1,0:T(8,128)(2,1)S(1)}, u32[]{:S(2)}, u32[]{:S(2)}) %collective-permute-start.11) | collective-permute-done | bytes 294944 | tf_op jit(solution)/shard_map/ppermute | solution.py:35
  57.6 3.0 %dynamic-slice_bitcast_fusion = (bf16[256,1280]{1,0:T(8,128)(2,1)S(1)}, bf16[256,1280]{1,0:T(8,128)(2,1)}, bf16[256,1280]{1,0:T(8,128)(2,1)}, bf16[256,1280]{1,0:T(8,128)(2,1)S(1)}) fusion(bf16[4,256,1280]{2,1,0:T(8,128)(2,1)} %quarters.3, s32[]{:T(128)S(6)} %select_n.32, s32[]{:T(128)S(6)} %select_n.31, s32[]{:T(128)S(6)} %select_n.30, s32[]{:T(128)S(6)} %select_n.29), kind=kLoop, calls=%fused_computation | loop fusion | bytes 5242896 | tf_op jit(solution)/shard_map/jit(dynamic_index_in_dim)/squeeze | solution.py:415
  66.9 14.1 %collective-permute-done.17 = bf16[128,1152]{1,0:T(8,128)(2,1)} collective-permute-done((bf16[128,1152]{1,0:T(8,128)(2,1)}, bf16[128,1152]{1,0:T(8,128)(2,1)}, u32[]{:S(2)}, u32[]{:S(2)}) %collective-permute-start.17) | collective-permute-done | bytes 294944 | tf_op jit(solution)/shard_map/ppermute | solution.py:420
  81.0 3.7 %collective-permute-done.18 = bf16[128,1152]{1,0:T(8,128)(2,1)} collective-permute-done((bf16[128,1152]{1,0:T(8,128)(2,1)}, bf16[128,1152]{1,0:T(8,128)(2,1)}, u32[]{:S(2)}, u32[]{:S(2)}) %collective-permute-start.18) | collective-permute-done | bytes 294944 | tf_op jit(solution)/shard_map/ppermute | solution.py:421
  85.2 1.7 collective-permute-start.24
  90.0 1.6 collective-permute-start.26
  92.5 7.7 %slots_block.5.refs_21_ = bf16[512,1024]{1,0:T(8,128)(2,1)} custom-call(s32[3]{0:T(128)} %pad_add_fusion.where_ref, bf16[128,1152]{1,0:T(8,128)(2,1)} %get-tuple-element.76.refs_0_.refs_4_, bf16[128,1152]{1,0:T(8,128)(2,1)} %copy-done.9, bf16[128,1152]{1,0:T(8,128)(2,1)} %copy-done.10, bf16[128,1152]{1,0:T(8,128)(2,1)} %copy-done.11, ...), custom_call_target="tpu_custom_call" | custom-call | flops 2415919104 | bytes 7995392 | tf_op jit(solution)/shard_map/slots_block/pallas_call | solution.py:321
  100.2 5.2 %collective-permute-done.25.refs_1_.refs_5_ = bf16[256,1152]{1,0:T(8,128)(2,1)} collective-permute-done((bf16[256,1152]{1,0:T(8,128)(2,1)}, bf16[256,1152]{1,0:T(8,128)(2,1)}, u32[]{:S(2)}, u32[]{:S(2)}) %collective-permute-start.25) | collective-permute-done | bytes 589856 | tf_op jit(solution)/shard_map/ppermute | solution.py:35
  105.5 11.4 %collective-permute-done.26.refs_2_.refs_6_ = bf16[256,1152]{1,0:T(8,128)(2,1)} collective-permute-done((bf16[256,1152]{1,0:T(8,128)(2,1)}, bf16[256,1152]{1,0:T(8,128)(2,1)}, u32[]{:S(2)}, u32[]{:S(2)}) %collective-permute-start.26) | collective-permute-done | bytes 589856 | tf_op jit(solution)/shard_map/ppermute | solution.py:35
  118.0 1.8 collective-permute-start.29
  119.8 4.4 %collective-permute-start.28 = (bf16[256,1280]{1,0:T(8,128)(2,1)S(1)}, bf16[256,1280]{1,0:T(8,128)(2,1)}, u32[]{:S(2)}, u32[]{:S(2)}) collective-permute-start(bf16[256,1280]{1,0:T(8,128)(2,1)S(1)} %get-tuple-element.104), channel_id=1, source_target_pairs={{0,3},{3,0},{4,7},{7,4},{8,11},{11,8},{12,15},{15,12},{16,19},{19,... | collective-permute-start | bytes 1966088 | tf_op jit(solution)/shard_map/ppermute | solution.py:447
  124.3 10.0 %slots_block.6.refs_20_.refs_21_ = bf16[1024,1024]{1,0:T(8,128)(2,1)} custom-call(s32[3]{0:T(128)} %pad_add_fusion.where_ref, bf16[256,1152]{1,0:T(8,128)(2,1)} %pad_maximum_fusion.refs_0_.refs_4_, bf16[256,1152]{1,0:T(8,128)(2,1)} %collective-permute-done.25.refs_1_.refs_5_, bf16[256,1152]{1,0:T(8,128)(2,1)} %collective-permute-done.26.refs_2_.refs_6_, ...), custom_call_target="tpu_custom_call" | custom-call | flops 4831838208 | bytes 11272192 | tf_op jit(solution)/shard_map/slots_block/pallas_call | solution.py:321
  134.9 7.7 %slots_block.7.refs_20_ = bf16[512,1024]{1,0:T(8,128)(2,1)} custom-call(s32[3]{0:T(128)} %pad_add_fusion.where_ref, bf16[128,1152]{1,0:T(8,128)(2,1)} %copy-done.8, bf16[128,1152]{1,0:T(8,128)(2,1)} %copy-done.12, bf16[128,1152]{1,0:T(8,128)(2,1)} %collective-permute-done.21.refs_2_, bf16[128,1152]{1,0:T(8,128)(2,1)} %collective-permute-done.29.refs_3_, ...), custom_call_target="tpu_custom_call" | custom-call | flops 2415919104 | bytes 7995392 | tf_op jit(solution)/shard_map/slots_block/pallas_call | solution.py:321
  142.8 2.3 %collective-permute-done.34.refs_17_ = bf16[256,1280]{1,0:T(8,128)(2,1)S(1)} collective-permute-done((bf16[256,1280]{1,0:T(8,128)(2,1)}, bf16[256,1280]{1,0:T(8,128)(2,1)S(1)}, u32[]{:S(2)}, u32[]{:S(2)}) %collective-permute-start.34) | collective-permute-done | bytes 655392 | tf_op jit(solution)/shard_map/ppermute | solution.py:35
  145.8 15.2 %slots_block.8 = (bf16[2,2,128,512]{3,2,1,0:T(8,128)(2,1)}, bf16[2,2,128,512]{3,2,1,0:T(8,128)(2,1)}, bf16[2,2,128,512]{3,2,1,0:T(8,128)(2,1)}, bf16[2,2,128,512]{3,2,1,0:T(8,128)(2,1)}) custom-call(s32[3]{0:T(128)} %pad_add_fusion.where_ref, bf16[256,1152]{1,0:T(8,128)(2,1)} %pad_maximum_fusion.refs_0_.refs_4_, ...), custom_call_target="tpu_custom_call" | custom-call | flops 8053063680 | bytes 14417920 | tf_op jit(solution)/shard_map/slots_block/pallas_call | solution.py:321
  162.8 15.4 %slots_block.9 = (bf16[2,2,128,512]{3,2,1,0:T(8,128)(2,1)}, bf16[2,2,128,512]{3,2,1,0:T(8,128)(2,1)}, bf16[2,2,128,512]{3,2,1,0:T(8,128)(2,1)}, bf16[2,2,128,512]{3,2,1,0:T(8,128)(2,1)}) custom-call(s32[3]{0:T(128)} %pad_add_fusion.where_ref, bf16[128,1152]{1,0:T(8,128)(2,1)} %copy-done.8, bf16[128,1152]{1,0:T(8,128)(2,1)} %copy-done.12, ...), custom_call_target="tpu_custom_call" | custom-call | flops 8053063680 | bytes 14417920 | tf_op jit(solution)/shard_map/slots_block/pallas_call | solution.py:321
  181.4 1.5 collective-permute-start.43
  184.6 4.0 %collective-permute-done.42 = bf16[2,128,512]{2,1,0:T(8,128)(2,1)S(1)} collective-permute-done((bf16[2,128,512]{2,1,0:T(8,128)(2,1)S(1)}, bf16[2,128,512]{2,1,0:T(8,128)(2,1)S(1)}, u32[]{:S(2)}, u32[]{:S(2)}) %collective-permute-start.42) | collective-permute-done | bytes 262176 | tf_op jit(solution)/shard_map/ppermute | solution.py:35
  191.9 8.3 %collective-permute-done.37 = bf16[2,2,128,512]{3,2,1,0:T(8,128)(2,1)S(1)} collective-permute-done((bf16[2,2,128,512]{3,2,1,0:T(8,128)(2,1)}, bf16[2,2,128,512]{3,2,1,0:T(8,128)(2,1)S(1)}, u32[]{:S(2)}, u32[]{:S(2)}) %collective-permute-start.37) | collective-permute-done | bytes 524320 | tf_op jit(solution)/shard_map/ppermute | solution.py:35
  201.4 1.7 collective-permute-start.45
  204.2 2.7 %collective-permute-done.38 = bf16[2,128,512]{2,1,0:T(8,128)(2,1)S(1)} collective-permute-done((bf16[2,128,512]{2,1,0:T(8,128)(2,1)S(1)}, bf16[2,128,512]{2,1,0:T(8,128)(2,1)S(1)}, u32[]{:S(2)}, u32[]{:S(2)}) %collective-permute-start.38) | collective-permute-done | bytes 262176 | tf_op jit(solution)/shard_map/ppermute | solution.py:35
  207.0 2.6 %collective-permute-done.40 = bf16[2,128,512]{2,1,0:T(8,128)(2,1)S(1)} collective-permute-done((bf16[2,128,512]{2,1,0:T(8,128)(2,1)S(1)}, bf16[2,128,512]{2,1,0:T(8,128)(2,1)S(1)}, u32[]{:S(2)}, u32[]{:S(2)}) %collective-permute-start.40) | collective-permute-done | bytes 262176 | tf_op jit(solution)/shard_map/ppermute | solution.py:35
  210.0 6.3 %collective-permute-done.41 = bf16[128,1024]{1,0:T(8,128)(2,1)S(1)} collective-permute-done((bf16[128,1024]{1,0:T(8,128)(2,1)S(1)}, bf16[128,1024]{1,0:T(8,128)(2,1)S(1)}, u32[]{:S(2)}, u32[]{:S(2)}) %collective-permute-start.41) | collective-permute-done | bytes 262176 | tf_op jit(solution)/shard_map/ppermute | solution.py:35
  (141 shorter events, 42.4 us)
Async XLA Ops:
  11.5 20.1 %collective-permute-start.6 = (bf16[1024,1024]{1,0:T(8,128)(2,1)}, bf16[1024,1024]{1,0:T(8,128)(2,1)}, u32[]{:S(2)}, u32[]{:S(2)}) collective-permute-start(bf16[1024,1024]{1,0:T(8,128)(2,1)} %bitcast.58), channel_id=1, source_target_pairs={{0,4},{4,0},{8,12},{12,8},{16,20},{20,16},{24,28},{28,24},{1,5},{5... | collective-permute-start | bytes 6291464 | tf_op jit(solution)/shard_map/ppermute | solution.py:35
  11.5 55.4 %all-to-all-start = ((bf16[4,256,768]{2,1,0:T(8,128)(2,1)}), bf16[4,256,768]{2,1,0:T(8,128)(2,1)}, u32[]{:S(2)}, u32[]{:S(2)}) async-start(bf16[4,256,768]{2,1,0:T(8,128)(2,1)} %quarters.2), calls=%async_computation | async-start | bytes 3145728 | tf_op jit(solution)/shard_map/all_to_all | solution.py:396
  15.9 9.2 %collective-permute-start.3 = (bf16[4,32,1024]{2,1,0:T(8,128)(2,1)S(1)}, bf16[4,32,1024]{2,1,0:T(8,128)(2,1)S(1)}, u32[]{:S(2)}, u32[]{:S(2)}) collective-permute-start(bf16[4,32,1024]{2,1,0:T(8,128)(2,1)S(1)} %pad_maximum_fusion.1.refs_0_), channel_id=1, source_target_pairs={{0,8},{4,12},{8,0},{12,4},{16,24},{20,28},{24,16},{28,20},{1,9},{5... | collective-permute-start | bytes 786440 | tf_op jit(solution)/shard_map/ppermute | solution.py:35
  17.5 14.0 %collective-permute-start.4 = (bf16[4,32,1024]{2,1,0:T(8,128)(2,1)S(1)}, bf16[4,32,1024]{2,1,0:T(8,128)(2,1)S(1)}, u32[]{:S(2)}, u32[]{:S(2)}) collective-permute-start(bf16[4,32,1024]{2,1,0:T(8,128)(2,1)S(1)} %pad_maximum_fusion.1.refs_0_), channel_id=1, source_target_pairs={{0,16},{4,20},{8,24},{12,28},{16,0},{20,4},{24,8},{28,12},{1,17},{... | collective-permute-start | bytes 786440 | tf_op jit(solution)/shard_map/ppermute | solution.py:35
  19.0 12.5 %collective-permute-start.5 = (bf16[4,32,1024]{2,1,0:T(8,128)(2,1)S(1)}, bf16[4,32,1024]{2,1,0:T(8,128)(2,1)S(1)}, u32[]{:S(2)}, u32[]{:S(2)}) collective-permute-start(bf16[4,32,1024]{2,1,0:T(8,128)(2,1)S(1)} %pad_maximum_fusion.1.refs_0_), channel_id=1, source_target_pairs={{0,24},{4,28},{8,16},{12,20},{16,8},{20,12},{24,0},{28,4},{1,25},{... | collective-permute-start | bytes 786440 | tf_op jit(solution)/shard_map/ppermute | solution.py:35
  39.5 16.8 %collective-permute-start.11 = (bf16[128,1152]{1,0:T(8,128)(2,1)}, bf16[128,1152]{1,0:T(8,128)(2,1)S(1)}, u32[]{:S(2)}, u32[]{:S(2)}) collective-permute-start(bf16[128,1152]{1,0:T(8,128)(2,1)} %get-tuple-element.76.refs_0_.refs_4_), channel_id=1, source_target_pairs={{0,1},{1,0},{2,3},{3,2},{4,5},{5,4},{6,7},{7,6},{8,9},{9,8},{10,11... | collective-permute-start | bytes 884744 | tf_op jit(solution)/shard_map/ppermute | solution.py:35
  41.2 19.4 %collective-permute-start.12 = (bf16[128,1152]{1,0:T(8,128)(2,1)}, bf16[128,1152]{1,0:T(8,128)(2,1)}, u32[]{:S(2)}, u32[]{:S(2)}) collective-permute-start(bf16[128,1152]{1,0:T(8,128)(2,1)} %get-tuple-element.76.refs_0_.refs_4_), channel_id=1, source_target_pairs={{1,2},{2,1},{5,6},{6,5},{9,10},{10,9},{13,14},{14,13},{17,18},{18,... | collective-permute-start | bytes 884744 | tf_op jit(solution)/shard_map/ppermute | solution.py:413
  42.5 18.0 %collective-permute-start.14 = (bf16[128,1152]{1,0:T(8,128)(2,1)}, bf16[128,1152]{1,0:T(8,128)(2,1)S(1)}, u32[]{:S(2)}, u32[]{:S(2)}) collective-permute-start(bf16[128,1152]{1,0:T(8,128)(2,1)} %get-tuple-element.76.refs_0_.refs_4_), channel_id=1, source_target_pairs={{0,8},{4,12},{8,0},{12,4},{16,24},{20,28},{24,16},{28,20},{1,9},{5... | collective-permute-start | bytes 884744 | tf_op jit(solution)/shard_map/ppermute | solution.py:35
  43.7 16.9 %collective-permute-start.15 = (bf16[128,1152]{1,0:T(8,128)(2,1)}, bf16[128,1152]{1,0:T(8,128)(2,1)S(1)}, u32[]{:S(2)}, u32[]{:S(2)}) collective-permute-start(bf16[128,1152]{1,0:T(8,128)(2,1)} %get-tuple-element.76.refs_0_.refs_4_), channel_id=1, source_target_pairs={{0,16},{4,20},{8,24},{12,28},{16,0},{20,4},{24,8},{28,12},{1,17},{... | collective-permute-start | bytes 884744 | tf_op jit(solution)/shard_map/ppermute | solution.py:35
  44.6 16.0 %collective-permute-start.16 = (bf16[128,1152]{1,0:T(8,128)(2,1)}, bf16[128,1152]{1,0:T(8,128)(2,1)S(1)}, u32[]{:S(2)}, u32[]{:S(2)}) collective-permute-start(bf16[128,1152]{1,0:T(8,128)(2,1)} %get-tuple-element.76.refs_0_.refs_4_), channel_id=1, source_target_pairs={{0,24},{4,28},{8,16},{12,20},{16,8},{20,12},{24,0},{28,4},{1,25},{... | collective-permute-start | bytes 884744 | tf_op jit(solution)/shard_map/ppermute | solution.py:35
  60.7 24.1 %collective-permute-start.19 = (bf16[256,1280]{1,0:T(8,128)(2,1)S(1)}, bf16[256,1280]{1,0:T(8,128)(2,1)}, u32[]{:S(2)}, u32[]{:S(2)}) collective-permute-start(bf16[256,1280]{1,0:T(8,128)(2,1)S(1)} %get-tuple-element.104), channel_id=1, source_target_pairs={{1,2},{2,1},{5,6},{6,5},{9,10},{10,9},{13,14},{14,13},{17,18},{18,... | collective-permute-start | bytes 1966088 | tf_op jit(solution)/shard_map/ppermute | solution.py:422
  62.2 18.8 %collective-permute-start.17 = (bf16[128,1152]{1,0:T(8,128)(2,1)}, bf16[128,1152]{1,0:T(8,128)(2,1)}, u32[]{:S(2)}, u32[]{:S(2)}) collective-permute-start(bf16[128,1152]{1,0:T(8,128)(2,1)} %collective-permute-done.12), channel_id=1, source_target_pairs={{1,0},{2,3},{5,4},{6,7},{9,8},{10,11},{13,12},{14,15},{17,16},{18,... | collective-permute-start | bytes 884744 | tf_op jit(solution)/shard_map/ppermute | solution.py:420
  63.5 21.3 %collective-permute-start.18 = (bf16[128,1152]{1,0:T(8,128)(2,1)}, bf16[128,1152]{1,0:T(8,128)(2,1)}, u32[]{:S(2)}, u32[]{:S(2)}) collective-permute-start(bf16[128,1152]{1,0:T(8,128)(2,1)} %collective-permute-done.13), channel_id=1, source_target_pairs={{1,0},{2,3},{5,4},{6,7},{9,8},{10,11},{13,12},{14,15},{17,16},{18,... | collective-permute-start | bytes 884744 | tf_op jit(solution)/shard_map/ppermute | solution.py:421
  64.8 20.0 %collective-permute-start.20 = (bf16[128,1152]{1,0:T(8,128)(2,1)S(1)}, bf16[128,1152]{1,0:T(8,128)(2,1)S(1)}, u32[]{:S(2)}, u32[]{:S(2)}) collective-permute-start(bf16[128,1152]{1,0:T(8,128)(2,1)S(1)} %collective-permute-done.11.refs_0_), channel_id=1, source_target_pairs={{0,8},{4,12},{8,0},{12,4},{16,24},{20,28},{24,16},{28,20},{1,9},{5... | collective-permute-start | bytes 884744 | tf_op jit(solution)/shard_map/ppermute | solution.py:35
  66.0 18.7 %collective-permute-start.21 = (bf16[128,1152]{1,0:T(8,128)(2,1)S(1)}, bf16[128,1152]{1,0:T(8,128)(2,1)}, u32[]{:S(2)}, u32[]{:S(2)}) collective-permute-start(bf16[128,1152]{1,0:T(8,128)(2,1)S(1)} %collective-permute-done.11.refs_0_), channel_id=1, source_target_pairs={{0,16},{4,20},{8,24},{12,28},{16,0},{20,4},{24,8},{28,12},{1,17},{... | collective-permute-start | bytes 884744 | tf_op jit(solution)/shard_map/ppermute | solution.py:35
  84.8 33.1 %collective-permute-start.23 = (bf16[256,1280]{1,0:T(8,128)(2,1)}, bf16[256,1280]{1,0:T(8,128)(2,1)}, u32[]{:S(2)}, u32[]{:S(2)}) collective-permute-start(bf16[256,1280]{1,0:T(8,128)(2,1)} %get-tuple-element.90), channel_id=1, source_target_pairs={{0,1},{1,0},{2,3},{3,2},{4,5},{5,4},{6,7},{7,6},{8,9},{9,8},{10,11... | collective-permute-start | bytes 1966088 | tf_op jit(solution)/shard_map/ppermute | solution.py:35
  85.2 32.7 %collective-permute-start.24 = (bf16[256,1280]{1,0:T(8,128)(2,1)}, bf16[256,1280]{1,0:T(8,128)(2,1)}, u32[]{:S(2)}, u32[]{:S(2)}) collective-permute-start(bf16[256,1280]{1,0:T(8,128)(2,1)} %get-tuple-element.91), channel_id=1, source_target_pairs={{0,2},{1,3},{2,0},{3,1},{4,6},{5,7},{6,4},{7,5},{8,10},{9,11},{10,... | collective-permute-start | bytes 1966088 | tf_op jit(solution)/shard_map/ppermute | solution.py:35
  89.0 16.5 %collective-permute-start.25 = (bf16[256,1152]{1,0:T(8,128)(2,1)}, bf16[256,1152]{1,0:T(8,128)(2,1)}, u32[]{:S(2)}, u32[]{:S(2)}) collective-permute-start(bf16[256,1152]{1,0:T(8,128)(2,1)} %pad_maximum_fusion.refs_0_.refs_4_), channel_id=1, source_target_pairs={{0,8},{4,12},{8,0},{12,4},{16,24},{20,28},{24,16},{28,20},{1,9},{5... | collective-permute-start | bytes 1769480 | tf_op jit(solution)/shard_map/ppermute | solution.py:35
  90.0 26.9 %collective-permute-start.26 = (bf16[256,1152]{1,0:T(8,128)(2,1)}, bf16[256,1152]{1,0:T(8,128)(2,1)}, u32[]{:S(2)}, u32[]{:S(2)}) collective-permute-start(bf16[256,1152]{1,0:T(8,128)(2,1)} %pad_maximum_fusion.refs_0_.refs_4_), channel_id=1, source_target_pairs={{0,16},{4,20},{8,24},{12,28},{16,0},{20,4},{24,8},{28,12},{1,17},{... | collective-permute-start | bytes 1769480 | tf_op jit(solution)/shard_map/ppermute | solution.py:35
  91.6 26.4 %collective-permute-start.27 = (bf16[256,1152]{1,0:T(8,128)(2,1)}, bf16[256,1152]{1,0:T(8,128)(2,1)}, u32[]{:S(2)}, u32[]{:S(2)}) collective-permute-start(bf16[256,1152]{1,0:T(8,128)(2,1)} %pad_maximum_fusion.refs_0_.refs_4_), channel_id=1, source_target_pairs={{0,24},{4,28},{8,16},{12,20},{16,8},{20,12},{24,0},{28,4},{1,25},{... | collective-permute-start | bytes 1769480 | tf_op jit(solution)/shard_map/ppermute | solution.py:35
  105.5 37.2 %collective-permute-start.30 = (bf16[256,1280]{1,0:T(8,128)(2,1)S(1)}, bf16[256,1280]{1,0:T(8,128)(2,1)}, u32[]{:S(2)}, u32[]{:S(2)}) collective-permute-start(bf16[256,1280]{1,0:T(8,128)(2,1)S(1)} %get-tuple-element.100.refs_8_), channel_id=1, source_target_pairs={{0,4},{4,0},{8,12},{12,8},{16,20},{20,16},{24,28},{28,24},{1,5},{5... | collective-permute-start | bytes 1966088 | tf_op jit(solution)/shard_map/ppermute | solution.py:35
  116.9 25.9 %collective-permute-start.33 = (bf16[256,1280]{1,0:T(8,128)(2,1)}, bf16[256,1280]{1,0:T(8,128)(2,1)}, u32[]{:S(2)}, u32[]{:S(2)}) collective-permute-start(bf16[256,1280]{1,0:T(8,128)(2,1)} %collective-permute-done.19.refs_11_), channel_id=1, source_target_pairs={{0,4},{4,0},{8,12},{12,8},{16,20},{20,16},{24,28},{28,24},{1,5},{5... | collective-permute-start | bytes 1966088 | tf_op jit(solution)/shard_map/ppermute | solution.py:35
  118.0 16.4 %collective-permute-start.29 = (bf16[128,1152]{1,0:T(8,128)(2,1)}, bf16[128,1152]{1,0:T(8,128)(2,1)}, u32[]{:S(2)}, u32[]{:S(2)}) collective-permute-start(bf16[128,1152]{1,0:T(8,128)(2,1)} %copy-done.8), channel_id=1, source_target_pairs={{0,24},{4,28},{8,16},{12,20},{16,8},{20,12},{24,0},{28,4},{1,25},{... | collective-permute-start | bytes 884744 | tf_op jit(solution)/shard_map/ppermute | solution.py:35
  119.8 22.8 %collective-permute-start.28 = (bf16[256,1280]{1,0:T(8,128)(2,1)S(1)}, bf16[256,1280]{1,0:T(8,128)(2,1)}, u32[]{:S(2)}, u32[]{:S(2)}) collective-permute-start(bf16[256,1280]{1,0:T(8,128)(2,1)S(1)} %get-tuple-element.104), channel_id=1, source_target_pairs={{0,3},{3,0},{4,7},{7,4},{8,11},{11,8},{12,15},{15,12},{16,19},{19,... | collective-permute-start | bytes 1966088 | tf_op jit(solution)/shard_map/ppermute | solution.py:447
  124.2 18.5 %collective-permute-start.31 = (bf16[256,1280]{1,0:T(8,128)(2,1)}, bf16[256,1280]{1,0:T(8,128)(2,1)}, u32[]{:S(2)}, u32[]{:S(2)}) collective-permute-start(bf16[256,1280]{1,0:T(8,128)(2,1)} %collective-permute-done.23.refs_9_), channel_id=1, source_target_pairs={{0,4},{4,0},{8,12},{12,8},{16,20},{20,16},{24,28},{28,24},{1,5},{5... | collective-permute-start | bytes 1966088 | tf_op jit(solution)/shard_map/ppermute | solution.py:35
  161.1 17.2 %collective-permute-start.35 = (bf16[2,2,128,512]{3,2,1,0:T(8,128)(2,1)}, bf16[2,2,128,512]{3,2,1,0:T(8,128)(2,1)}, u32[]{:S(2)}, u32[]{:S(2)}) collective-permute-start(bf16[2,2,128,512]{3,2,1,0:T(8,128)(2,1)} %get-tuple-element.110), channel_id=1, source_target_pairs={{0,8},{4,12},{8,0},{12,4},{16,24},{20,28},{24,16},{28,20},{1,9},{5... | collective-permute-start | bytes 1572872 | tf_op jit(solution)/shard_map/ppermute | solution.py:35
  161.7 16.6 %collective-permute-start.36 = (bf16[2,2,128,512]{3,2,1,0:T(8,128)(2,1)}, bf16[2,2,128,512]{3,2,1,0:T(8,128)(2,1)}, u32[]{:S(2)}, u32[]{:S(2)}) collective-permute-start(bf16[2,2,128,512]{3,2,1,0:T(8,128)(2,1)} %get-tuple-element.111), channel_id=1, source_target_pairs={{0,16},{4,20},{8,24},{12,28},{16,0},{20,4},{24,8},{28,12},{1,17},{... | collective-permute-start | bytes 1572872 | tf_op jit(solution)/shard_map/ppermute | solution.py:35
  179.3 9.3 %collective-permute-start.42 = (bf16[2,128,512]{2,1,0:T(8,128)(2,1)S(1)}, bf16[2,128,512]{2,1,0:T(8,128)(2,1)S(1)}, u32[]{:S(2)}, u32[]{:S(2)}) collective-permute-start(bf16[2,128,512]{2,1,0:T(8,128)(2,1)S(1)} %fusion.7), channel_id=1, source_target_pairs={{0,16},{4,20},{8,24},{12,28},{16,0},{20,4},{24,8},{28,12},{1,17},{... | collective-permute-start | bytes 786440 | tf_op jit(solution)/shard_map/ppermute | solution.py:35
  181.4 9.3 %collective-permute-start.43 = (bf16[2,128,512]{2,1,0:T(8,128)(2,1)S(1)}, bf16[2,128,512]{2,1,0:T(8,128)(2,1)S(1)}, u32[]{:S(2)}, u32[]{:S(2)}) collective-permute-start(bf16[2,128,512]{2,1,0:T(8,128)(2,1)S(1)} %fusion.8), channel_id=1, source_target_pairs={{0,8},{4,12},{8,0},{12,4},{16,24},{20,28},{24,16},{28,20},{1,9},{5... | collective-permute-start | bytes 786440 | tf_op jit(solution)/shard_map/ppermute | solution.py:35
  182.9 17.3 %collective-permute-start.37 = (bf16[2,2,128,512]{3,2,1,0:T(8,128)(2,1)}, bf16[2,2,128,512]{3,2,1,0:T(8,128)(2,1)S(1)}, u32[]{:S(2)}, u32[]{:S(2)}) collective-permute-start(bf16[2,2,128,512]{3,2,1,0:T(8,128)(2,1)} %get-tuple-element.121), channel_id=1, source_target_pairs={{0,8},{4,12},{8,0},{12,4},{16,24},{20,28},{24,16},{28,20},{1,9},{5... | collective-permute-start | bytes 1572872 | tf_op jit(solution)/shard_map/ppermute | solution.py:35
  183.5 19.7 %collective-permute-start.39 = (bf16[2,2,128,512]{3,2,1,0:T(8,128)(2,1)}, bf16[2,2,128,512]{3,2,1,0:T(8,128)(2,1)S(1)}, u32[]{:S(2)}, u32[]{:S(2)}) collective-permute-start(bf16[2,2,128,512]{3,2,1,0:T(8,128)(2,1)} %get-tuple-element.123), channel_id=1, source_target_pairs={{0,16},{4,20},{8,24},{12,28},{16,0},{20,4},{24,8},{28,12},{1,17},{... | collective-permute-start | bytes 1572872 | tf_op jit(solution)/shard_map/ppermute | solution.py:35
  191.8 18.1 %collective-permute-start.44 = (bf16[128,1024]{1,0:T(8,128)(2,1)S(1)}, bf16[128,1024]{1,0:T(8,128)(2,1)S(1)}, u32[]{:S(2)}, u32[]{:S(2)}) collective-permute-start(bf16[128,1024]{1,0:T(8,128)(2,1)S(1)} %pad_maximum_fusion.3), channel_id=1, source_target_pairs={{0,2},{1,3},{2,0},{3,1},{4,6},{5,7},{6,4},{7,5},{8,10},{9,11},{10,... | collective-permute-start | bytes 786440 | tf_op jit(solution)/shard_map/ppermute | solution.py:35
  (37 other events, 358.8 us)

commit v6 on v5

--- a/solution.py
+++ b/solution.py
@@ -395,7 +395,7 @@
     def exchange(send):
         return lax.all_to_all(send, "shard", split_axis=0, concat_axis=0, tiled=True)
 
-    over_z, send = stage(over_z, sends[0])
+    over_z, send, where = stage(over_z, sends[0], where)
     weights = [exchange(send)]
     down = placed_down.reshape(slots * units, width)
     pieces = chip_gather(over_z)

time: 218 us -> 219 us (level)
  transfers between devices with their start and end apart: 47 -> 47, of which waited for: 20 -> 21; matrix products, arithmetic and copies ran while one was open for 4% -> 4% of each run, Pallas kernels for 25% -> 25%
where the time goes in v6:
time: 219 us
  waiting for transfers between devices  83.4 us (38%)
  Pallas kernels  69.1 us (32%)
  starting transfers between devices  51.5 us (24%)
  other arithmetic  8.39 us (4%)
  local copies, waits for them, and re-layouts  5.78 us (3%)
    ppermute x40, waiting for transfers between devices, swap(): return lax.ppermute(value, axis, [(i, i ^ bits) for i in range(size)])  65.4 us
    pallas_call x5, Pallas kernels, slots_block(): pl.pallas_call(functools.partial(slots_kernel, slot_sets, group_slots, bl...  56.1 us
    ppermute x40, starting transfers between devices, swap(): return lax.ppermute(value, axis, [(i, i ^ bits) for i in range(size)])  35.9 us
    ppermute x1, waiting for transfers between devices, quarter_body(): first_out = lax.ppermute(first_in, 'shard', outward)  14.2 us
    pallas_call x2, Pallas kernels, quarters(): pl.pallas_call(quarters_kernel, out_shape=jax.ShapeDtypeStruct((shards, d...  8.52 us
    pallas_call x1, Pallas kernels, project(): pl.pallas_call(project_kernel, out_shape=(jax.ShapeDtypeStruct((rows, wid...  4.51 us
    ppermute x1, starting transfers between devices, quarter_body(): part_out = lax.ppermute(parts[3], 'shard', [(0, 3), (3, 0)])  4.4 us
  transfers between devices with their start and end apart: 47, of which 21 were waited for; matrix products, arithmetic and copies ran while one was open for 4% of the time, Pallas kernels for 25%

profile of v6, /device:TPU:0, one launch (start us, length us, event | category | flops | bytes accessed | tf_op | source)
XLA Modules:
  0.0 218.7 jit_solution(13746732419864582770)
XLA Ops:
  1.0 3.0 %collective-permute-start = (bf16[32,1024]{1,0:T(8,128)(2,1)S(1)}, bf16[32,1024]{1,0:T(8,128)(2,1)S(1)}, u32[]{:S(2)}, u32[]{:S(2)}) collective-permute-start(bf16[32,1024]{1,0:T(8,128)(2,1)S(1)} %constant_dynamic-slice_fusion), channel_id=1, source_target_pairs={{0,1},{1,0},{2,3},{3,2},{4,5},{5,4},{6,7},{7,6},{8,9},{9,8},{10,11... | collective-permute-start | bytes 196616 | tf_op jit(solution)/shard_map/ppermute | solution.py:35
  4.1 2.6 %collective-permute-start.1 = (bf16[32,1024]{1,0:T(8,128)(2,1)S(1)}, bf16[32,1024]{1,0:T(8,128)(2,1)S(1)}, u32[]{:S(2)}, u32[]{:S(2)}) collective-permute-start(bf16[32,1024]{1,0:T(8,128)(2,1)S(1)} %constant_dynamic-slice_fusion), channel_id=1, source_target_pairs={{0,2},{1,3},{2,0},{3,1},{4,6},{5,7},{6,4},{7,5},{8,10},{9,11},{10,... | collective-permute-start | bytes 196616 | tf_op jit(solution)/shard_map/ppermute | solution.py:35
  6.7 3.6 %quarters.2 = bf16[4,256,768]{2,1,0:T(8,128)(2,1)} custom-call(bf16[8,256,1024]{2,1,0:T(8,128)(2,1)} %weights_ref.2), custom_call_target="tpu_custom_call" | custom-call | bytes 3145728 | tf_op jit(solution)/shard_map/quarters/pallas_call | solution.py:68
  12.9 4.4 %all-to-all-start = ((bf16[4,256,768]{2,1,0:T(8,128)(2,1)}), bf16[4,256,768]{2,1,0:T(8,128)(2,1)}, u32[]{:S(2)}, u32[]{:S(2)}) async-start(bf16[4,256,768]{2,1,0:T(8,128)(2,1)} %quarters.2), calls=%async_computation | async-start | bytes 3145728 | tf_op jit(solution)/shard_map/all_to_all | solution.py:396
  17.2 1.6 collective-permute-start.3
  18.8 1.5 collective-permute-start.4
  20.8 5.6 %collective-permute-done.3.refs_1_ = bf16[4,32,1024]{2,1,0:T(8,128)(2,1)S(1)} collective-permute-done((bf16[4,32,1024]{2,1,0:T(8,128)(2,1)S(1)}, bf16[4,32,1024]{2,1,0:T(8,128)(2,1)S(1)}, u32[]{:S(2)}, u32[]{:S(2)}) %collective-permute-start.3) | collective-permute-done | bytes 262176 | tf_op jit(solution)/shard_map/ppermute | solution.py:35
  26.4 5.0 %quarters.3 = bf16[4,256,1280]{2,1,0:T(8,128)(2,1)} custom-call(bf16[8,256,1024]{2,1,0:T(8,128)(2,1)} %weights_ref.2), custom_call_target="tpu_custom_call" | custom-call | bytes 5242880 | tf_op jit(solution)/shard_map/quarters/pallas_call | solution.py:68
  36.3 4.5 %project.1 = (bf16[128,1152]{1,0:T(8,128)(2,1)}, bf16[128,1024]{1,0:T(8,128)(2,1)}) custom-call(s32[3]{0:T(128)} %pad_add_fusion.where_ref, bf16[128,1024]{1,0:T(8,128)(2,1)} %heads_hbm.1, bf16[128,1024]{1,0:T(8,128)(2,1)} %residual_hbm.1, f32[1,1024]{1,0:T(1,128)} %bitcast.68, bf16[32,1024]{1,0:T(8,128)(2,1)} %bitcast.64, s32[8,128]{1,0:T(8,128)} %bitcast.69, ...), custom_call_target="tpu_custom_call" | custom-call | flops 268435456 | bytes 3145728 | tf_op jit(solution)/shard_map/project/pallas_call | solution.py:155
  40.8 1.7 collective-permute-start.11
  47.4 10.1 %collective-permute-done.11.refs_0_ = bf16[128,1152]{1,0:T(8,128)(2,1)S(1)} collective-permute-done((bf16[128,1152]{1,0:T(8,128)(2,1)}, bf16[128,1152]{1,0:T(8,128)(2,1)S(1)}, u32[]{:S(2)}, u32[]{:S(2)}) %collective-permute-start.11) | collective-permute-done | bytes 294944 | tf_op jit(solution)/shard_map/ppermute | solution.py:35
  58.9 3.0 %dynamic-slice_bitcast_fusion = (bf16[256,1280]{1,0:T(8,128)(2,1)S(1)}, bf16[256,1280]{1,0:T(8,128)(2,1)}, bf16[256,1280]{1,0:T(8,128)(2,1)}, bf16[256,1280]{1,0:T(8,128)(2,1)S(1)}) fusion(bf16[4,256,1280]{2,1,0:T(8,128)(2,1)} %quarters.3, s32[]{:T(128)S(6)} %select_n.32, s32[]{:T(128)S(6)} %select_n.31, s32[]{:T(128)S(6)} %select_n.30, s32[]{:T(128)S(6)} %select_n.29), kind=kLoop, calls=%fused_computation | loop fusion | bytes 5242896 | tf_op jit(solution)/shard_map/jit(dynamic_index_in_dim)/squeeze | solution.py:415
  68.2 14.2 %collective-permute-done.17 = bf16[128,1152]{1,0:T(8,128)(2,1)} collective-permute-done((bf16[128,1152]{1,0:T(8,128)(2,1)}, bf16[128,1152]{1,0:T(8,128)(2,1)}, u32[]{:S(2)}, u32[]{:S(2)}) %collective-permute-start.17) | collective-permute-done | bytes 294944 | tf_op jit(solution)/shard_map/ppermute | solution.py:420
  82.3 3.8 %collective-permute-done.18 = bf16[128,1152]{1,0:T(8,128)(2,1)} collective-permute-done((bf16[128,1152]{1,0:T(8,128)(2,1)}, bf16[128,1152]{1,0:T(8,128)(2,1)}, u32[]{:S(2)}, u32[]{:S(2)}) %collective-permute-start.18) | collective-permute-done | bytes 294944 | tf_op jit(solution)/shard_map/ppermute | solution.py:421
  86.6 1.7 collective-permute-start.24
  93.9 7.7 %slots_block.5.refs_21_ = bf16[512,1024]{1,0:T(8,128)(2,1)} custom-call(s32[3]{0:T(128)} %pad_add_fusion.where_ref, bf16[128,1152]{1,0:T(8,128)(2,1)} %get-tuple-element.78.refs_0_.refs_4_, bf16[128,1152]{1,0:T(8,128)(2,1)} %copy-done.9, bf16[128,1152]{1,0:T(8,128)(2,1)} %copy-done.10, bf16[128,1152]{1,0:T(8,128)(2,1)} %copy-done.11, ...), custom_call_target="tpu_custom_call" | custom-call | flops 2415919104 | bytes 7995392 | tf_op jit(solution)/shard_map/slots_block/pallas_call | solution.py:321
  101.6 5.2 %collective-permute-done.25.refs_1_.refs_5_ = bf16[256,1152]{1,0:T(8,128)(2,1)} collective-permute-done((bf16[256,1152]{1,0:T(8,128)(2,1)}, bf16[256,1152]{1,0:T(8,128)(2,1)}, u32[]{:S(2)}, u32[]{:S(2)}) %collective-permute-start.25) | collective-permute-done | bytes 589856 | tf_op jit(solution)/shard_map/ppermute | solution.py:35
  106.8 11.3 %collective-permute-done.26.refs_2_.refs_6_ = bf16[256,1152]{1,0:T(8,128)(2,1)} collective-permute-done((bf16[256,1152]{1,0:T(8,128)(2,1)}, bf16[256,1152]{1,0:T(8,128)(2,1)}, u32[]{:S(2)}, u32[]{:S(2)}) %collective-permute-start.26) | collective-permute-done | bytes 589856 | tf_op jit(solution)/shard_map/ppermute | solution.py:35
  119.3 1.8 collective-permute-start.29
  121.2 4.4 %collective-permute-start.28 = (bf16[256,1280]{1,0:T(8,128)(2,1)S(1)}, bf16[256,1280]{1,0:T(8,128)(2,1)}, u32[]{:S(2)}, u32[]{:S(2)}) collective-permute-start(bf16[256,1280]{1,0:T(8,128)(2,1)S(1)} %get-tuple-element.106), channel_id=1, source_target_pairs={{0,3},{3,0},{4,7},{7,4},{8,11},{11,8},{12,15},{15,12},{16,19},{19,... | collective-permute-start | bytes 1966088 | tf_op jit(solution)/shard_map/ppermute | solution.py:447
  125.7 10.0 %slots_block.6.refs_20_.refs_21_ = bf16[1024,1024]{1,0:T(8,128)(2,1)} custom-call(s32[3]{0:T(128)} %pad_add_fusion.where_ref, bf16[256,1152]{1,0:T(8,128)(2,1)} %pad_maximum_fusion.refs_0_.refs_4_, bf16[256,1152]{1,0:T(8,128)(2,1)} %collective-permute-done.25.refs_1_.refs_5_, bf16[256,1152]{1,0:T(8,128)(2,1)} %collective-permute-done.26.refs_2_.refs_6_, ...), custom_call_target="tpu_custom_call" | custom-call | flops 4831838208 | bytes 11272192 | tf_op jit(solution)/shard_map/slots_block/pallas_call | solution.py:321
  136.3 7.7 %slots_block.7.refs_20_ = bf16[512,1024]{1,0:T(8,128)(2,1)} custom-call(s32[3]{0:T(128)} %pad_add_fusion.where_ref, bf16[128,1152]{1,0:T(8,128)(2,1)} %copy-done.8, bf16[128,1152]{1,0:T(8,128)(2,1)} %copy-done.12, bf16[128,1152]{1,0:T(8,128)(2,1)} %collective-permute-done.21.refs_2_, bf16[128,1152]{1,0:T(8,128)(2,1)} %collective-permute-done.29.refs_3_, ...), custom_call_target="tpu_custom_call" | custom-call | flops 2415919104 | bytes 7995392 | tf_op jit(solution)/shard_map/slots_block/pallas_call | solution.py:321
  144.1 2.3 %collective-permute-done.34.refs_17_ = bf16[256,1280]{1,0:T(8,128)(2,1)S(1)} collective-permute-done((bf16[256,1280]{1,0:T(8,128)(2,1)}, bf16[256,1280]{1,0:T(8,128)(2,1)S(1)}, u32[]{:S(2)}, u32[]{:S(2)}) %collective-permute-start.34) | collective-permute-done | bytes 655392 | tf_op jit(solution)/shard_map/ppermute | solution.py:35
  147.2 15.2 %slots_block.8 = (bf16[2,2,128,512]{3,2,1,0:T(8,128)(2,1)}, bf16[2,2,128,512]{3,2,1,0:T(8,128)(2,1)}, bf16[2,2,128,512]{3,2,1,0:T(8,128)(2,1)}, bf16[2,2,128,512]{3,2,1,0:T(8,128)(2,1)}) custom-call(s32[3]{0:T(128)} %pad_add_fusion.where_ref, bf16[256,1152]{1,0:T(8,128)(2,1)} %pad_maximum_fusion.refs_0_.refs_4_, ...), custom_call_target="tpu_custom_call" | custom-call | flops 8053063680 | bytes 14417920 | tf_op jit(solution)/shard_map/slots_block/pallas_call | solution.py:321
  164.2 15.4 %slots_block.9 = (bf16[2,2,128,512]{3,2,1,0:T(8,128)(2,1)}, bf16[2,2,128,512]{3,2,1,0:T(8,128)(2,1)}, bf16[2,2,128,512]{3,2,1,0:T(8,128)(2,1)}, bf16[2,2,128,512]{3,2,1,0:T(8,128)(2,1)}) custom-call(s32[3]{0:T(128)} %pad_add_fusion.where_ref, bf16[128,1152]{1,0:T(8,128)(2,1)} %copy-done.8, bf16[128,1152]{1,0:T(8,128)(2,1)} %copy-done.12, ...), custom_call_target="tpu_custom_call" | custom-call | flops 8053063680 | bytes 14417920 | tf_op jit(solution)/shard_map/slots_block/pallas_call | solution.py:321
  182.7 1.5 collective-permute-start.43
  185.9 4.0 %collective-permute-done.42 = bf16[2,128,512]{2,1,0:T(8,128)(2,1)S(1)} collective-permute-done((bf16[2,128,512]{2,1,0:T(8,128)(2,1)S(1)}, bf16[2,128,512]{2,1,0:T(8,128)(2,1)S(1)}, u32[]{:S(2)}, u32[]{:S(2)}) %collective-permute-start.42) | collective-permute-done | bytes 262176 | tf_op jit(solution)/shard_map/ppermute | solution.py:35
  193.3 8.3 %collective-permute-done.37 = bf16[2,2,128,512]{3,2,1,0:T(8,128)(2,1)S(1)} collective-permute-done((bf16[2,2,128,512]{3,2,1,0:T(8,128)(2,1)}, bf16[2,2,128,512]{3,2,1,0:T(8,128)(2,1)S(1)}, u32[]{:S(2)}, u32[]{:S(2)}) %collective-permute-start.37) | collective-permute-done | bytes 524320 | tf_op jit(solution)/shard_map/ppermute | solution.py:35
  202.8 1.6 collective-permute-start.45
  205.6 2.6 %collective-permute-done.38 = bf16[2,128,512]{2,1,0:T(8,128)(2,1)S(1)} collective-permute-done((bf16[2,128,512]{2,1,0:T(8,128)(2,1)S(1)}, bf16[2,128,512]{2,1,0:T(8,128)(2,1)S(1)}, u32[]{:S(2)}, u32[]{:S(2)}) %collective-permute-start.38) | collective-permute-done | bytes 262176 | tf_op jit(solution)/shard_map/ppermute | solution.py:35
  208.4 2.5 %collective-permute-done.40 = bf16[2,128,512]{2,1,0:T(8,128)(2,1)S(1)} collective-permute-done((bf16[2,128,512]{2,1,0:T(8,128)(2,1)S(1)}, bf16[2,128,512]{2,1,0:T(8,128)(2,1)S(1)}, u32[]{:S(2)}, u32[]{:S(2)}) %collective-permute-start.40) | collective-permute-done | bytes 262176 | tf_op jit(solution)/shard_map/ppermute | solution.py:35
  211.2 6.3 %collective-permute-done.41 = bf16[128,1024]{1,0:T(8,128)(2,1)S(1)} collective-permute-done((bf16[128,1024]{1,0:T(8,128)(2,1)S(1)}, bf16[128,1024]{1,0:T(8,128)(2,1)S(1)}, u32[]{:S(2)}, u32[]{:S(2)}) %collective-permute-start.41) | collective-permute-done | bytes 262176 | tf_op jit(solution)/shard_map/ppermute | solution.py:35
  (141 shorter events, 44.1 us)
Async XLA Ops:
  1.0 9.8 %collective-permute-start = (bf16[32,1024]{1,0:T(8,128)(2,1)S(1)}, bf16[32,1024]{1,0:T(8,128)(2,1)S(1)}, u32[]{:S(2)}, u32[]{:S(2)}) collective-permute-start(bf16[32,1024]{1,0:T(8,128)(2,1)S(1)} %constant_dynamic-slice_fusion), channel_id=1, source_target_pairs={{0,1},{1,0},{2,3},{3,2},{4,5},{5,4},{6,7},{7,6},{8,9},{9,8},{10,11... | collective-permute-start | bytes 196616 | tf_op jit(solution)/shard_map/ppermute | solution.py:35
  12.8 20.1 %collective-permute-start.6 = (bf16[1024,1024]{1,0:T(8,128)(2,1)}, bf16[1024,1024]{1,0:T(8,128)(2,1)}, u32[]{:S(2)}, u32[]{:S(2)}) collective-permute-start(bf16[1024,1024]{1,0:T(8,128)(2,1)} %bitcast.58), channel_id=1, source_target_pairs={{0,4},{4,0},{8,12},{12,8},{16,20},{20,16},{24,28},{28,24},{1,5},{5... | collective-permute-start | bytes 6291464 | tf_op jit(solution)/shard_map/ppermute | solution.py:35
  12.9 55.3 %all-to-all-start = ((bf16[4,256,768]{2,1,0:T(8,128)(2,1)}), bf16[4,256,768]{2,1,0:T(8,128)(2,1)}, u32[]{:S(2)}, u32[]{:S(2)}) async-start(bf16[4,256,768]{2,1,0:T(8,128)(2,1)} %quarters.2), calls=%async_computation | async-start | bytes 3145728 | tf_op jit(solution)/shard_map/all_to_all | solution.py:396
  18.8 14.0 %collective-permute-start.4 = (bf16[4,32,1024]{2,1,0:T(8,128)(2,1)S(1)}, bf16[4,32,1024]{2,1,0:T(8,128)(2,1)S(1)}, u32[]{:S(2)}, u32[]{:S(2)}) collective-permute-start(bf16[4,32,1024]{2,1,0:T(8,128)(2,1)S(1)} %pad_maximum_fusion.1.refs_0_), channel_id=1, source_target_pairs={{0,16},{4,20},{8,24},{12,28},{16,0},{20,4},{24,8},{28,12},{1,17},{... | collective-permute-start | bytes 786440 | tf_op jit(solution)/shard_map/ppermute | solution.py:35
  20.3 12.5 %collective-permute-start.5 = (bf16[4,32,1024]{2,1,0:T(8,128)(2,1)S(1)}, bf16[4,32,1024]{2,1,0:T(8,128)(2,1)S(1)}, u32[]{:S(2)}, u32[]{:S(2)}) collective-permute-start(bf16[4,32,1024]{2,1,0:T(8,128)(2,1)S(1)} %pad_maximum_fusion.1.refs_0_), channel_id=1, source_target_pairs={{0,24},{4,28},{8,16},{12,20},{16,8},{20,12},{24,0},{28,4},{1,25},{... | collective-permute-start | bytes 786440 | tf_op jit(solution)/shard_map/ppermute | solution.py:35
  40.8 16.7 %collective-permute-start.11 = (bf16[128,1152]{1,0:T(8,128)(2,1)}, bf16[128,1152]{1,0:T(8,128)(2,1)S(1)}, u32[]{:S(2)}, u32[]{:S(2)}) collective-permute-start(bf16[128,1152]{1,0:T(8,128)(2,1)} %get-tuple-element.78.refs_0_.refs_4_), channel_id=1, source_target_pairs={{0,1},{1,0},{2,3},{3,2},{4,5},{5,4},{6,7},{7,6},{8,9},{9,8},{10,11... | collective-permute-start | bytes 884744 | tf_op jit(solution)/shard_map/ppermute | solution.py:35
  42.5 19.4 %collective-permute-start.12 = (bf16[128,1152]{1,0:T(8,128)(2,1)}, bf16[128,1152]{1,0:T(8,128)(2,1)}, u32[]{:S(2)}, u32[]{:S(2)}) collective-permute-start(bf16[128,1152]{1,0:T(8,128)(2,1)} %get-tuple-element.78.refs_0_.refs_4_), channel_id=1, source_target_pairs={{1,2},{2,1},{5,6},{6,5},{9,10},{10,9},{13,14},{14,13},{17,18},{18,... | collective-permute-start | bytes 884744 | tf_op jit(solution)/shard_map/ppermute | solution.py:413
  43.9 18.0 %collective-permute-start.14 = (bf16[128,1152]{1,0:T(8,128)(2,1)}, bf16[128,1152]{1,0:T(8,128)(2,1)S(1)}, u32[]{:S(2)}, u32[]{:S(2)}) collective-permute-start(bf16[128,1152]{1,0:T(8,128)(2,1)} %get-tuple-element.78.refs_0_.refs_4_), channel_id=1, source_target_pairs={{0,8},{4,12},{8,0},{12,4},{16,24},{20,28},{24,16},{28,20},{1,9},{5... | collective-permute-start | bytes 884744 | tf_op jit(solution)/shard_map/ppermute | solution.py:35
  45.1 16.8 %collective-permute-start.15 = (bf16[128,1152]{1,0:T(8,128)(2,1)}, bf16[128,1152]{1,0:T(8,128)(2,1)S(1)}, u32[]{:S(2)}, u32[]{:S(2)}) collective-permute-start(bf16[128,1152]{1,0:T(8,128)(2,1)} %get-tuple-element.78.refs_0_.refs_4_), channel_id=1, source_target_pairs={{0,16},{4,20},{8,24},{12,28},{16,0},{20,4},{24,8},{28,12},{1,17},{... | collective-permute-start | bytes 884744 | tf_op jit(solution)/shard_map/ppermute | solution.py:35
  45.9 16.0 %collective-permute-start.16 = (bf16[128,1152]{1,0:T(8,128)(2,1)}, bf16[128,1152]{1,0:T(8,128)(2,1)S(1)}, u32[]{:S(2)}, u32[]{:S(2)}) collective-permute-start(bf16[128,1152]{1,0:T(8,128)(2,1)} %get-tuple-element.78.refs_0_.refs_4_), channel_id=1, source_target_pairs={{0,24},{4,28},{8,16},{12,20},{16,8},{20,12},{24,0},{28,4},{1,25},{... | collective-permute-start | bytes 884744 | tf_op jit(solution)/shard_map/ppermute | solution.py:35
  61.9 24.2 %collective-permute-start.19 = (bf16[256,1280]{1,0:T(8,128)(2,1)S(1)}, bf16[256,1280]{1,0:T(8,128)(2,1)}, u32[]{:S(2)}, u32[]{:S(2)}) collective-permute-start(bf16[256,1280]{1,0:T(8,128)(2,1)S(1)} %get-tuple-element.106), channel_id=1, source_target_pairs={{1,2},{2,1},{5,6},{6,5},{9,10},{10,9},{13,14},{14,13},{17,18},{18,... | collective-permute-start | bytes 1966088 | tf_op jit(solution)/shard_map/ppermute | solution.py:422
  63.5 18.9 %collective-permute-start.17 = (bf16[128,1152]{1,0:T(8,128)(2,1)}, bf16[128,1152]{1,0:T(8,128)(2,1)}, u32[]{:S(2)}, u32[]{:S(2)}) collective-permute-start(bf16[128,1152]{1,0:T(8,128)(2,1)} %collective-permute-done.12), channel_id=1, source_target_pairs={{1,0},{2,3},{5,4},{6,7},{9,8},{10,11},{13,12},{14,15},{17,16},{18,... | collective-permute-start | bytes 884744 | tf_op jit(solution)/shard_map/ppermute | solution.py:420
  64.8 21.3 %collective-permute-start.18 = (bf16[128,1152]{1,0:T(8,128)(2,1)}, bf16[128,1152]{1,0:T(8,128)(2,1)}, u32[]{:S(2)}, u32[]{:S(2)}) collective-permute-start(bf16[128,1152]{1,0:T(8,128)(2,1)} %collective-permute-done.13), channel_id=1, source_target_pairs={{1,0},{2,3},{5,4},{6,7},{9,8},{10,11},{13,12},{14,15},{17,16},{18,... | collective-permute-start | bytes 884744 | tf_op jit(solution)/shard_map/ppermute | solution.py:421
  66.1 20.0 %collective-permute-start.20 = (bf16[128,1152]{1,0:T(8,128)(2,1)S(1)}, bf16[128,1152]{1,0:T(8,128)(2,1)S(1)}, u32[]{:S(2)}, u32[]{:S(2)}) collective-permute-start(bf16[128,1152]{1,0:T(8,128)(2,1)S(1)} %collective-permute-done.11.refs_0_), channel_id=1, source_target_pairs={{0,8},{4,12},{8,0},{12,4},{16,24},{20,28},{24,16},{28,20},{1,9},{5... | collective-permute-start | bytes 884744 | tf_op jit(solution)/shard_map/ppermute | solution.py:35
  67.3 18.8 %collective-permute-start.21 = (bf16[128,1152]{1,0:T(8,128)(2,1)S(1)}, bf16[128,1152]{1,0:T(8,128)(2,1)}, u32[]{:S(2)}, u32[]{:S(2)}) collective-permute-start(bf16[128,1152]{1,0:T(8,128)(2,1)S(1)} %collective-permute-done.11.refs_0_), channel_id=1, source_target_pairs={{0,16},{4,20},{8,24},{12,28},{16,0},{20,4},{24,8},{28,12},{1,17},{... | collective-permute-start | bytes 884744 | tf_op jit(solution)/shard_map/ppermute | solution.py:35
  86.2 33.1 %collective-permute-start.23 = (bf16[256,1280]{1,0:T(8,128)(2,1)}, bf16[256,1280]{1,0:T(8,128)(2,1)}, u32[]{:S(2)}, u32[]{:S(2)}) collective-permute-start(bf16[256,1280]{1,0:T(8,128)(2,1)} %get-tuple-element.92), channel_id=1, source_target_pairs={{0,1},{1,0},{2,3},{3,2},{4,5},{5,4},{6,7},{7,6},{8,9},{9,8},{10,11... | collective-permute-start | bytes 1966088 | tf_op jit(solution)/shard_map/ppermute | solution.py:35
  86.6 32.7 %collective-permute-start.24 = (bf16[256,1280]{1,0:T(8,128)(2,1)}, bf16[256,1280]{1,0:T(8,128)(2,1)}, u32[]{:S(2)}, u32[]{:S(2)}) collective-permute-start(bf16[256,1280]{1,0:T(8,128)(2,1)} %get-tuple-element.93), channel_id=1, source_target_pairs={{0,2},{1,3},{2,0},{3,1},{4,6},{5,7},{6,4},{7,5},{8,10},{9,11},{10,... | collective-permute-start | bytes 1966088 | tf_op jit(solution)/shard_map/ppermute | solution.py:35
  90.3 16.5 %collective-permute-start.25 = (bf16[256,1152]{1,0:T(8,128)(2,1)}, bf16[256,1152]{1,0:T(8,128)(2,1)}, u32[]{:S(2)}, u32[]{:S(2)}) collective-permute-start(bf16[256,1152]{1,0:T(8,128)(2,1)} %pad_maximum_fusion.refs_0_.refs_4_), channel_id=1, source_target_pairs={{0,8},{4,12},{8,0},{12,4},{16,24},{20,28},{24,16},{28,20},{1,9},{5... | collective-permute-start | bytes 1769480 | tf_op jit(solution)/shard_map/ppermute | solution.py:35
  91.3 26.8 %collective-permute-start.26 = (bf16[256,1152]{1,0:T(8,128)(2,1)}, bf16[256,1152]{1,0:T(8,128)(2,1)}, u32[]{:S(2)}, u32[]{:S(2)}) collective-permute-start(bf16[256,1152]{1,0:T(8,128)(2,1)} %pad_maximum_fusion.refs_0_.refs_4_), channel_id=1, source_target_pairs={{0,16},{4,20},{8,24},{12,28},{16,0},{20,4},{24,8},{28,12},{1,17},{... | collective-permute-start | bytes 1769480 | tf_op jit(solution)/shard_map/ppermute | solution.py:35
  92.8 26.5 %collective-permute-start.27 = (bf16[256,1152]{1,0:T(8,128)(2,1)}, bf16[256,1152]{1,0:T(8,128)(2,1)}, u32[]{:S(2)}, u32[]{:S(2)}) collective-permute-start(bf16[256,1152]{1,0:T(8,128)(2,1)} %pad_maximum_fusion.refs_0_.refs_4_), channel_id=1, source_target_pairs={{0,24},{4,28},{8,16},{12,20},{16,8},{20,12},{24,0},{28,4},{1,25},{... | collective-permute-start | bytes 1769480 | tf_op jit(solution)/shard_map/ppermute | solution.py:35
  106.8 37.2 %collective-permute-start.30 = (bf16[256,1280]{1,0:T(8,128)(2,1)S(1)}, bf16[256,1280]{1,0:T(8,128)(2,1)}, u32[]{:S(2)}, u32[]{:S(2)}) collective-permute-start(bf16[256,1280]{1,0:T(8,128)(2,1)S(1)} %get-tuple-element.102.refs_8_), channel_id=1, source_target_pairs={{0,4},{4,0},{8,12},{12,8},{16,20},{20,16},{24,28},{28,24},{1,5},{5... | collective-permute-start | bytes 1966088 | tf_op jit(solution)/shard_map/ppermute | solution.py:35
  118.1 26.0 %collective-permute-start.33 = (bf16[256,1280]{1,0:T(8,128)(2,1)}, bf16[256,1280]{1,0:T(8,128)(2,1)}, u32[]{:S(2)}, u32[]{:S(2)}) collective-permute-start(bf16[256,1280]{1,0:T(8,128)(2,1)} %collective-permute-done.19.refs_11_), channel_id=1, source_target_pairs={{0,4},{4,0},{8,12},{12,8},{16,20},{20,16},{24,28},{28,24},{1,5},{5... | collective-permute-start | bytes 1966088 | tf_op jit(solution)/shard_map/ppermute | solution.py:35
  119.3 16.4 %collective-permute-start.29 = (bf16[128,1152]{1,0:T(8,128)(2,1)}, bf16[128,1152]{1,0:T(8,128)(2,1)}, u32[]{:S(2)}, u32[]{:S(2)}) collective-permute-start(bf16[128,1152]{1,0:T(8,128)(2,1)} %copy-done.8), channel_id=1, source_target_pairs={{0,24},{4,28},{8,16},{12,20},{16,8},{20,12},{24,0},{28,4},{1,25},{... | collective-permute-start | bytes 884744 | tf_op jit(solution)/shard_map/ppermute | solution.py:35
  121.2 22.8 %collective-permute-start.28 = (bf16[256,1280]{1,0:T(8,128)(2,1)S(1)}, bf16[256,1280]{1,0:T(8,128)(2,1)}, u32[]{:S(2)}, u32[]{:S(2)}) collective-permute-start(bf16[256,1280]{1,0:T(8,128)(2,1)S(1)} %get-tuple-element.106), channel_id=1, source_target_pairs={{0,3},{3,0},{4,7},{7,4},{8,11},{11,8},{12,15},{15,12},{16,19},{19,... | collective-permute-start | bytes 1966088 | tf_op jit(solution)/shard_map/ppermute | solution.py:447
  125.6 18.5 %collective-permute-start.31 = (bf16[256,1280]{1,0:T(8,128)(2,1)}, bf16[256,1280]{1,0:T(8,128)(2,1)}, u32[]{:S(2)}, u32[]{:S(2)}) collective-permute-start(bf16[256,1280]{1,0:T(8,128)(2,1)} %collective-permute-done.23.refs_9_), channel_id=1, source_target_pairs={{0,4},{4,0},{8,12},{12,8},{16,20},{20,16},{24,28},{28,24},{1,5},{5... | collective-permute-start | bytes 1966088 | tf_op jit(solution)/shard_map/ppermute | solution.py:35
  162.4 17.2 %collective-permute-start.35 = (bf16[2,2,128,512]{3,2,1,0:T(8,128)(2,1)}, bf16[2,2,128,512]{3,2,1,0:T(8,128)(2,1)}, u32[]{:S(2)}, u32[]{:S(2)}) collective-permute-start(bf16[2,2,128,512]{3,2,1,0:T(8,128)(2,1)} %get-tuple-element.112), channel_id=1, source_target_pairs={{0,8},{4,12},{8,0},{12,4},{16,24},{20,28},{24,16},{28,20},{1,9},{5... | collective-permute-start | bytes 1572872 | tf_op jit(solution)/shard_map/ppermute | solution.py:35
  163.1 16.6 %collective-permute-start.36 = (bf16[2,2,128,512]{3,2,1,0:T(8,128)(2,1)}, bf16[2,2,128,512]{3,2,1,0:T(8,128)(2,1)}, u32[]{:S(2)}, u32[]{:S(2)}) collective-permute-start(bf16[2,2,128,512]{3,2,1,0:T(8,128)(2,1)} %get-tuple-element.113), channel_id=1, source_target_pairs={{0,16},{4,20},{8,24},{12,28},{16,0},{20,4},{24,8},{28,12},{1,17},{... | collective-permute-start | bytes 1572872 | tf_op jit(solution)/shard_map/ppermute | solution.py:35
  180.7 9.3 %collective-permute-start.42 = (bf16[2,128,512]{2,1,0:T(8,128)(2,1)S(1)}, bf16[2,128,512]{2,1,0:T(8,128)(2,1)S(1)}, u32[]{:S(2)}, u32[]{:S(2)}) collective-permute-start(bf16[2,128,512]{2,1,0:T(8,128)(2,1)S(1)} %fusion.7), channel_id=1, source_target_pairs={{0,16},{4,20},{8,24},{12,28},{16,0},{20,4},{24,8},{28,12},{1,17},{... | collective-permute-start | bytes 786440 | tf_op jit(solution)/shard_map/ppermute | solution.py:35
  182.7 9.3 %collective-permute-start.43 = (bf16[2,128,512]{2,1,0:T(8,128)(2,1)S(1)}, bf16[2,128,512]{2,1,0:T(8,128)(2,1)S(1)}, u32[]{:S(2)}, u32[]{:S(2)}) collective-permute-start(bf16[2,128,512]{2,1,0:T(8,128)(2,1)S(1)} %fusion.8), channel_id=1, source_target_pairs={{0,8},{4,12},{8,0},{12,4},{16,24},{20,28},{24,16},{28,20},{1,9},{5... | collective-permute-start | bytes 786440 | tf_op jit(solution)/shard_map/ppermute | solution.py:35
  184.3 17.3 %collective-permute-start.37 = (bf16[2,2,128,512]{3,2,1,0:T(8,128)(2,1)}, bf16[2,2,128,512]{3,2,1,0:T(8,128)(2,1)S(1)}, u32[]{:S(2)}, u32[]{:S(2)}) collective-permute-start(bf16[2,2,128,512]{3,2,1,0:T(8,128)(2,1)} %get-tuple-element.123), channel_id=1, source_target_pairs={{0,8},{4,12},{8,0},{12,4},{16,24},{20,28},{24,16},{28,20},{1,9},{5... | collective-permute-start | bytes 1572872 | tf_op jit(solution)/shard_map/ppermute | solution.py:35
  184.8 19.6 %collective-permute-start.39 = (bf16[2,2,128,512]{3,2,1,0:T(8,128)(2,1)}, bf16[2,2,128,512]{3,2,1,0:T(8,128)(2,1)S(1)}, u32[]{:S(2)}, u32[]{:S(2)}) collective-permute-start(bf16[2,2,128,512]{3,2,1,0:T(8,128)(2,1)} %get-tuple-element.125), channel_id=1, source_target_pairs={{0,16},{4,20},{8,24},{12,28},{16,0},{20,4},{24,8},{28,12},{1,17},{... | collective-permute-start | bytes 1572872 | tf_op jit(solution)/shard_map/ppermute | solution.py:35
  193.2 18.0 %collective-permute-start.44 = (bf16[128,1024]{1,0:T(8,128)(2,1)S(1)}, bf16[128,1024]{1,0:T(8,128)(2,1)S(1)}, u32[]{:S(2)}, u32[]{:S(2)}) collective-permute-start(bf16[128,1024]{1,0:T(8,128)(2,1)S(1)} %pad_maximum_fusion.3), channel_id=1, source_target_pairs={{0,2},{1,3},{2,0},{3,1},{4,6},{5,7},{6,4},{7,5},{8,10},{9,11},{10,... | collective-permute-start | bytes 786440 | tf_op jit(solution)/shard_map/ppermute | solution.py:35
  (37 other events, 360.5 us)
